TPU v7x, 32 devices: a whole 2x2x4 slice. The times are simulated.
32 devices in a mesh: lat: 4 (over y, core), lon: 8 (over z, x).
Axes of the slice: x: 2, y: 2, z: 4, core: 2. Of those that a mesh axis runs over, the one named last changes fastest.
Arguments:
- obs_pert: bfloat16 [1024, 512, 256], P(('lat', 'lon')), may hold values from -3 to 3
- obs_weight: bfloat16 [1024, 512], P(('lat', 'lon')), may hold values from 0.5 to 2
- innovation: bfloat16 [1024, 512], P(('lat', 'lon')), may hold values from -6 to 6
- batch_len: int32 [32, 32], P(('lat', 'lon')), may hold values from 1 to 512, 10240 in all within a row
- batch_owner: int32 [1024, 1], P(('lat', 'lon')), may hold values from 0 to 7; in each aligned block of 32 rows (0 to 31, 32 to 63, ...) at most 4 rows name the same one
- batch_points: int32 [1024, 3], P(('lat', 'lon')), may hold values from 0 to 7, all different within a row
- batch_count: int32 [1024], P(('lat', 'lon')), may hold values from 1 to 3
- batch_taper: bfloat16 [1024, 3], P(('lat', 'lon')), may hold values from 0.25 to 1
- background: bfloat16 [32, 1024, 256], P('lat', 'lon'), may hold values from -6 to 6
- stencil: int32 [2, 32, 1024], P(None, 'lat', 'lon'), may hold values from 0 to 31, as said below
- frac: float32 [2, 32, 1024], P(None, 'lat', 'lon'), may hold values from 0 to 1
Outputs:
- analysis: bfloat16 [32, 1024, 256], P('lat', 'lon')
Inputs may be any that keep to these rules, and one draw needn't show every extreme that they name: `batch_owner`: among the 32 batches held by one device, at most 4 share an owner, and in every draw some owner has exactly 4 of them. `batch_points`: the entries of a row are distinct; local point p of an owner is its point p // 4 along latitude and p % 4 along longitude. Only the first batch_count entries of a batch's row of batch_points and batch_taper count. `batch_len`: each row sums to 10240 and its largest entry is 512. For a cell in the block of cells a * 8 .. (a + 1) * 8 - 1 along latitude and c * 128 .. (c + 1) * 128 - 1 along longitude, stencil[0] lies in a * 2 - 1 .. (a + 1) * 2 - 1 and in 0 .. 6, and stencil[1] is (c * 4 - 1 + t) mod 32 for some t in 0 .. 4.
All inputs are finite; a program needn't handle non-finite values.
Results may differ from a plain program's by a relative error of at most 0.0059.
Values may be sent and summed in bfloat16 or wider, within the bound.
No kernel may reach another device: no remote copies, remote signals or barrier semaphores. Data moves between devices by JAX's collectives and lax.ppermute only.
A program may use at most 128 MiB of HBM per device.

v0:
```python
import jax
import jax.numpy as jnp
from jax import lax
from jax.sharding import PartitionSpec as P

MEMBERS = 256
NOBS = 512
CAP = 4
TOP = 3
PLAT = 2
PLON = 4
PTS_DEV = 8
ITERS = 6


def extended(value, sides, width, wrap):
    for axis, dim in sides:
        count, length = (lax.axis_size(axis), value.shape[dim])
        up = [(i, (i + 1) % count) for i in range(count if wrap else count - 1)]
        down = [(j, i) for i, j in up]
        last = lax.slice_in_dim(value, length - width, length, axis=dim)
        initial = lax.slice_in_dim(value, 0, width, axis=dim)
        before = lax.ppermute(last, axis, up)
        after = lax.ppermute(initial, axis, down)
        value = jnp.concatenate([before, value, after], axis=dim)
    return value


def point_weights(batch_points, batch_count, batch_taper):
    listed = jnp.arange(TOP, dtype=jnp.int32)
    valid = listed[None, :] < batch_count[:, None]
    onehot = batch_points[:, :, None] == jnp.arange(PTS_DEV, dtype=jnp.int32)[None, None, :]
    picked = jnp.where(
        valid[:, :, None] & onehot, batch_taper.astype(jnp.float32)[:, :, None], jnp.float32(0.0)
    )
    return jnp.sum(picked, axis=1).astype(jnp.bfloat16)


def batch_moments(pert_rows, kept_weight, innov_rows):
    scaled = (kept_weight.astype(jnp.float32)[..., None] * pert_rows.astype(jnp.float32)).astype(
        jnp.bfloat16
    )
    batch_gram = jnp.einsum(
        "...ok,...ol->...kl", scaled, pert_rows, preferred_element_type=jnp.float32
    ).astype(jnp.bfloat16)
    batch_proj = jnp.einsum(
        "...o,...ok->...k", innov_rows, scaled, preferred_element_type=jnp.float32
    ).astype(jnp.bfloat16)
    return (batch_gram, batch_proj)


def interp_weights(stencil, frac, lat_pos, lon_pos, point_cols):
    row_off = stencil[0] - (lat_pos * PLAT - 1)
    col_off = (stencil[1] - lon_pos * PLON + 1) % point_cols
    lat_frac = frac[0].reshape(-1)[:, None]
    lon_frac = frac[1].reshape(-1)[:, None]
    corner_id = (row_off * (PLON + 2) + col_off).reshape(-1)[:, None]
    all_ids = jnp.arange((PLAT + 2) * (PLON + 2), dtype=jnp.int32)[None, :]
    zero_val = jnp.float32(0.0)
    weights = jnp.where(corner_id == all_ids, (1.0 - lat_frac) * (1.0 - lon_frac), zero_val)
    weights = weights + jnp.where(
        corner_id + (PLON + 2) == all_ids, lat_frac * (1.0 - lon_frac), zero_val
    )
    weights = weights + jnp.where(corner_id + 1 == all_ids, (1.0 - lat_frac) * lon_frac, zero_val)
    weights = weights + jnp.where(corner_id + (PLON + 3) == all_ids, lat_frac * lon_frac, zero_val)
    return weights


def point_transforms(totals, shifts):
    highest = lax.Precision.HIGHEST
    identity = jnp.eye(MEMBERS, dtype=jnp.float32)[None]
    system = totals + (MEMBERS - 1) * identity
    scale = jnp.sqrt(jnp.sum(system * system, axis=(1, 2)))
    iterate = system / scale[:, None, None]
    inverse_root = jnp.broadcast_to(identity, system.shape)
    for sweep in range(ITERS):
        factor = 1.5 * identity - 0.5 * jnp.einsum(
            "pij,pjk->pik", inverse_root, iterate, precision=highest
        )
        iterate = jnp.einsum("pij,pjk->pik", iterate, factor, precision=highest)
        inverse_root = jnp.einsum("pij,pjk->pik", factor, inverse_root, precision=highest)
    inner = jnp.einsum("pij,pj->pi", inverse_root, shifts, precision=highest)
    mean_weight = jnp.einsum("pij,pj->pi", inverse_root, inner, precision=highest) / scale[:, None]
    result = jnp.sqrt((MEMBERS - 1) / scale)[:, None, None] * inverse_root + mean_weight[:, :, None]
    return result.astype(jnp.bfloat16)


def on_device(
    obs_pert,
    obs_weight,
    innovation,
    batch_len,
    batch_owner,
    batch_points,
    batch_count,
    batch_taper,
    background,
    stencil,
    frac,
):
    lon_size = lax.axis_size("lon")
    held_batches = obs_pert.shape[0]
    owners = batch_owner[:, 0]
    owner_hot = (owners[:, None] == jnp.arange(lon_size, dtype=jnp.int32)[None, :]).astype(
        jnp.int32
    )
    earlier = jnp.cumsum(owner_hot, axis=0) - owner_hot
    place_id = owners * CAP + jnp.sum(earlier * owner_hot, axis=1)
    matched = place_id[None, :] == jnp.arange(lon_size * CAP, dtype=jnp.int32)[:, None]
    source_row = jnp.sum(
        jnp.where(matched, jnp.arange(held_batches, dtype=jnp.int32)[None, :], 0), axis=1
    )
    filled = jnp.any(matched, axis=1)

    def arrange(values):
        taken = jnp.take(values, source_row, axis=0)
        shaped = filled.reshape((-1,) + (1,) * (values.ndim - 1))
        placed = jnp.where(shaped, taken, jnp.zeros_like(taken))
        return placed.reshape((lon_size, CAP) + values.shape[1:])

    live_rows = jnp.arange(NOBS, dtype=jnp.int32)[None, :] < batch_len[0][:, None]
    kept_weight = jnp.where(live_rows, obs_weight, jnp.zeros_like(obs_weight))
    coef = point_weights(batch_points, batch_count, batch_taper)
    batch_gram, batch_proj = batch_moments(obs_pert, kept_weight, innovation)
    got_gram, got_proj, got_coef = (
        lax.all_to_all(arrange(batch_gram), "lon", split_axis=0, concat_axis=0, tiled=True),
        lax.all_to_all(arrange(batch_proj), "lon", split_axis=0, concat_axis=0, tiled=True),
        lax.all_to_all(arrange(coef), "lon", split_axis=0, concat_axis=0, tiled=True),
    )
    slot_total = lon_size * CAP
    flat_coef = got_coef.reshape(slot_total, PTS_DEV)
    flat_gram = got_gram.reshape(slot_total, MEMBERS * MEMBERS)
    flat_proj = got_proj.reshape(slot_total, MEMBERS)
    totals = jnp.einsum(
        "sp,sx->px", flat_coef, flat_gram, preferred_element_type=jnp.float32
    ).reshape(PTS_DEV, MEMBERS, MEMBERS)
    shifts = jnp.einsum("sp,sk->pk", flat_coef, flat_proj, preferred_element_type=jnp.float32)
    transforms = point_transforms(totals, shifts).reshape(PLAT, PLON, MEMBERS, MEMBERS)
    widened = extended(transforms, (("lon", 1),), 1, True)
    window = extended(widened, (("lat", 0),), 1, False)
    lat_pos = lax.axis_index("lat")
    lon_pos = lax.axis_index("lon")
    weights = interp_weights(stencil, frac, lat_pos, lon_pos, PLON * lon_size)
    mean_field = jnp.mean(background.astype(jnp.float32), axis=-1)
    deviation = (
        (background.astype(jnp.float32) - mean_field[..., None])
        .astype(jnp.bfloat16)
        .reshape(-1, MEMBERS)
    )

    def accumulate(carry, item):
        matrix, column = item
        return (
            carry
            + column[:, None] * jnp.dot(deviation, matrix, preferred_element_type=jnp.float32),
            None,
        )

    start_sum = jnp.zeros(deviation.shape, jnp.float32)
    mixed, unused = lax.scan(
        accumulate, start_sum, (window.reshape(-1, MEMBERS, MEMBERS), weights.T)
    )
    return (mean_field[..., None] + mixed.reshape(background.shape)).astype(jnp.bfloat16)


def solution(mesh):
    return jax.shard_map(
        on_device,
        mesh=mesh,
        in_specs=(
            P(("lat", "lon"), None, None),
            P(("lat", "lon"), None),
            P(("lat", "lon"), None),
            P(("lat", "lon"), None),
            P(("lat", "lon"), None),
            P(("lat", "lon"), None),
            P(("lat", "lon")),
            P(("lat", "lon"), None),
            P("lat", "lon", None),
            P(None, "lat", "lon"),
            P(None, "lat", "lon"),
        ),
        out_specs=P("lat", "lon", None),
        check_vma=False,
    )
```

profile of v0, /device:TPU:1, one launch (start us, length us, event | category | flops | bytes accessed | tf_op | source)
XLA Modules:
  0.0 266.0 jit_solution(14022554439948275594)
XLA Ops:
  6.1 6.4 %all-to-all-start = ((bf16[8,4,8]{2,1,0:T(4,128)(2,1)}), bf16[8,4,8]{2,1,0:T(4,128)(2,1)S(1)}, u32[]{:S(2)}, u32[]{:S(2)}) async-start(bf16[8,4,8]{2,1,0:T(4,128)(2,1)} %select_select_fusion.2), calls=%async_computation | async-start | bytes 16384 | tf_op jit(solution)/shard_map/all_to_all | solution.py:128
  13.3 12.1 %fusion.12 = bf16[32,256,256]{2,1,0:T(8,128)(2,1)} fusion(bf16[32,512,256]{2,1,0:T(8,128)(2,1)} %param.13, f32[32,512]{1,0:T(8,128)S(1)} %fusion.59), kind=kOutput, calls=%fused_computation.20 | convolution fusion | flops 2162163712 | bytes 12648448 | tf_op jit(solution)/shard_map/...ok,...ol->...kl/dot_general | solution.py:43
  25.5 3.7 %fusion.5 = bf16[32,1,256]{2,1,0:T(2,128)(2,1)S(1)} fusion(bf16[32,512,256]{2,1,0:T(8,128)(2,1)S(1)} %copy-done.6, f32[32,512]{1,0:T(8,128)S(1)} %fusion.59, bf16[32,512,1]{1,0,2:T(8,128)(2,1)S(1)} %bitcast.107), kind=kOutput, calls=%fused_computation.11 | convolution fusion | flops 20971520 | bytes 8503296 | tf_op jit(solution)/shard_map/...o,...ok->...k/dot_general | solution.py:46
  30.5 4.9 %gather_fusion.1 = bf16[32,256,256]{2,1,0:T(8,128)(2,1)} fusion(bf16[32,256,256]{2,1,0:T(8,128)(2,1)} %fusion.12, s32[1024]{0:T(1024)S(1)} %pad_clamp_fusion), kind=kCustom, calls=%fused_computation.1 | custom fusion | bytes 8388736 | tf_op jit(solution)/shard_map/jit(_take)/gather | solution.py:116
  35.4 5.4 %all-to-all-start.2 = ((bf16[8,4,256]{2,1,0:T(4,128)(2,1)}), bf16[8,4,256]{2,1,0:T(4,128)(2,1)S(1)}, u32[]{:S(2)}, u32[]{:S(2)}) async-start(bf16[8,4,256]{2,1,0:T(4,128)(2,1)} %select_select_fusion.1), calls=%async_computation.2 | async-start | bytes 32768 | tf_op jit(solution)/shard_map/all_to_all | solution.py:127
  40.9 4.7 %select_select_fusion = bf16[8,4,256,256]{3,2,1,0:T(8,128)(2,1)} fusion(bf16[8,4,256,256]{3,2,1,0:T(8,128)(2,1)} %bitcast.109, pred[8,4]{1,0:T(8,128)(4,1)S(1)} %compare_and_fusion, pred[8,4]{1,0:T(8,128)(4,1)S(1)} %broadcast_in_dim.159), kind=kLoop, calls=%fused_computation.18 | loop fusion | flops 4194304 | bytes 8388672 | tf_op jit(solution)/shard_map/jit(_where)/select_n | solution.py:118
  46.3 5.3 %all-to-all-start.1 = ((bf16[8,4,256,256]{3,2,1,0:T(8,128)(2,1)}), bf16[8,4,256,256]{3,2,1,0:T(8,128)(2,1)}, u32[]{:S(2)}, u32[]{:S(2)}) async-start(bf16[8,4,256,256]{3,2,1,0:T(8,128)(2,1)} %select_select_fusion), calls=%async_computation.1 | async-start | bytes 8388608 | tf_op jit(solution)/shard_map/all_to_all | solution.py:126
  51.9 90.3 %all-to-all-done.1 = bf16[8,4,256,256]{3,2,1,0:T(8,128)(2,1)} async-done(((bf16[8,4,256,256]{3,2,1,0:T(8,128)(2,1)}), bf16[8,4,256,256]{3,2,1,0:T(8,128)(2,1)}, u32[]{:S(2)}, u32[]{:S(2)}) %all-to-all-start.1) | async-done | bytes 4194336 | tf_op jit(solution)/shard_map/all_to_all | solution.py:126
  142.2 4.7 %multiply_reduce_fusion = (f32[8]{0:T(128)S(1)}, f32[8,256,256]{2,0,1:T(8,128)S(1)}) fusion(f32[256,256]{1,0:T(8,128)S(1)} %fusion.56, bf16[32,8,1]{1,0,2:T(8,128)(2,1)S(1)} %bitcast.119, bf16[4,8,256,256]{3,2,1,0:T(8,128)(2,1)} %bitcast.30), kind=kOutput, calls=%fused_computation.30 | convolution fusion | flops 35127288 | bytes 6554144 | tf_op jit(solution)/shard_map/sp,sx->px/dot_general | solution.py:134
  147.3 2.5 fusion.18
  149.7 2.8 %fusion.16 = f32[8,256,256]{2,1,0:T(8,128)S(1)} fusion(f32[8,256,256]{2,0,1:T(8,128)S(1)} %add_divide_fusion, f32[8,256,256]{2,1,0:T(8,128)S(1)} %fusion.18, f32[256,256]{1,0:T(8,128)S(1)} %fusion.55), kind=kOutput, calls=%fused_computation.31 | convolution fusion | flops 1611661312 | bytes 6553600 | tf_op jit(solution)/shard_map/pij,pjk->pik/dot_general | solution.py:80
  154.6 2.4 fusion.85
  157.0 2.3 fusion.21
  159.3 2.3 fusion.22
  161.6 2.2 fusion.86
  163.8 2.3 fusion.23
  166.1 2.3 fusion.24
  168.4 2.4 fusion.87
  170.8 2.3 fusion.25
  173.2 2.3 fusion.26
  177.6 2.3 fusion.27
  180.0 2.6 fusion.28
  182.5 2.2 fusion.89
  184.7 2.3 fusion.13
  191.3 2.9 %collective-permute-start = (bf16[2,1,256,256]{3,2,1,0:T(8,128)(2,1)S(1)}, bf16[2,1,256,256]{3,2,1,0:T(8,128)(2,1)S(1)}, u32[]{:S(2)}, u32[]{:S(2)}) collective-permute-start(bf16[2,1,256,256]{3,2,1,0:T(8,128)(2,1)S(1)} %get-tuple-element.65), channel_id=1, source_target_pairs={{0,1},{1,2},{2,3},{3,4},{4,5},{5,6},{6,7},{7,0},{8,9},{9,10},{10,1... | collective-permute-start | bytes 786440 | tf_op jit(solution)/shard_map/ppermute | solution.py:23
  196.4 8.4 %collective-permute-done = bf16[2,1,256,256]{3,2,1,0:T(8,128)(2,1)S(1)} collective-permute-done((bf16[2,1,256,256]{3,2,1,0:T(8,128)(2,1)S(1)}, bf16[2,1,256,256]{3,2,1,0:T(8,128)(2,1)S(1)}, u32[]{:S(2)}, u32[]{:S(2)}) %collective-permute-start) | collective-permute-done | bytes 262176 | tf_op jit(solution)/shard_map/ppermute | solution.py:23
  204.8 2.8 %collective-permute-done.1 = bf16[2,1,256,256]{3,2,1,0:T(8,128)(2,1)S(1)} collective-permute-done((bf16[2,1,256,256]{3,2,1,0:T(8,128)(2,1)S(1)}, bf16[2,1,256,256]{3,2,1,0:T(8,128)(2,1)S(1)}, u32[]{:S(2)}, u32[]{:S(2)}) %collective-permute-start.1) | collective-permute-done | bytes 262176 | tf_op jit(solution)/shard_map/ppermute | solution.py:24
  209.1 4.0 %collective-permute-start.2 = (bf16[1,6,256,256]{3,2,1,0:T(8,128)(2,1)}, bf16[1,6,256,256]{3,2,1,0:T(8,128)(2,1)}, u32[]{:S(2)}, u32[]{:S(2)}) collective-permute-start(bf16[1,6,256,256]{3,2,1,0:T(8,128)(2,1)} %get-tuple-element.63), channel_id=1, source_target_pairs={{0,8},{8,16},{16,24},{1,9},{9,17},{17,25},{2,10},{10,18},{18,26},{... | collective-permute-start | bytes 2359304 | tf_op jit(solution)/shard_map/ppermute | solution.py:23
  215.3 7.0 %collective-permute-done.2 = bf16[1,6,256,256]{3,2,1,0:T(8,128)(2,1)} collective-permute-done((bf16[1,6,256,256]{3,2,1,0:T(8,128)(2,1)}, bf16[1,6,256,256]{3,2,1,0:T(8,128)(2,1)}, u32[]{:S(2)}, u32[]{:S(2)}) %collective-permute-start.2) | collective-permute-done | bytes 786464 | tf_op jit(solution)/shard_map/ppermute | solution.py:23
  222.3 4.4 %collective-permute-done.3 = bf16[1,6,256,256]{3,2,1,0:T(8,128)(2,1)} collective-permute-done((bf16[1,6,256,256]{3,2,1,0:T(8,128)(2,1)}, bf16[1,6,256,256]{3,2,1,0:T(8,128)(2,1)}, u32[]{:S(2)}, u32[]{:S(2)}) %collective-permute-start.3) | collective-permute-done | bytes 786464 | tf_op jit(solution)/shard_map/ppermute | solution.py:24
  226.7 3.1 %pad_maximum_fusion = bf16[4,6,256,256]{3,2,1,0:T(8,128)(2,1)} fusion(bf16[1,6,256,256]{3,2,1,0:T(8,128)(2,1)} %collective-permute-done.3, bf16[2,1,256,256]{3,2,1,0:T(8,128)(2,1)} %copy-done.3, bf16[2,4,256,256]{3,2,1,0:T(8,128)(2,1)S(1)} %bitcast.112, bf16[2,1,256,256]{3,2,1,0:T(8,128)(2,1)S(1)} %collective-permute-done, ...), kind=kLoop, calls=%fused_computation.19 | loop fusion | flops 6291456 | bytes 6291456 | tf_op jit(solution)/shard_map/concatenate | solution.py:25
  229.8 34.3 %while.11 = (s32[]{:T(128)}, f32[1024,256]{0,1:T(8,128)S(1)}, f32[24,1024]{1,0:T(8,128)S(1)}, bf16[24,256,256]{2,1,0:T(8,128)(2,1)}, bf16[1024,256]{1,0:T(8,128)(2,1)S(1)}, /*index=5*/s32[]{:T(128)}, s32[]{:T(128)}) while((s32[]{:T(128)}, f32[1024,256]{0,1:T(8,128)S(1)}, f32[24,1024]{1,0:T(8,128)S(1)}, ...), condition=%wide.region_8.9_spmd.clone, body=%wide.region_7.8_spmd.clone.sunk | while | flops 135004160 | bytes 2765403 | solution.py:160
  (114 shorter events, 58.8 us)
Async XLA Ops:
  0.0 25.5 %copy-start = (bf16[32,512]{1,0:T(8,128)(2,1)S(1)}, bf16[32,512]{1,0:T(8,128)(2,1)}, u32[]{:S(2)}) copy-start(bf16[32,512]{1,0:T(8,128)(2,1)} %param.15) | copy-start | bytes 98308
  6.1 29.3 %all-to-all-start = ((bf16[8,4,8]{2,1,0:T(4,128)(2,1)}), bf16[8,4,8]{2,1,0:T(4,128)(2,1)S(1)}, u32[]{:S(2)}, u32[]{:S(2)}) async-start(bf16[8,4,8]{2,1,0:T(4,128)(2,1)} %select_select_fusion.2), calls=%async_computation | async-start | bytes 16384 | tf_op jit(solution)/shard_map/all_to_all | solution.py:128
  13.3 12.1 %copy-start.6 = (bf16[32,512,256]{2,1,0:T(8,128)(2,1)S(1)}, bf16[32,512,256]{2,1,0:T(8,128)(2,1)}, u32[]{:S(2)}) copy-start(bf16[32,512,256]{2,1,0:T(8,128)(2,1)} %param.13) | copy-start | bytes 25165828
  35.4 10.9 %all-to-all-start.2 = ((bf16[8,4,256]{2,1,0:T(4,128)(2,1)}), bf16[8,4,256]{2,1,0:T(4,128)(2,1)S(1)}, u32[]{:S(2)}, u32[]{:S(2)}) async-start(bf16[8,4,256]{2,1,0:T(4,128)(2,1)} %select_select_fusion.1), calls=%async_computation.2 | async-start | bytes 32768 | tf_op jit(solution)/shard_map/all_to_all | solution.py:127
  45.5 6.1 %copy-start.5 = (s32[2,8,128]{2,1,0:T(8,128)S(1)}, s32[2,8,128]{2,1,0:T(8,128)}, u32[]{:S(2)}) copy-start(s32[2,8,128]{2,1,0:T(8,128)} %param.22) | copy-start | bytes 24580
  46.3 95.9 %all-to-all-start.1 = ((bf16[8,4,256,256]{3,2,1,0:T(8,128)(2,1)}), bf16[8,4,256,256]{3,2,1,0:T(8,128)(2,1)}, u32[]{:S(2)}, u32[]{:S(2)}) async-start(bf16[8,4,256,256]{3,2,1,0:T(8,128)(2,1)} %select_select_fusion), calls=%async_computation.1 | async-start | bytes 8388608 | tf_op jit(solution)/shard_map/all_to_all | solution.py:126
  190.8 5.4 %copy-start.2 = (bf16[8,128,256]{2,1,0:T(8,128)(2,1)S(1)}, bf16[8,128,256]{2,1,0:T(8,128)(2,1)}, u32[]{:S(2)}) copy-start(bf16[8,128,256]{2,1,0:T(8,128)(2,1)} %param.21) | copy-start | bytes 1572868
  191.3 13.5 %collective-permute-start = (bf16[2,1,256,256]{3,2,1,0:T(8,128)(2,1)S(1)}, bf16[2,1,256,256]{3,2,1,0:T(8,128)(2,1)S(1)}, u32[]{:S(2)}, u32[]{:S(2)}) collective-permute-start(bf16[2,1,256,256]{3,2,1,0:T(8,128)(2,1)S(1)} %get-tuple-element.65), channel_id=1, source_target_pairs={{0,1},{1,2},{2,3},{3,4},{4,5},{5,6},{6,7},{7,0},{8,9},{9,10},{10,1... | collective-permute-start | bytes 786440 | tf_op jit(solution)/shard_map/ppermute | solution.py:23
  194.3 13.4 %collective-permute-start.1 = (bf16[2,1,256,256]{3,2,1,0:T(8,128)(2,1)S(1)}, bf16[2,1,256,256]{3,2,1,0:T(8,128)(2,1)S(1)}, u32[]{:S(2)}, u32[]{:S(2)}) collective-permute-start(bf16[2,1,256,256]{3,2,1,0:T(8,128)(2,1)S(1)} %get-tuple-element.66), channel_id=1, source_target_pairs={{1,0},{2,1},{3,2},{4,3},{5,4},{6,5},{7,6},{0,7},{9,8},{10,9},{11,1... | collective-permute-start | bytes 786440 | tf_op jit(solution)/shard_map/ppermute | solution.py:24
  207.6 1.5 copy-start.3
  207.8 7.2 %copy-start.4 = (f32[2,8,128]{2,1,0:T(8,128)S(1)}, f32[2,8,128]{2,1,0:T(8,128)}, u32[]{:S(2)}) copy-start(f32[2,8,128]{2,1,0:T(8,128)} %param.23) | copy-start | bytes 24580
  209.1 13.2 %collective-permute-start.2 = (bf16[1,6,256,256]{3,2,1,0:T(8,128)(2,1)}, bf16[1,6,256,256]{3,2,1,0:T(8,128)(2,1)}, u32[]{:S(2)}, u32[]{:S(2)}) collective-permute-start(bf16[1,6,256,256]{3,2,1,0:T(8,128)(2,1)} %get-tuple-element.63), channel_id=1, source_target_pairs={{0,8},{8,16},{16,24},{1,9},{9,17},{17,25},{2,10},{10,18},{18,26},{... | collective-permute-start | bytes 2359304 | tf_op jit(solution)/shard_map/ppermute | solution.py:23
  213.1 13.6 %collective-permute-start.3 = (bf16[1,6,256,256]{3,2,1,0:T(8,128)(2,1)}, bf16[1,6,256,256]{3,2,1,0:T(8,128)(2,1)}, u32[]{:S(2)}, u32[]{:S(2)}) collective-permute-start(bf16[1,6,256,256]{3,2,1,0:T(8,128)(2,1)} %get-tuple-element.64), channel_id=1, source_target_pairs={{8,0},{16,8},{24,16},{9,1},{17,9},{25,17},{10,2},{18,10},{26,18},{... | collective-permute-start | bytes 2359304 | tf_op jit(solution)/shard_map/ppermute | solution.py:24
  264.2 1.4 copy-start.1
where the time goes:
time: 271 us; the launch traced here: 266 us
  waiting for transfers between devices  114 us (42%)
  matrix products  97.3 us (36%)
  starting transfers between devices  27.9 us (10%)
  other arithmetic  17.2 us (6%)
  local copies, waits for them, and re-layouts  8.37 us (3%)
    all_to_all x1, waiting for transfers between devices, on_device(): lax.all_to_all(arrange(batch_gram), 'lon', split_axis=0, concat_axis=0, t...  90.3 us
    dot_general x24, matrix products, accumulate(): jnp.dot(deviation, matrix, preferred_element_type=jnp.float32)  33.2 us
    ppermute x2, waiting for transfers between devices, extended(): before = lax.ppermute(last, axis, up)  15.4 us
    dot_general x6, matrix products, point_transforms(): jnp.einsum('pij,pjk->pik', factor, inverse_root, precision=highest)  13.9 us
    dot_general x6, matrix products, point_transforms(): jnp.einsum('pij,pjk->pik', inverse_root, iterate, precision=highest)  13.7 us
    dot_general x1, matrix products, batch_moments(): jnp.einsum('...ok,...ol->...kl', scaled, pert_rows, preferred_element_typ...  12.1 us
    dot_general x5, matrix products, point_transforms(): iterate = jnp.einsum('pij,pjk->pik', iterate, factor, precision=highest)  12 us
    ppermute x2, waiting for transfers between devices, extended(): after = lax.ppermute(initial, axis, down)  7.23 us
  transfers between devices with their start and end apart: 7, of which 6 were waited for; matrix products, arithmetic and copies ran while one was open for 11% of the time, Pallas kernels for 0%

commit v1 on v0

v1 whole, which is shorter than its diff:
```python
import functools

import jax
import jax.numpy as jnp
from jax import lax
from jax.experimental import pallas as pl
from jax.experimental.pallas import tpu as pltpu
from jax.sharding import PartitionSpec as P

CAP = 4
PLAT = 2
PLON = 4
POINTS = PLAT * PLON
ITERS = 6
HALF = 128
MEMBERS = 2 * HALF
TILE = 16
BLOCK = CAP * MEMBERS + TILE
PACKED = MEMBERS + TILE
F32 = jnp.float32
BF16 = jnp.bfloat16
VMEM_LIMIT = 56 * 1024 * 1024

SMEM_SPEC = pl.BlockSpec(memory_space=pltpu.SMEM)
VMEM_SPEC = pl.BlockSpec(memory_space=pltpu.VMEM)
ANY_SPEC = pl.BlockSpec(memory_space=pl.ANY)


def params():
    return pltpu.CompilerParams(vmem_limit_bytes=VMEM_LIMIT)


def dot_nn(a, b):
    return lax.dot_general(a, b, (((1,), (0,)), ((), ())), preferred_element_type=F32)


def dot_nt(a, b):
    return lax.dot_general(a, b, (((1,), (1,)), ((), ())), preferred_element_type=F32)


def iota(shape, dim):
    return lax.broadcasted_iota(jnp.int32, shape, dim)


def partner_of(me, offset, lon_size):
    if lon_size & (lon_size - 1) == 0:
        return me ^ offset
    return lax.rem(me + offset, lon_size)


def partner_pairs(offset, lon_size):
    if lon_size & (lon_size - 1) == 0:
        return [(i, i ^ offset) for i in range(lon_size)]
    return [(i, (i + offset) % lon_size) for i in range(lon_size)]


def gram_kernel(first, count, lon_size, me_ref, owner_ref, len_ref, points_ref, num_ref,
                weight_ref, innov_ref, taper_ref, pert_ref, *rest):
    outs, (source, filled, rows, w32, i32, t32, built, in_sem, out_sem) = rest[:count], rest[count:]
    held = pert_ref.shape[0]
    me = me_ref[0]
    nobs = pert_ref.shape[1]

    @pl.loop(0, lon_size * CAP)
    def _(s):
        source[s] = -1

    @pl.loop(0, lon_size)
    def _(k):
        filled[k] = 0

    @pl.loop(0, held)
    def _(b):
        owner = owner_ref[b, 0]
        if lon_size & (lon_size - 1) == 0:
            k = owner ^ me
        else:
            k = lax.rem(owner - me + lon_size, lon_size)
        n = filled[k]
        source[k * CAP + n] = b
        filled[k] = n + 1

    def fetch(k, j):
        b = jnp.maximum(source[k * CAP + j], 0)
        return pltpu.make_async_copy(pert_ref.at[b], rows.at[j], in_sem.at[j])

    for j in range(CAP):
        fetch(first, j).start()
    w32[...] = weight_ref[...].astype(F32)
    i32[...] = innov_ref[...].astype(F32)
    t32[:, 0:3] = taper_ref[...].astype(F32)
    lane_obs = iota((1, nobs), 1)
    lane = iota((1, HALF), 1)
    row_id = iota((HALF, HALF), 0)
    col_id = iota((HALF, HALF), 1)

    @pl.loop(0, count)
    def _(step):
        k = first + step
        lo, hi, dg, cf = [], [], [], []
        for j in range(CAP):
            b = source[k * CAP + j]
            present = b >= 0
            b = jnp.maximum(b, 0)
            fetch(k, j).wait()
            live = jnp.where(present, len_ref[0, b], 0)
            keep = jnp.where(lane_obs < live, w32[pl.ds(b, 1), :], 0.0)
            pulled = (keep * i32[pl.ds(b, 1), :]).astype(BF16)
            x = rows[j]
            xt = x.T
            scaled = xt * keep.astype(BF16)
            lhs = jnp.concatenate([scaled, jnp.broadcast_to(pulled, (TILE, nobs))], axis=0)
            gram = dot_nn(lhs, x)
            a11 = gram[0:HALF, 0:HALF]
            a22 = gram[HALF:MEMBERS, HALF:MEMBERS]
            built[step, pl.ds(j * MEMBERS, HALF), :] = jnp.where(row_id <= col_id, a11, a22).astype(BF16)
            built[step, pl.ds(j * MEMBERS + HALF, HALF), :] = gram[0:HALF, HALF:MEMBERS].astype(BF16)
            lo.append(gram[MEMBERS:MEMBERS + 1, 0:HALF])
            hi.append(gram[MEMBERS:MEMBERS + 1, HALF:MEMBERS])
            dg.append(jnp.sum(jnp.where(row_id == col_id, a22, 0.0), axis=0, keepdims=True))
            taper = t32[pl.ds(b, 1), :]
            limit = jnp.where(present, num_ref[b], 0)
            coef = jnp.zeros((1, HALF), F32)
            for q in range(3):
                hit = (lane == points_ref[b, q]) & (q < limit)
                coef = coef + jnp.where(hit, taper[:, q:q + 1], 0.0)
            cf.append(coef)

            @pl.when(step + 1 < count)
            def _():
                fetch(k + 1, j).start()

        built[step, pl.ds(CAP * MEMBERS, TILE), :] = jnp.concatenate(lo + hi + dg + cf, axis=0).astype(BF16)
        for i in range(count):
            @pl.when(step == i)
            def _():
                pltpu.make_async_copy(built.at[i], outs[i], out_sem.at[i]).start()

    for i in range(count):
        pltpu.make_async_copy(built.at[i], outs[i], out_sem.at[i]).wait()


def batch_blocks(first, count, lon_size, me, owner, length, points, num, weight, innov, taper, pert):
    held, nobs, members = pert.shape
    return pl.pallas_call(
        functools.partial(gram_kernel, first, count, lon_size),
        out_shape=[jax.ShapeDtypeStruct((BLOCK, HALF), BF16)] * count,
        in_specs=[SMEM_SPEC] * 5 + [VMEM_SPEC] * 3 + [ANY_SPEC],
        out_specs=[ANY_SPEC] * count,
        scratch_shapes=[
            pltpu.SMEM((lon_size * CAP,), jnp.int32),
            pltpu.SMEM((lon_size,), jnp.int32),
            pltpu.VMEM((CAP, nobs, members), BF16),
            pltpu.VMEM((held, nobs), F32),
            pltpu.VMEM((held, nobs), F32),
            pltpu.VMEM((held, HALF), F32),
            pltpu.VMEM((count, BLOCK, HALF), BF16),
            pltpu.SemaphoreType.DMA((CAP,)),
            pltpu.SemaphoreType.DMA((count,)),
        ],
        compiler_params=params(),
        cost_estimate=pl.CostEstimate(
            flops=count * CAP * 2 * nobs * members * members,
            bytes_accessed=count * CAP * nobs * members * 2, transcendentals=0),
    )(me, owner, length, points, num, weight, innov, taper, pert)


def unpack(triangle, corner, diagonal):
    row_id = iota((HALF, HALF), 0)
    col_id = iota((HALF, HALF), 1)
    flipped = triangle.T
    a11 = jnp.where(row_id <= col_id, triangle, flipped)
    a22 = jnp.where(row_id > col_id, triangle, jnp.where(row_id == col_id, diagonal, flipped))
    return jnp.concatenate(
        [jnp.concatenate([a11, corner], axis=1), jnp.concatenate([corner.T, a22], axis=1)], axis=0)


def mm(a, b):
    return dot_nn(a.astype(BF16), b.astype(BF16))


def transform_points(listed, total_of, side_of, wz, out_of):
    eye = (iota((MEMBERS, MEMBERS), 0) == iota((MEMBERS, MEMBERS), 1)).astype(F32)
    scales = []
    for i, p in enumerate(listed):
        packed = total_of(p)
        system = unpack(packed[0:HALF], packed[HALF:MEMBERS], side_of(p)[2]) + (MEMBERS - 1) * eye
        square = jnp.sum(jnp.sum(system * system, axis=0, keepdims=True), axis=1, keepdims=True)
        inv = lax.rsqrt(square)
        inv = inv * (1.5 - 0.5 * square * inv * inv)
        scales.append(inv)
        wz[0, i] = system * inv
        wz[1, i] = 1.5 * eye - 0.5 * wz[0, i]
    count = len(listed)

    def advance(i):
        w = wz[0, i]
        wb = w.astype(BF16)
        u = dot_nn(wb, wb)
        wz[0, i] = 2.25 * w - 1.5 * u + 0.25 * dot_nn(wb, u.astype(BF16))

    def apply(i):
        z = wz[1, i]
        wz[1, i] = 1.5 * z - 0.5 * mm(wz[0, i], z)

    for i in range(count):
        advance(i)

    @pl.loop(0, ITERS - 2)
    def _(sweep):
        for i in range(count):
            apply(i)
            advance(i)

    for i in range(count):
        apply(i)
    row_id = iota((HALF, HALF), 0)
    col_id = iota((HALF, HALF), 1)
    for i, p in enumerate(listed):
        root = wz[1, i]
        low, high, _ = side_of(p)
        shift = jnp.concatenate([low, high], axis=1)
        inner = jnp.sum(root * shift, axis=1, keepdims=True)
        mean_weight = jnp.sum(root * inner, axis=0, keepdims=True) * scales[i]
        result = root * jnp.sqrt((MEMBERS - 1) * scales[i])
        a22 = result[HALF:MEMBERS, HALF:MEMBERS]
        ref, where = out_of(p)
        ref[where, pl.ds(0, HALF), :] = jnp.where(row_id <= col_id, result[0:HALF, 0:HALF], a22).astype(BF16)
        ref[where, pl.ds(HALF, HALF), :] = result[0:HALF, HALF:MEMBERS].astype(BF16)
        diagonal = jnp.sum(jnp.where(row_id == col_id, a22, 0.0), axis=0, keepdims=True)
        extra = jnp.concatenate(
            [diagonal, mean_weight[:, 0:HALF], mean_weight[:, HALF:MEMBERS], jnp.zeros((TILE - 3, HALF), F32)],
            axis=0)
        ref[where, pl.ds(MEMBERS, TILE), :] = extra.astype(BF16)


def edge_kernel(lon_size, *refs):
    blocks = refs[:lon_size]
    left_ref, right_ref, total_ref, side_ref, wz, acc = refs[lon_size:]
    slots = lon_size * CAP
    extras = [blk[pl.ds(CAP * MEMBERS, TILE), :].astype(F32) for blk in blocks]
    low, high, diag, coef = [
        jnp.concatenate([e[CAP * q:CAP * (q + 1)] for e in extras], axis=0).astype(BF16) for q in range(4)]
    pick = (iota((POINTS, HALF), 0) == iota((POINTS, HALF), 1)).astype(BF16)
    by_point = dot_nt(pick, coef).astype(BF16)
    for q, part in enumerate((low, high, diag)):
        side_ref[q] = dot_nn(by_point, part)
    spread = (iota((POINTS * TILE, HALF), 0) // TILE == iota((POINTS * TILE, HALF), 1)).astype(BF16)
    tall = dot_nt(spread, coef).astype(BF16)
    wide = (iota((slots, slots * TILE), 1) // TILE == iota((slots, slots * TILE), 0)).astype(BF16)
    mixing = dot_nn(tall, wide)
    shape = (POINTS * TILE, slots * TILE)
    mixing = jnp.where(iota(shape, 0) % TILE == iota(shape, 1) % TILE, mixing, 0.0).astype(BF16)
    for g in range(0, MEMBERS // TILE, 2):
        pair = []
        for h in (g, g + 1):
            pair.append(jnp.concatenate(
                [blk[pl.ds(j * MEMBERS + h * TILE, TILE), :] for blk in blocks for j in range(CAP)], axis=0))
        summed = dot_nn(mixing, jnp.concatenate(pair, axis=1))
        for p in range(POINTS):
            for h in (0, 1):
                acc[p, pl.ds((g + h) * TILE, TILE), :] = summed[p * TILE:(p + 1) * TILE, h * HALF:(h + 1) * HALF]
    edge = [r * PLON + c for r in range(PLAT) for c in (0, PLON - 1)]
    inner = [p for p in range(POINTS) if p not in edge]
    for i, p in enumerate(inner):
        total_ref[i] = acc[p]
    transform_points(
        edge,
        lambda p: acc[p],
        lambda p: [side_ref[q, pl.ds(p, 1), :] for q in range(3)],
        wz,
        lambda p: (left_ref if p % PLON == 0 else right_ref, p // PLON))


def inner_kernel(total_in, side_in, out_ref, wz):
    edge = [r * PLON + c for r in range(PLAT) for c in (0, PLON - 1)]
    inner = [p for p in range(POINTS) if p not in edge]
    transform_points(
        inner,
        lambda p: total_in[inner.index(p)],
        lambda p: [side_in[q, pl.ds(p, 1), :] for q in range(3)],
        wz,
        lambda p: (out_ref, inner.index(p)))


def edge_transforms(blocks):
    lon_size = len(blocks)
    columns = jax.ShapeDtypeStruct((PLAT, PACKED, HALF), BF16)
    return pl.pallas_call(
        functools.partial(edge_kernel, lon_size),
        out_shape=[
            columns, columns,
            jax.ShapeDtypeStruct((POINTS - 2 * PLAT, MEMBERS, HALF), F32),
            jax.ShapeDtypeStruct((3, POINTS, HALF), F32),
        ],
        in_specs=[VMEM_SPEC] * lon_size,
        out_specs=[VMEM_SPEC] * 4,
        scratch_shapes=[
            pltpu.VMEM((2, 2 * PLAT, MEMBERS, MEMBERS), F32),
            pltpu.VMEM((POINTS, MEMBERS, HALF), F32),
        ],
        compiler_params=params(),
    )(*blocks)


def inner_transforms(total, side):
    count = total.shape[0]
    return pl.pallas_call(
        inner_kernel,
        out_shape=jax.ShapeDtypeStruct((count, PACKED, HALF), BF16),
        in_specs=[VMEM_SPEC] * 2,
        out_specs=VMEM_SPEC,
        scratch_shapes=[pltpu.VMEM((2, count, MEMBERS, MEMBERS), F32)],
        compiler_params=params(),
        cost_estimate=pl.CostEstimate(
            flops=count * 15 * 2 * MEMBERS ** 3, bytes_accessed=count * MEMBERS * HALF * 6, transcendentals=0),
    )(total, side)


def cell_kernel(point_cols, pos_ref, stencil_ref, frac_ref, field_ref, dev_ref, weight_ref):
    rows, width = stencil_ref.shape[1:]
    lat_pos, lon_pos = pos_ref[0], pos_ref[1]
    wide = PLON + 2
    ids = iota((HALF, width), 0)

    @pl.loop(0, rows)
    def _(i):
        x = field_ref[i].astype(F32)
        mean = jnp.mean(x, axis=1, keepdims=True)
        dev_ref[i] = (x - mean).astype(BF16)
        row_off = stencil_ref[0, pl.ds(i, 1), :] - (lat_pos * PLAT - 1)
        col_off = stencil_ref[1, pl.ds(i, 1), :] - (lon_pos * PLON - 1)
        col_off = jnp.where(col_off < 0, col_off + point_cols, col_off)
        col_off = jnp.where(col_off >= point_cols, col_off - point_cols, col_off)
        y = frac_ref[0, pl.ds(i, 1), :]
        x_frac = frac_ref[1, pl.ds(i, 1), :]
        corner = row_off * wide + col_off
        weights = jnp.where(corner == ids, (1.0 - y) * (1.0 - x_frac), 0.0)
        weights = weights + jnp.where(corner + wide == ids, y * (1.0 - x_frac), 0.0)
        weights = weights + jnp.where(corner + 1 == ids, (1.0 - y) * x_frac, 0.0)
        weights = weights + jnp.where(corner + wide + 1 == ids, y * x_frac, 0.0)
        turned = weights.T
        weight_ref[i] = jnp.where(iota((width, HALF), 1) == HALF - 1, mean, turned)


def cell_parts(point_cols, pos, stencil, frac, background):
    rows, width, members = background.shape
    return pl.pallas_call(
        functools.partial(cell_kernel, point_cols),
        out_shape=[
            jax.ShapeDtypeStruct((rows, width, members), BF16),
            jax.ShapeDtypeStruct((rows, width, HALF), F32),
        ],
        in_specs=[SMEM_SPEC] + [VMEM_SPEC] * 3,
        out_specs=[VMEM_SPEC] * 2,
        compiler_params=params(),
        cost_estimate=pl.CostEstimate(
            flops=rows * width * members * 4, bytes_accessed=rows * width * members * 6, transcendentals=0),
    )(pos, stencil, frac, background)


def mix_kernel(groups, final, tile_rows, *refs):
    n = len(groups)
    packed_refs = refs[:n]
    dev_ref, weight_ref = refs[n:n + 2]
    rest = refs[n + 2:]
    if final:
        base_ref, out_ref, matrices, lhs = rest
    else:
        out_ref, matrices, lhs = rest
    ids, extra_low, extra_high = [], [], []
    for ref, group in zip(packed_refs, groups):
        for i, point in enumerate(group):
            extra = ref[i, pl.ds(MEMBERS, TILE), :].astype(F32)
            full = unpack(
                ref[i, pl.ds(0, HALF), :].astype(F32), ref[i, pl.ds(HALF, HALF), :].astype(F32), extra[0:1])
            matrices[pl.ds(len(ids) * MEMBERS, MEMBERS), :] = full.astype(BF16)
            extra_low.append(extra[1:2])
            extra_high.append(extra[2:3])
            ids.append(point)
    count = len(ids)
    pad = jnp.zeros((HALF - count, HALF), F32)
    shifts = jnp.concatenate(
        [jnp.concatenate(extra_low + [pad], axis=0), jnp.concatenate(extra_high + [pad], axis=0)],
        axis=1).astype(BF16)
    rows, width, members = dev_ref.shape

    @pl.loop(0, rows // tile_rows)
    def _(t):
        dev_all = dev_ref[pl.ds(t * tile_rows, tile_rows)].reshape(tile_rows * width, members)
        weights = weight_ref[pl.ds(t * tile_rows, tile_rows)].reshape(tile_rows * width, HALF)
        spread = dev_all.astype(F32)
        shifted = dot_nt(dev_all, shifts)
        moved = jnp.zeros((tile_rows * width, 1), F32)
        for i, point in enumerate(ids):
            column = weights[:, point:point + 1]
            lhs[:, i * MEMBERS:(i + 1) * MEMBERS] = (spread * column).astype(BF16)
            moved = moved + column * shifted[:, i:i + 1]
        value = dot_nn(lhs[...], matrices[...]) + moved
        if final:
            value = value + weights[:, HALF - 1:HALF]
            value = value.reshape(tile_rows, width, members) + base_ref[pl.ds(t * tile_rows, tile_rows)]
            out_ref[pl.ds(t * tile_rows, tile_rows)] = value.astype(out_ref.dtype)
        else:
            out_ref[pl.ds(t * tile_rows, tile_rows)] = value.reshape(tile_rows, width, members)


def mix(groups, packed, dev, weights, base=None):
    rows, width, members = dev.shape
    count = sum(len(g) for g in groups)
    final = base is not None
    tile_rows = 2
    args = list(packed) + [dev, weights] + ([base] if final else [])
    return pl.pallas_call(
        functools.partial(mix_kernel, groups, final, tile_rows),
        out_shape=jax.ShapeDtypeStruct(dev.shape, BF16 if final else F32),
        in_specs=[VMEM_SPEC] * len(args),
        out_specs=VMEM_SPEC,
        scratch_shapes=[
            pltpu.VMEM((count * MEMBERS, MEMBERS), BF16),
            pltpu.VMEM((tile_rows * width, count * MEMBERS), BF16),
        ],
        compiler_params=params(),
        cost_estimate=pl.CostEstimate(
            flops=2 * rows * width * members * members * count,
            bytes_accessed=rows * width * members * 8, transcendentals=0),
    )(*args)


def on_device(obs_pert, obs_weight, innovation, batch_len, batch_owner, batch_points, batch_count,
              batch_taper, background, stencil, frac):
    lon_size, lat_size = lax.axis_size("lon"), lax.axis_size("lat")
    lat_pos, lon_pos = lax.axis_index("lat"), lax.axis_index("lon")
    me = lon_pos.astype(jnp.int32).reshape(1)
    pos = jnp.stack([lat_pos, lon_pos]).astype(jnp.int32)
    fixed = (me, batch_owner, batch_len, batch_points, batch_count, obs_weight, innovation, batch_taper, obs_pert)
    half = max(lon_size // 2, 1)
    far = batch_blocks(half, lon_size - half, lon_size, *fixed)
    got = [lax.ppermute(b, "lon", partner_pairs(half + i, lon_size)) for i, b in enumerate(far)]
    near = batch_blocks(0, half, lon_size, *fixed)
    got += [near[0]] + [lax.ppermute(b, "lon", partner_pairs(i, lon_size)) for i, b in enumerate(near) if i]
    dev, weights = cell_parts(PLON * lon_size, pos, stencil, frac, background)

    left, right, total, side = edge_transforms(got)
    up = [(i, (i + 1) % lon_size) for i in range(lon_size)]
    down = [(j, i) for i, j in up]
    before = lax.ppermute(right, "lon", up)
    after = lax.ppermute(left, "lon", down)
    inner = inner_transforms(total, side)
    inner_cols = PLON - 2

    def row_of(r):
        return jnp.concatenate(
            [before[r:r + 1], left[r:r + 1], inner[r * inner_cols:(r + 1) * inner_cols], right[r:r + 1],
             after[r:r + 1]], axis=0)

    north = [(i, i + 1) for i in range(lat_size - 1)]
    south = [(j, i) for i, j in north]
    below = lax.ppermute(row_of(PLAT - 1), "lat", north)
    above = lax.ppermute(row_of(0), "lat", south)
    wide = PLON + 2

    def ident(r, c):
        return (r + 1) * wide + c + 1

    own = [
        [ident(r, -1) for r in range(PLAT)],
        [ident(r, 0) for r in range(PLAT)],
        [ident(r, c) for r in range(PLAT) for c in range(1, PLON - 1)],
        [ident(r, PLON - 1) for r in range(PLAT)],
        [ident(r, PLON) for r in range(PLAT)],
    ]
    partial = mix(own, [before, left, inner, right, after], dev, weights)
    rims = [[ident(-1, c) for c in range(-1, PLON + 1)], [ident(PLAT, c) for c in range(-1, PLON + 1)]]
    return mix(rims, [below, above], dev, weights, partial)


def solution(mesh):
    return jax.shard_map(
        on_device,
        mesh=mesh,
        in_specs=(
            P(("lat", "lon"), None, None),
            P(("lat", "lon"), None),
            P(("lat", "lon"), None),
            P(("lat", "lon"), None),
            P(("lat", "lon"), None),
            P(("lat", "lon"), None),
            P(("lat", "lon")),
            P(("lat", "lon"), None),
            P("lat", "lon", None),
            P(None, "lat", "lon"),
            P(None, "lat", "lon"),
        ),
        out_specs=P("lat", "lon", None),
        check_vma=False,
    )
```

time: 271 us -> 117 us (0.43); the launches traced: 266 us -> 117 us
  matrix products: 97.3 us -> 0 us
  waiting for transfers between devices: 114 us -> 30.6 us
  Pallas kernels: 0 us -> 54.8 us
  other arithmetic: 17.2 us -> 0.67 us
  starting transfers between devices: 27.9 us -> 21.9 us
    dot_general x47 -> x0, matrix products: 97.3 us -> none  [the longest x24 33.2 us: accumulate(): jnp.dot(deviation, matrix, preferred_element_type=jnp.float32)]
    all_to_all x3 -> x0, waiting for transfers between devices: 91.1 us -> none  [the longest x1 90.3 us: on_device(): lax.all_to_all(arrange(batch_gram), 'lon', split_axis=0, concat_axis=0, t...]
    pallas_call x0 -> x7, Pallas kernels: none -> 54.8 us  [the longest x2 17.8 us: batch_blocks(): pl.pallas_call(functools.partial(gram_kernel, first, count, lon_size), ou...]
    all_to_all x3 -> x0, starting transfers between devices: 17.1 us -> none  [the longest x1 6.35 us: on_device(): lax.all_to_all(arrange(coef), 'lon', split_axis=0, concat_axis=0, tiled=T...]
    ppermute x4 -> x11, starting transfers between devices: 10.8 us -> 21.9 us  [the longest x4 7.51 us: on_device(): lax.ppermute(b, 'lon', partner_pairs(half + i, lon_size))]
    unnamed x14 -> x31, local copies, waits for them, and re-layouts: 0.03 us -> 8.3 us
    ppermute x4 -> x11, waiting for transfers between devices: 22.6 us -> 30.6 us  [the longest x4 19.9 us: on_device(): lax.ppermute(b, 'lon', partner_pairs(half + i, lon_size))]
    gather x4 -> x0, local copies, waits for them, and re-layouts: 6.17 us -> none  [arrange(): taken = jnp.take(values, source_row, axis=0)]
  transfers between devices with their start and end apart: 7 -> 11, of which waited for: 6 -> 4; matrix products, arithmetic and copies ran while one was open for 11% -> 2% of each run, Pallas kernels for 0% -> 25%
where the time goes in v1:
time: 117 us
  Pallas kernels  54.8 us (47%)
  waiting for transfers between devices  30.6 us (26%)
  starting transfers between devices  21.9 us (19%)
  local copies, waits for them, and re-layouts  8.32 us (7%)
    ppermute x4, waiting for transfers between devices, on_device(): lax.ppermute(b, 'lon', partner_pairs(half + i, lon_size))  19.9 us
    pallas_call x2, Pallas kernels, batch_blocks(): pl.pallas_call(functools.partial(gram_kernel, first, count, lon_size), ou...  17.8 us
    pallas_call x2, Pallas kernels, mix(): pl.pallas_call(functools.partial(mix_kernel, groups, final, tile_rows), o...  16.3 us
    ppermute x3, waiting for transfers between devices, on_device(): lax.ppermute(b, 'lon', partner_pairs(i, lon_size))  10.7 us
    pallas_call x1, Pallas kernels, edge_transforms(): pl.pallas_call(functools.partial(edge_kernel, lon_size), out_shape=[colum...  9.48 us
    unnamed x31, local copies, waits for them, and re-layouts  8.3 us
    pallas_call x1, Pallas kernels, inner_transforms(): pl.pallas_call(inner_kernel, out_shape=jax.ShapeDtypeStruct((count, PACKE...  8.12 us
    ppermute x4, starting transfers between devices, on_device(): lax.ppermute(b, 'lon', partner_pairs(half + i, lon_size))  7.51 us
  transfers between devices with their start and end apart: 11, of which 4 were waited for; matrix products, arithmetic and copies ran while one was open for 2% of the time, Pallas kernels for 25%

profile of v1, /device:TPU:1, one launch (start us, length us, event | category | flops | bytes accessed | tf_op | source)
XLA Modules:
  0.0 116.5 jit_solution(4797502961622156593)
XLA Ops:
  0.0 1.3 %copy.12.owner_ref = s32[32,1]{1,0:T(8,128)} copy(s32[32,1]{0,1:T(1,128)} %param.15) | data formatting | bytes 256 | tf_op args[4]
  1.3 1.4 %copy.13.points_ref = s32[32,3]{1,0:T(8,128)} copy(s32[32,3]{0,1:T(4,128)} %param.16) | data formatting | bytes 768 | tf_op args[5]
  2.7 1.4 %copy.14.taper_ref = bf16[32,3]{1,0:T(8,128)(2,1)} copy(bf16[32,3]{0,1:T(4,128)(2,1)} %param.18) | data formatting | bytes 384 | tf_op args[7]
  4.0 8.9 %shard_map.109 = (bf16[1040,128]{1,0:T(8,128)(2,1)}, bf16[1040,128]{1,0:T(8,128)(2,1)}, bf16[1040,128]{1,0:T(8,128)(2,1)}, bf16[1040,128]{1,0:T(8,128)(2,1)}) custom-call(s32[1]{0:T(128)} %bitcast.me_ref, s32[32,1]{1,0:T(8,128)} %copy.12.owner_ref, s32[1,32]{1,0:T(1,128)} %len_ref.3, s32[32,3]{1,0:T(8,128)} %copy.13.points_ref, s32[32]{0:T(128)} %num_ref.3, ...), custom_call_target="tpu_custom_call" | custom-call | flops 1073741824 | bytes 4194304 | tf_op jit(solution)/shard_map/pallas_call | solution.py:145
  13.0 3.2 %collective-permute-start = (bf16[1040,128]{1,0:T(8,128)(2,1)}, bf16[1040,128]{1,0:T(8,128)(2,1)S(1)}, u32[]{:S(2)}, u32[]{:S(2)}) collective-permute-start(bf16[1040,128]{1,0:T(8,128)(2,1)} %get-tuple-element.19), channel_id=1, source_target_pairs={{0,4},{1,5},{2,6},{3,7},{4,0},{5,1},{6,2},{7,3},{8,12},{9,13},{10,... | collective-permute-start | bytes 798728 | tf_op jit(solution)/shard_map/ppermute | solution.py:439
  16.2 1.0 collective-permute-start.1
  17.2 3.3 %collective-permute-start.2 = (bf16[1040,128]{1,0:T(8,128)(2,1)}, bf16[1040,128]{1,0:T(8,128)(2,1)S(1)}, u32[]{:S(2)}, u32[]{:S(2)}) collective-permute-start(bf16[1040,128]{1,0:T(8,128)(2,1)} %get-tuple-element.21), channel_id=1, source_target_pairs={{0,6},{1,7},{2,4},{3,5},{4,2},{5,3},{6,0},{7,1},{8,14},{9,15},{10,... | collective-permute-start | bytes 798728 | tf_op jit(solution)/shard_map/ppermute | solution.py:439
  20.5 0.0 collective-permute-start.3
  20.5 8.9 %shard_map.110 = (bf16[1040,128]{1,0:T(8,128)(2,1)}, bf16[1040,128]{1,0:T(8,128)(2,1)}, bf16[1040,128]{1,0:T(8,128)(2,1)}, bf16[1040,128]{1,0:T(8,128)(2,1)}) custom-call(s32[1]{0:T(128)} %bitcast.me_ref, s32[32,1]{1,0:T(8,128)} %copy.12.owner_ref, s32[1,32]{1,0:T(1,128)} %len_ref.3, s32[32,3]{1,0:T(8,128)} %copy.13.points_ref, s32[32]{0:T(128)} %num_ref.3, ...), custom_call_target="tpu_custom_call" | custom-call | flops 1073741824 | bytes 4194304 | tf_op jit(solution)/shard_map/pallas_call | solution.py:145
  29.4 1.2 %collective-permute-start.4 = (bf16[1040,128]{1,0:T(8,128)(2,1)}, bf16[1040,128]{1,0:T(8,128)(2,1)S(1)}, u32[]{:S(2)}, u32[]{:S(2)}) collective-permute-start(bf16[1040,128]{1,0:T(8,128)(2,1)} %get-tuple-element.24), channel_id=1, source_target_pairs={{0,1},{1,0},{2,3},{3,2},{4,5},{5,4},{6,7},{7,6},{8,9},{9,8},{10,11... | collective-permute-start | bytes 798728 | tf_op jit(solution)/shard_map/ppermute | solution.py:441
  30.6 14.7 %collective-permute-done.refs_0_ = bf16[1040,128]{1,0:T(8,128)(2,1)S(1)} collective-permute-done((bf16[1040,128]{1,0:T(8,128)(2,1)}, bf16[1040,128]{1,0:T(8,128)(2,1)S(1)}, u32[]{:S(2)}, u32[]{:S(2)}) %collective-permute-start) | collective-permute-done | bytes 266272 | tf_op jit(solution)/shard_map/ppermute | solution.py:439
  45.3 1.3 %collective-permute-start.5 = (bf16[1040,128]{1,0:T(8,128)(2,1)}, bf16[1040,128]{1,0:T(8,128)(2,1)S(1)}, u32[]{:S(2)}, u32[]{:S(2)}) collective-permute-start(bf16[1040,128]{1,0:T(8,128)(2,1)} %get-tuple-element.25), channel_id=1, source_target_pairs={{0,2},{1,3},{2,0},{3,1},{4,6},{5,7},{6,4},{7,5},{8,10},{9,11},{10,... | collective-permute-start | bytes 798728 | tf_op jit(solution)/shard_map/ppermute | solution.py:441
  46.6 5.2 %collective-permute-done.1.refs_1_ = bf16[1040,128]{1,0:T(8,128)(2,1)S(1)} collective-permute-done((bf16[1040,128]{1,0:T(8,128)(2,1)}, bf16[1040,128]{1,0:T(8,128)(2,1)S(1)}, u32[]{:S(2)}, u32[]{:S(2)}) %collective-permute-start.1) | collective-permute-done | bytes 266272 | tf_op jit(solution)/shard_map/ppermute | solution.py:439
  51.8 1.5 %collective-permute-start.6 = (bf16[1040,128]{1,0:T(8,128)(2,1)}, bf16[1040,128]{1,0:T(8,128)(2,1)S(1)}, u32[]{:S(2)}, u32[]{:S(2)}) collective-permute-start(bf16[1040,128]{1,0:T(8,128)(2,1)} %get-tuple-element.26), channel_id=1, source_target_pairs={{0,3},{1,2},{2,1},{3,0},{4,7},{5,6},{6,5},{7,4},{8,11},{9,10},{10,... | collective-permute-start | bytes 798728 | tf_op jit(solution)/shard_map/ppermute | solution.py:441
  53.3 0.0 collective-permute-done.2.refs_2_
  53.4 4.1 %collective-permute-done.5.refs_6_ = bf16[1040,128]{1,0:T(8,128)(2,1)S(1)} collective-permute-done((bf16[1040,128]{1,0:T(8,128)(2,1)}, bf16[1040,128]{1,0:T(8,128)(2,1)S(1)}, u32[]{:S(2)}, u32[]{:S(2)}) %collective-permute-start.5) | collective-permute-done | bytes 266272 | tf_op jit(solution)/shard_map/ppermute | solution.py:441
  57.5 6.6 %collective-permute-done.6.refs_7_ = bf16[1040,128]{1,0:T(8,128)(2,1)S(1)} collective-permute-done((bf16[1040,128]{1,0:T(8,128)(2,1)}, bf16[1040,128]{1,0:T(8,128)(2,1)S(1)}, u32[]{:S(2)}, u32[]{:S(2)}) %collective-permute-start.6) | collective-permute-done | bytes 266272 | tf_op jit(solution)/shard_map/ppermute | solution.py:441
  64.1 0.7 copy-done.6
  64.8 9.5 %shard_map.111 = (bf16[2,272,128]{2,1,0:T(8,128)(2,1)}, bf16[2,272,128]{2,1,0:T(8,128)(2,1)}, f32[4,256,128]{2,1,0:T(8,128)}, f32[3,8,128]{2,1,0:T(8,128)}) custom-call(bf16[1040,128]{1,0:T(8,128)(2,1)} %copy-done, bf16[1040,128]{1,0:T(8,128)(2,1)} %copy-done.1, bf16[1040,128]{1,0:T(8,128)(2,1)} %copy-done.2, bf16[1040,128]{1,0:T(8,128)(2,1)} %copy-done.3, ...), custom_call_target="tpu_custom_call" | custom-call | tf_op jit(solution)/shard_map/pallas_call | solution.py:289
  74.3 0.4 collective-permute-start.7
  74.7 3.9 %collective-permute-start.8 = (bf16[2,272,128]{2,1,0:T(8,128)(2,1)}, bf16[2,272,128]{2,1,0:T(8,128)(2,1)S(1)}, u32[]{:S(2)}, u32[]{:S(2)}) collective-permute-start(bf16[2,272,128]{2,1,0:T(8,128)(2,1)} %get-tuple-element.28.refs_1_), channel_id=1, source_target_pairs={{1,0},{2,1},{3,2},{4,3},{5,4},{6,5},{7,6},{0,7},{9,8},{10,9},{11,1... | collective-permute-start | bytes 417800 | tf_op jit(solution)/shard_map/ppermute | solution.py:448
  78.5 8.1 %shard_map.112.refs_2_ = bf16[4,272,128]{2,1,0:T(8,128)(2,1)} custom-call(f32[4,256,128]{2,1,0:T(8,128)} %get-tuple-element.29.total_in, f32[3,8,128]{2,1,0:T(8,128)} %get-tuple-element.30.side_in), custom_call_target="tpu_custom_call" | custom-call | flops 2013265920 | bytes 786432 | tf_op jit(solution)/shard_map/pallas_call | solution.py:308
  86.6 1.0 slice_dynamic-update-slice_fusion.7
  87.6 1.0 slice_dynamic-update-slice_fusion
  88.7 4.2 %collective-permute-start.9 = (bf16[6,272,128]{2,1,0:T(8,128)(2,1)S(1)}, bf16[6,272,128]{2,1,0:T(8,128)(2,1)S(1)}, u32[]{:S(2)}, u32[]{:S(2)}) collective-permute-start(bf16[6,272,128]{2,1,0:T(8,128)(2,1)S(1)} %get-tuple-element.36), channel_id=1, source_target_pairs={{0,8},{8,16},{16,24},{1,9},{9,17},{17,25},{2,10},{10,18},{18,26},{... | collective-permute-start | bytes 1253384 | tf_op jit(solution)/shard_map/ppermute | solution.py:459
  92.9 1.9 %collective-permute-start.10 = (bf16[6,272,128]{2,1,0:T(8,128)(2,1)S(1)}, bf16[6,272,128]{2,1,0:T(8,128)(2,1)S(1)}, u32[]{:S(2)}, u32[]{:S(2)}) collective-permute-start(bf16[6,272,128]{2,1,0:T(8,128)(2,1)S(1)} %get-tuple-element.35), channel_id=1, source_target_pairs={{8,0},{16,8},{24,16},{9,1},{17,9},{25,17},{10,2},{18,10},{26,18},{... | collective-permute-start | bytes 1253384 | tf_op jit(solution)/shard_map/ppermute | solution.py:460
  94.9 0.7 pad_add_fusion.pos_ref
  95.5 3.1 %shard_map.113 = (bf16[8,128,256]{2,1,0:T(8,128)(2,1)}, f32[8,128,128]{2,1,0:T(8,128)}) custom-call(s32[2]{0:T(128)} %pad_add_fusion.pos_ref, s32[2,8,128]{2,1,0:T(8,128)} %stencil_ref.1, f32[2,8,128]{2,1,0:T(8,128)} %frac_ref.1, bf16[8,128,256]{2,1,0:T(8,128)(2,1)} %field_ref.1), custom_call_target="tpu_custom_call" | custom-call | flops 1048576 | bytes 1572864 | tf_op jit(solution)/shard_map/pallas_call | solution.py:348
  98.7 9.0 %shard_map.114.refs_4_ = f32[8,128,256]{2,1,0:T(8,128)} custom-call(bf16[2,272,128]{2,1,0:T(8,128)(2,1)} %copy-done.8, bf16[2,272,128]{2,1,0:T(8,128)(2,1)} %get-tuple-element.28.refs_1_, bf16[4,272,128]{2,1,0:T(8,128)(2,1)} %shard_map.112.refs_2_, bf16[2,272,128]{2,1,0:T(8,128)(2,1)} %get-tuple-element.27.refs_3_, bf16[2,272,128]{2,1,0:T(8,128)(2,1)} %copy-done.9, ...), custom_call_target="tpu_custom_call" | custom-call | flops 1610612736 | bytes 2097152 | tf_op jit(solution)/shard_map/pallas_call | solution.py:414
  107.7 0.8 copy-done.10
  108.5 0.8 copy-done.11
  109.2 7.3 %shard_map.115 = bf16[8,128,256]{2,1,0:T(8,128)(2,1)} custom-call(bf16[6,272,128]{2,1,0:T(8,128)(2,1)} %copy-done.10, bf16[6,272,128]{2,1,0:T(8,128)(2,1)} %copy-done.11, bf16[8,128,256]{2,1,0:T(8,128)(2,1)} %get-tuple-element.31.refs_5_.refs_2_, f32[8,128,128]{2,1,0:T(8,128)} %get-tuple-element.32.refs_6_.refs_3_, f32[8,128,256]{2,1,0:T(8,128)} %shard_map.114.refs_4_), custom_call_target="tpu_custom_call" | custom-call | flops 1610612736 | bytes 2097152 | tf_op jit(solution)/shard_map/pallas_call | solution.py:414
  (30 shorter events, 0.1 us)
Async XLA Ops:
  13.0 32.3 %collective-permute-start = (bf16[1040,128]{1,0:T(8,128)(2,1)}, bf16[1040,128]{1,0:T(8,128)(2,1)S(1)}, u32[]{:S(2)}, u32[]{:S(2)}) collective-permute-start(bf16[1040,128]{1,0:T(8,128)(2,1)} %get-tuple-element.19), channel_id=1, source_target_pairs={{0,4},{1,5},{2,6},{3,7},{4,0},{5,1},{6,2},{7,3},{8,12},{9,13},{10,... | collective-permute-start | bytes 798728 | tf_op jit(solution)/shard_map/ppermute | solution.py:439
  16.2 35.6 %collective-permute-start.1 = (bf16[1040,128]{1,0:T(8,128)(2,1)}, bf16[1040,128]{1,0:T(8,128)(2,1)S(1)}, u32[]{:S(2)}, u32[]{:S(2)}) collective-permute-start(bf16[1040,128]{1,0:T(8,128)(2,1)} %get-tuple-element.20), channel_id=1, source_target_pairs={{0,5},{1,4},{2,7},{3,6},{4,1},{5,0},{6,3},{7,2},{8,13},{9,12},{10,... | collective-permute-start | bytes 798728 | tf_op jit(solution)/shard_map/ppermute | solution.py:439
  17.2 36.2 %collective-permute-start.2 = (bf16[1040,128]{1,0:T(8,128)(2,1)}, bf16[1040,128]{1,0:T(8,128)(2,1)S(1)}, u32[]{:S(2)}, u32[]{:S(2)}) collective-permute-start(bf16[1040,128]{1,0:T(8,128)(2,1)} %get-tuple-element.21), channel_id=1, source_target_pairs={{0,6},{1,7},{2,4},{3,5},{4,2},{5,3},{6,0},{7,1},{8,14},{9,15},{10,... | collective-permute-start | bytes 798728 | tf_op jit(solution)/shard_map/ppermute | solution.py:439
  20.5 32.9 %collective-permute-start.3 = (bf16[1040,128]{1,0:T(8,128)(2,1)}, bf16[1040,128]{1,0:T(8,128)(2,1)S(1)}, u32[]{:S(2)}, u32[]{:S(2)}) collective-permute-start(bf16[1040,128]{1,0:T(8,128)(2,1)} %get-tuple-element.22), channel_id=1, source_target_pairs={{0,7},{1,6},{2,5},{3,4},{4,3},{5,2},{6,1},{7,0},{8,15},{9,14},{10,... | collective-permute-start | bytes 798728 | tf_op jit(solution)/shard_map/ppermute | solution.py:439
  29.4 24.0 %collective-permute-start.4 = (bf16[1040,128]{1,0:T(8,128)(2,1)}, bf16[1040,128]{1,0:T(8,128)(2,1)S(1)}, u32[]{:S(2)}, u32[]{:S(2)}) collective-permute-start(bf16[1040,128]{1,0:T(8,128)(2,1)} %get-tuple-element.24), channel_id=1, source_target_pairs={{0,1},{1,0},{2,3},{3,2},{4,5},{5,4},{6,7},{7,6},{8,9},{9,8},{10,11... | collective-permute-start | bytes 798728 | tf_op jit(solution)/shard_map/ppermute | solution.py:441
  45.3 18.8 %copy-start = (bf16[1040,128]{1,0:T(8,128)(2,1)}, bf16[1040,128]{1,0:T(8,128)(2,1)S(1)}, u32[]{:S(2)}) copy-start(bf16[1040,128]{1,0:T(8,128)(2,1)S(1)} %collective-permute-done.refs_0_) | copy-start | bytes 798724
  45.3 12.2 %collective-permute-start.5 = (bf16[1040,128]{1,0:T(8,128)(2,1)}, bf16[1040,128]{1,0:T(8,128)(2,1)S(1)}, u32[]{:S(2)}, u32[]{:S(2)}) collective-permute-start(bf16[1040,128]{1,0:T(8,128)(2,1)} %get-tuple-element.25), channel_id=1, source_target_pairs={{0,2},{1,3},{2,0},{3,1},{4,6},{5,7},{6,4},{7,5},{8,10},{9,11},{10,... | collective-permute-start | bytes 798728 | tf_op jit(solution)/shard_map/ppermute | solution.py:441
  51.8 12.3 %copy-start.1 = (bf16[1040,128]{1,0:T(8,128)(2,1)}, bf16[1040,128]{1,0:T(8,128)(2,1)S(1)}, u32[]{:S(2)}) copy-start(bf16[1040,128]{1,0:T(8,128)(2,1)S(1)} %collective-permute-done.1.refs_1_) | copy-start | bytes 798724
  51.8 12.3 %collective-permute-start.6 = (bf16[1040,128]{1,0:T(8,128)(2,1)}, bf16[1040,128]{1,0:T(8,128)(2,1)S(1)}, u32[]{:S(2)}, u32[]{:S(2)}) collective-permute-start(bf16[1040,128]{1,0:T(8,128)(2,1)} %get-tuple-element.26), channel_id=1, source_target_pairs={{0,3},{1,2},{2,1},{3,0},{4,7},{5,6},{6,5},{7,4},{8,11},{9,10},{10,... | collective-permute-start | bytes 798728 | tf_op jit(solution)/shard_map/ppermute | solution.py:441
  53.3 10.8 %copy-start.2 = (bf16[1040,128]{1,0:T(8,128)(2,1)}, bf16[1040,128]{1,0:T(8,128)(2,1)S(1)}, u32[]{:S(2)}) copy-start(bf16[1040,128]{1,0:T(8,128)(2,1)S(1)} %collective-permute-done.2.refs_2_) | copy-start | bytes 798724
  53.3 10.8 %copy-start.3 = (bf16[1040,128]{1,0:T(8,128)(2,1)}, bf16[1040,128]{1,0:T(8,128)(2,1)S(1)}, u32[]{:S(2)}) copy-start(bf16[1040,128]{1,0:T(8,128)(2,1)S(1)} %collective-permute-done.3.refs_3_) | copy-start | bytes 798724
  53.4 10.8 %copy-start.4 = (bf16[1040,128]{1,0:T(8,128)(2,1)}, bf16[1040,128]{1,0:T(8,128)(2,1)S(1)}, u32[]{:S(2)}) copy-start(bf16[1040,128]{1,0:T(8,128)(2,1)S(1)} %collective-permute-done.4.refs_5_) | copy-start | bytes 798724
  57.5 6.6 %copy-start.5 = (bf16[1040,128]{1,0:T(8,128)(2,1)}, bf16[1040,128]{1,0:T(8,128)(2,1)S(1)}, u32[]{:S(2)}) copy-start(bf16[1040,128]{1,0:T(8,128)(2,1)S(1)} %collective-permute-done.5.refs_6_) | copy-start | bytes 798724
  64.1 0.7 copy-start.6
  74.3 14.4 %copy-start.7 = (bf16[2,272,128]{2,1,0:T(8,128)(2,1)S(1)}, bf16[2,272,128]{2,1,0:T(8,128)(2,1)}, u32[]{:S(2)}) copy-start(bf16[2,272,128]{2,1,0:T(8,128)(2,1)} %get-tuple-element.27.refs_3_) | copy-start | bytes 417796
  74.3 12.3 %collective-permute-start.7 = (bf16[2,272,128]{2,1,0:T(8,128)(2,1)}, bf16[2,272,128]{2,1,0:T(8,128)(2,1)S(1)}, u32[]{:S(2)}, u32[]{:S(2)}) collective-permute-start(bf16[2,272,128]{2,1,0:T(8,128)(2,1)} %get-tuple-element.27.refs_3_), channel_id=1, source_target_pairs={{0,1},{1,2},{2,3},{3,4},{4,5},{5,6},{6,7},{7,0},{8,9},{9,10},{10,1... | collective-permute-start | bytes 417800 | tf_op jit(solution)/shard_map/ppermute | solution.py:447
  74.7 14.0 %collective-permute-start.8 = (bf16[2,272,128]{2,1,0:T(8,128)(2,1)}, bf16[2,272,128]{2,1,0:T(8,128)(2,1)S(1)}, u32[]{:S(2)}, u32[]{:S(2)}) collective-permute-start(bf16[2,272,128]{2,1,0:T(8,128)(2,1)} %get-tuple-element.28.refs_1_), channel_id=1, source_target_pairs={{1,0},{2,1},{3,2},{4,3},{5,4},{6,5},{7,6},{0,7},{9,8},{10,9},{11,1... | collective-permute-start | bytes 417800 | tf_op jit(solution)/shard_map/ppermute | solution.py:448
  86.6 12.1 %copy-start.8 = (bf16[2,272,128]{2,1,0:T(8,128)(2,1)}, bf16[2,272,128]{2,1,0:T(8,128)(2,1)S(1)}, u32[]{:S(2)}) copy-start(bf16[2,272,128]{2,1,0:T(8,128)(2,1)S(1)} %collective-permute-done.7.refs_0_) | copy-start | bytes 417796
  88.7 10.0 %copy-start.9 = (bf16[2,272,128]{2,1,0:T(8,128)(2,1)}, bf16[2,272,128]{2,1,0:T(8,128)(2,1)S(1)}, u32[]{:S(2)}) copy-start(bf16[2,272,128]{2,1,0:T(8,128)(2,1)S(1)} %collective-permute-done.8.refs_4_) | copy-start | bytes 417796
  88.7 19.0 %collective-permute-start.9 = (bf16[6,272,128]{2,1,0:T(8,128)(2,1)S(1)}, bf16[6,272,128]{2,1,0:T(8,128)(2,1)S(1)}, u32[]{:S(2)}, u32[]{:S(2)}) collective-permute-start(bf16[6,272,128]{2,1,0:T(8,128)(2,1)S(1)} %get-tuple-element.36), channel_id=1, source_target_pairs={{0,8},{8,16},{16,24},{1,9},{9,17},{17,25},{2,10},{10,18},{18,26},{... | collective-permute-start | bytes 1253384 | tf_op jit(solution)/shard_map/ppermute | solution.py:459
  92.9 14.8 %collective-permute-start.10 = (bf16[6,272,128]{2,1,0:T(8,128)(2,1)S(1)}, bf16[6,272,128]{2,1,0:T(8,128)(2,1)S(1)}, u32[]{:S(2)}, u32[]{:S(2)}) collective-permute-start(bf16[6,272,128]{2,1,0:T(8,128)(2,1)S(1)} %get-tuple-element.35), channel_id=1, source_target_pairs={{8,0},{16,8},{24,16},{9,1},{17,9},{25,17},{10,2},{18,10},{26,18},{... | collective-permute-start | bytes 1253384 | tf_op jit(solution)/shard_map/ppermute | solution.py:460
  107.7 0.8 copy-start.10
  108.5 0.8 copy-start.11

commit v2 on v1

v2 whole, which is shorter than its diff:
```python
import functools

import jax
import jax.numpy as jnp
from jax import lax
from jax.experimental import pallas as pl
from jax.experimental.pallas import tpu as pltpu
from jax.sharding import PartitionSpec as P

CAP = 4
PLAT = 2
PLON = 4
POINTS = PLAT * PLON
ITERS = 6
HALF = 128
MEMBERS = 2 * HALF
TILE = 16
BLOCK = CAP * MEMBERS + TILE
PACKED = MEMBERS + TILE
F32 = jnp.float32
BF16 = jnp.bfloat16
VMEM_LIMIT = 56 * 1024 * 1024

SMEM_SPEC = pl.BlockSpec(memory_space=pltpu.SMEM)
VMEM_SPEC = pl.BlockSpec(memory_space=pltpu.VMEM)
ANY_SPEC = pl.BlockSpec(memory_space=pl.ANY)


def params():
    return pltpu.CompilerParams(vmem_limit_bytes=VMEM_LIMIT)


def dot_nn(a, b):
    return lax.dot_general(a, b, (((1,), (0,)), ((), ())), preferred_element_type=F32)


def dot_nt(a, b):
    return lax.dot_general(a, b, (((1,), (1,)), ((), ())), preferred_element_type=F32)


def iota(shape, dim):
    return lax.broadcasted_iota(jnp.int32, shape, dim)


def gram_kernel(first, count, lon_size, me_ref, owner_ref, len_ref, points_ref, num_ref,
                weight_ref, innov_ref, taper_ref, pert_ref, *rest):
    outs, (source, filled, rows, w32, i32, t32, built, in_sem, out_sem) = rest[:count], rest[count:]
    held, nobs, _ = pert_ref.shape
    me = me_ref[0]

    @pl.loop(0, lon_size)
    def _(k):
        filled[k] = 0

    @pl.loop(0, count * CAP)
    def _(s):
        source[first * CAP + s] = 0

    @pl.loop(0, held)
    def _(b):
        k = owner_ref[0, b] ^ me
        n = filled[k]
        source[k * CAP + n] = b
        filled[k] = n + 1

    def fetch(step, j):
        b = source[(first + step) * CAP + j]
        return pltpu.make_async_copy(pert_ref.at[b], rows.at[step, j], in_sem.at[step, j])

    @pl.loop(0, count)
    def _(step):
        for j in range(CAP):
            fetch(step, j).start()

    w32[...] = weight_ref[...].astype(F32)
    i32[...] = innov_ref[...].astype(F32)
    t32[...] = jnp.concatenate(
        [taper_ref[...].astype(F32), jnp.zeros((8 - taper_ref.shape[0], held), F32)], axis=0)
    lane_obs = iota((1, nobs), 1)
    lane = iota((1, HALF), 1)
    lane_held = iota((1, held), 1)
    row_id = iota((HALF, HALF), 0)
    col_id = iota((HALF, HALF), 1)

    @pl.loop(0, count)
    def _(step):
        k = first + step
        for j in range(CAP):
            fetch(step, j).wait()
        lo, hi, dg, cf = [], [], [], []
        for j in range(CAP):
            b = source[k * CAP + j]
            present = j < filled[k]
            live = jnp.where(present, len_ref[0, b], 0)
            keep = jnp.where(lane_obs < live, w32[pl.ds(b, 1), :], 0.0)
            pulled = (keep * i32[pl.ds(b, 1), :]).astype(BF16)
            x = rows[step, j]
            scaled = x.T * keep.astype(BF16)
            lhs = jnp.concatenate([scaled, jnp.broadcast_to(pulled, (TILE, nobs))], axis=0)
            gram = dot_nn(lhs, x)
            a11 = gram[0:HALF, 0:HALF]
            a22 = gram[HALF:MEMBERS, HALF:MEMBERS]
            built[step, pl.ds(j * MEMBERS, HALF), :] = jnp.where(row_id <= col_id, a11, a22).astype(BF16)
            built[step, pl.ds(j * MEMBERS + HALF, HALF), :] = gram[0:HALF, HALF:MEMBERS].astype(BF16)
            lo.append(gram[MEMBERS:MEMBERS + 1, 0:HALF])
            hi.append(gram[MEMBERS:MEMBERS + 1, HALF:MEMBERS])
            dg.append(jnp.sum(jnp.where(row_id == col_id, a22, 0.0), axis=0, keepdims=True))
            limit = jnp.where(present, num_ref[b], 0)
            coef = jnp.zeros((1, HALF), F32)
            for q in range(3):
                taper = jnp.sum(jnp.where(lane_held == b, t32[q:q + 1, :], 0.0), axis=1, keepdims=True)
                hit = (lane == points_ref[q, b]) & (q < limit)
                coef = coef + jnp.where(hit, taper, 0.0)
            cf.append(coef)
        built[step, pl.ds(CAP * MEMBERS, TILE), :] = jnp.concatenate(lo + hi + dg + cf, axis=0).astype(BF16)
        for i in range(count):
            @pl.when(step == i)
            def _():
                pltpu.make_async_copy(built.at[i], outs[i], out_sem.at[i]).start()

    for i in range(count):
        pltpu.make_async_copy(built.at[i], outs[i], out_sem.at[i]).wait()


def batch_blocks(first, count, lon_size, me, owner, length, points, num, weight, innov, taper, pert):
    held, nobs, members = pert.shape
    return pl.pallas_call(
        functools.partial(gram_kernel, first, count, lon_size),
        out_shape=[jax.ShapeDtypeStruct((BLOCK, HALF), BF16)] * count,
        in_specs=[SMEM_SPEC] * 5 + [VMEM_SPEC] * 3 + [ANY_SPEC],
        out_specs=[ANY_SPEC] * count,
        scratch_shapes=[
            pltpu.SMEM((lon_size * CAP,), jnp.int32),
            pltpu.SMEM((lon_size,), jnp.int32),
            pltpu.VMEM((count, CAP, nobs, members), BF16),
            pltpu.VMEM((held, nobs), F32),
            pltpu.VMEM((held, nobs), F32),
            pltpu.VMEM((8, held), F32),
            pltpu.VMEM((count, BLOCK, HALF), BF16),
            pltpu.SemaphoreType.DMA((count, CAP)),
            pltpu.SemaphoreType.DMA((count,)),
        ],
        compiler_params=params(),
        cost_estimate=pl.CostEstimate(
            flops=count * CAP * 2 * nobs * members * members,
            bytes_accessed=count * CAP * nobs * members * 2, transcendentals=0),
    )(me, owner, length, points, num, weight, innov, taper, pert)


EDGE = [r * PLON + c for r in range(PLAT) for c in (0, PLON - 1)]
INNER = [r * PLON + c for r in range(PLAT) for c in range(1, PLON - 1)]


def unpack(triangle, corner, diagonal):
    row_id = iota((HALF, HALF), 0)
    col_id = iota((HALF, HALF), 1)
    flipped = triangle.T
    a11 = jnp.where(row_id <= col_id, triangle, flipped)
    a22 = jnp.where(row_id > col_id, triangle, jnp.where(row_id == col_id, diagonal, flipped))
    return jnp.concatenate(
        [jnp.concatenate([a11, corner], axis=1), jnp.concatenate([corner.T, a22], axis=1)], axis=0)


def pack(matrix):
    row_id = iota((HALF, HALF), 0)
    col_id = iota((HALF, HALF), 1)
    a22 = matrix[HALF:MEMBERS, HALF:MEMBERS]
    triangle = jnp.where(row_id <= col_id, matrix[0:HALF, 0:HALF], a22)
    diagonal = jnp.sum(jnp.where(row_id == col_id, a22, 0.0), axis=0, keepdims=True)
    return triangle, matrix[0:HALF, HALF:MEMBERS], diagonal


def sum_by_point(blocks, acc, side):
    slots = len(blocks) * CAP
    extras = [blk[pl.ds(CAP * MEMBERS, TILE), :].astype(F32) for blk in blocks]
    low, high, diag, coef = [
        jnp.concatenate([e[CAP * q:CAP * (q + 1)] for e in extras], axis=0).astype(BF16) for q in range(4)]
    pick = (iota((POINTS, HALF), 0) == iota((POINTS, HALF), 1)).astype(BF16)
    by_point = dot_nt(pick, coef).astype(BF16)
    for q, part in enumerate((diag, low, high)):
        side[q] = dot_nn(by_point, part)
    spread = (iota((POINTS * TILE, HALF), 0) // TILE == iota((POINTS * TILE, HALF), 1)).astype(BF16)
    tall = dot_nt(spread, coef).astype(BF16)
    wide = (iota((slots, slots * TILE), 1) // TILE == iota((slots, slots * TILE), 0)).astype(BF16)
    mixing = dot_nn(tall, wide)
    shape = (POINTS * TILE, slots * TILE)
    mixing = jnp.where(iota(shape, 0) % TILE == iota(shape, 1) % TILE, mixing, 0.0).astype(BF16)
    for g in range(0, MEMBERS // TILE, 2):
        pair = []
        for h in (g, g + 1):
            pair.append(jnp.concatenate(
                [blk[pl.ds(j * MEMBERS + h * TILE, TILE), :] for blk in blocks for j in range(CAP)], axis=0))
        summed = dot_nn(mixing, jnp.concatenate(pair, axis=1))
        for p in range(POINTS):
            for h in (0, 1):
                acc[p, pl.ds((g + h) * TILE, TILE), :] = summed[p * TILE:(p + 1) * TILE, h * HALF:(h + 1) * HALF]


def relay_kernel(count, *refs):
    blocks = refs[:count]
    edge_ref, inner_ref, acc, side = refs[count:]
    sum_by_point(blocks, acc, side)
    for ref, listed in ((edge_ref, EDGE), (inner_ref, INNER)):
        for i, p in enumerate(listed):
            ref[i, pl.ds(0, MEMBERS), :] = acc[p].astype(BF16)
            rows = [side[q, pl.ds(p, 1), :] for q in range(3)] + [jnp.zeros((TILE - 3, HALF), F32)]
            ref[i, pl.ds(MEMBERS, TILE), :] = jnp.concatenate(rows, axis=0).astype(BF16)


def relay_sums(blocks):
    return pl.pallas_call(
        functools.partial(relay_kernel, len(blocks)),
        out_shape=[
            jax.ShapeDtypeStruct((len(EDGE), PACKED, HALF), BF16),
            jax.ShapeDtypeStruct((len(INNER), PACKED, HALF), BF16),
        ],
        in_specs=[VMEM_SPEC] * len(blocks),
        out_specs=[VMEM_SPEC] * 2,
        scratch_shapes=[
            pltpu.VMEM((POINTS, MEMBERS, HALF), F32),
            pltpu.VMEM((3, POINTS, HALF), F32),
        ],
        compiler_params=params(),
        cost_estimate=pl.CostEstimate(
            flops=len(blocks) * CAP * POINTS * TILE * MEMBERS * HALF,
            bytes_accessed=len(blocks) * BLOCK * HALF * 4, transcendentals=0),
    )(*blocks)


def transform_points(listed, total_of, side_of, far_ref, scratch, full_ref, packed_out):
    w32, z32, wb, gb, zb = scratch
    eye = (iota((MEMBERS, MEMBERS), 0) == iota((MEMBERS, MEMBERS), 1)).astype(F32)
    scales, shifts = [], []
    points = range(len(listed))
    for i in points:
        p = listed[i]
        packed = total_of(p) + far_ref[i, pl.ds(0, MEMBERS), :].astype(F32)
        extra = far_ref[i, pl.ds(MEMBERS, TILE), :].astype(F32)
        diagonal, low, high = [side_of(p)[q] + extra[q:q + 1] for q in range(3)]
        shifts.append(jnp.concatenate([low, high], axis=1))
        system = unpack(packed[0:HALF], packed[HALF:MEMBERS], diagonal) + (MEMBERS - 1) * eye
        square = jnp.sum(jnp.sum(system * system, axis=0, keepdims=True), axis=1, keepdims=True)
        inv = lax.rsqrt(square)
        inv = inv * (1.5 - 0.5 * square * inv * inv)
        scales.append(inv)
        iterate = system * inv
        root = 1.5 * eye - 0.5 * iterate
        w32[i] = iterate
        wb[i] = iterate.astype(BF16)
        z32[i] = root
        zb[i] = root.astype(BF16)

    def advance():
        for i in points:
            gb[i] = (0.25 * dot_nn(wb[i], wb[i]) - 1.5 * w32[i]).astype(BF16)
        for i in points:
            value = 2.25 * w32[i] + dot_nn(wb[i], gb[i])
            w32[i] = value
            wb[i] = value.astype(BF16)

    advance()

    @pl.loop(0, ITERS - 2)
    def _(sweep):
        for i in points:
            value = 1.5 * z32[i] - 0.5 * dot_nn(wb[i], zb[i])
            z32[i] = value
            zb[i] = value.astype(BF16)
        advance()

    for i in points:
        z32[i] = 1.5 * z32[i] - 0.5 * dot_nn(wb[i], zb[i])
    for i in points:
        root = z32[i]
        inner = jnp.sum(root * shifts[i], axis=1, keepdims=True)
        mean_weight = jnp.sum(root * inner, axis=0, keepdims=True) * scales[i]
        result = root * jnp.sqrt((MEMBERS - 1) * scales[i])
        full_ref[i] = (result + mean_weight).astype(BF16)
        triangle, corner, diagonal = pack(result)
        extra = jnp.concatenate(
            [diagonal, mean_weight[:, 0:HALF], mean_weight[:, HALF:MEMBERS], jnp.zeros((TILE - 3, HALF), F32)],
            axis=0)
        ref, where = packed_out(listed[i])
        ref[where, pl.ds(0, HALF), :] = triangle.astype(BF16)
        ref[where, pl.ds(HALF, HALF), :] = corner.astype(BF16)
        ref[where, pl.ds(MEMBERS, TILE), :] = extra.astype(BF16)


def edge_kernel(count, *refs):
    blocks = refs[:count]
    far_ref, left_ref, right_ref, full_ref, total_ref, side_ref, w32, z32, wb, gb, zb, acc = refs[count:]
    sum_by_point(blocks, acc, side_ref)
    for i, p in enumerate(INNER):
        total_ref[i] = acc[p]
    transform_points(
        EDGE,
        lambda p: acc[p],
        lambda p: [side_ref[q, pl.ds(p, 1), :] for q in range(3)],
        far_ref, (w32, z32, wb, gb, zb), full_ref,
        lambda p: (left_ref if p % PLON == 0 else right_ref, p // PLON))


def inner_kernel(total_in, side_in, far_ref, left_ref, right_ref, full_ref, *refs):
    rows, scratch = refs[:PLAT], refs[PLAT:]
    transform_points(
        INNER,
        lambda p: total_in[INNER.index(p)],
        lambda p: [side_in[q, pl.ds(p, 1), :] for q in range(3)],
        far_ref, scratch, full_ref,
        lambda p: (rows[p // PLON], p % PLON + 1))
    for r in range(PLAT):
        rows[r][1] = left_ref[r]
        rows[r][PLON] = right_ref[r]


def newton_scratch(count):
    shape = (count, MEMBERS, MEMBERS)
    return [pltpu.VMEM(shape, F32)] * 2 + [pltpu.VMEM(shape, BF16)] * 3


def edge_transforms(blocks, far):
    columns = jax.ShapeDtypeStruct((PLAT, PACKED, HALF), BF16)
    return pl.pallas_call(
        functools.partial(edge_kernel, len(blocks)),
        out_shape=[
            columns, columns,
            jax.ShapeDtypeStruct((len(EDGE), MEMBERS, MEMBERS), BF16),
            jax.ShapeDtypeStruct((len(INNER), MEMBERS, HALF), F32),
            jax.ShapeDtypeStruct((3, POINTS, HALF), F32),
        ],
        in_specs=[VMEM_SPEC] * (len(blocks) + 1),
        out_specs=[VMEM_SPEC] * 5,
        scratch_shapes=newton_scratch(len(EDGE)) + [pltpu.VMEM((POINTS, MEMBERS, HALF), F32)],
        compiler_params=params(),
        cost_estimate=pl.CostEstimate(
            flops=len(EDGE) * 15 * 2 * MEMBERS ** 3, bytes_accessed=8 * MEMBERS * HALF * 6, transcendentals=0),
    )(*blocks, far)


def inner_transforms(total, side, far, left, right):
    count = total.shape[0]
    row = jax.ShapeDtypeStruct((PLON + 2, PACKED, HALF), BF16)
    return pl.pallas_call(
        inner_kernel,
        out_shape=[jax.ShapeDtypeStruct((count, MEMBERS, MEMBERS), BF16)] + [row] * PLAT,
        in_specs=[VMEM_SPEC] * 5,
        out_specs=[VMEM_SPEC] * (1 + PLAT),
        scratch_shapes=newton_scratch(count),
        compiler_params=params(),
        cost_estimate=pl.CostEstimate(
            flops=count * 15 * 2 * MEMBERS ** 3, bytes_accessed=count * MEMBERS * HALF * 6, transcendentals=0),
    )(total, side, far, left, right)


WIDE = PLON + 2
WINDOW = (PLAT + 2) * WIDE
MID = list(range(WIDE, WINDOW - WIDE))
RIM = list(range(WIDE)) + list(range(WINDOW - WIDE, WINDOW))


def cell_kernel(point_cols, pos_ref, stencil_ref, frac_ref, field_ref, mid_ref, rim_ref, mean_ref):
    width = stencil_ref.shape[2]
    lat_pos, lon_pos = pos_ref[0], pos_ref[1]
    i = pl.program_id(0)
    ids = iota((HALF, width), 0)
    field = field_ref[0].astype(F32)
    mean = jnp.mean(field, axis=1, keepdims=True)
    mean_ref[...] = jnp.broadcast_to(mean, mean_ref.shape)
    dev = (field - mean).astype(BF16).astype(F32)
    row_off = stencil_ref[0, pl.ds(i, 1), :] - (lat_pos * PLAT - 1)
    col_off = stencil_ref[1, pl.ds(i, 1), :] - (lon_pos * PLON - 1)
    col_off = jnp.where(col_off < 0, col_off + point_cols, col_off)
    col_off = jnp.where(col_off >= point_cols, col_off - point_cols, col_off)
    y = frac_ref[0, pl.ds(i, 1), :]
    x = frac_ref[1, pl.ds(i, 1), :]
    corner = row_off * WIDE + col_off
    weights = jnp.where(corner == ids, (1.0 - y) * (1.0 - x), 0.0)
    weights = weights + jnp.where(corner + WIDE == ids, y * (1.0 - x), 0.0)
    weights = weights + jnp.where(corner + 1 == ids, (1.0 - y) * x, 0.0)
    weights = weights + jnp.where(corner + WIDE + 1 == ids, y * x, 0.0)
    turned = weights.T
    for ref, listed in ((mid_ref, MID), (rim_ref, RIM)):
        for n, point in enumerate(listed):
            ref[:, n * MEMBERS:(n + 1) * MEMBERS] = (dev * turned[:, point:point + 1]).astype(BF16)


def cell_parts(point_cols, pos, stencil, frac, background):
    rows, width, members = background.shape
    cells = rows * width
    return pl.pallas_call(
        functools.partial(cell_kernel, point_cols),
        grid=(rows,),
        out_shape=[
            jax.ShapeDtypeStruct((cells, len(MID) * members), BF16),
            jax.ShapeDtypeStruct((cells, len(RIM) * members), BF16),
            jax.ShapeDtypeStruct((cells, HALF), F32),
        ],
        in_specs=[
            SMEM_SPEC,
            pl.BlockSpec(stencil.shape, lambda i: (0, 0, 0)),
            pl.BlockSpec(frac.shape, lambda i: (0, 0, 0)),
            pl.BlockSpec((1, width, members), lambda i: (i, 0, 0)),
        ],
        out_specs=[
            pl.BlockSpec((width, len(MID) * members), lambda i: (i, 0)),
            pl.BlockSpec((width, len(RIM) * members), lambda i: (i, 0)),
            pl.BlockSpec((width, HALF), lambda i: (i, 0)),
        ],
        compiler_params=params(),
        cost_estimate=pl.CostEstimate(
            flops=cells * members * WINDOW, bytes_accessed=cells * members * (2 * WINDOW + 4), transcendentals=0),
    )(pos, stencil, frac, background)


def place_packed(matrices, slot, ref, i):
    extra = ref[i, pl.ds(MEMBERS, TILE), :].astype(F32)
    full = unpack(ref[i, pl.ds(0, HALF), :].astype(F32), ref[i, pl.ds(HALF, HALF), :].astype(F32), extra[0:1])
    full = full + jnp.concatenate([extra[1:2], extra[2:3]], axis=1)
    matrices[:, slot * MEMBERS:(slot + 1) * MEMBERS] = full.astype(BF16)


def mid_kernel(before, after, edge, inner, lhs_ref, mean_ref, out_ref, matrices):
    @pl.when(pl.program_id(0) == 0)
    def _():
        for r in range(PLAT):
            place_packed(matrices, r * WIDE, before, r)
            place_packed(matrices, r * WIDE + PLON + 1, after, r)
            for c in range(PLON):
                p = r * PLON + c
                value = edge[EDGE.index(p)] if p in EDGE else inner[INNER.index(p)]
                slot = r * WIDE + c + 1
                matrices[:, slot * MEMBERS:(slot + 1) * MEMBERS] = value

    out_ref[...] = dot_nt(lhs_ref[...], matrices[...]) + mean_ref[:, 0:1]


def rim_kernel(above, below, lhs_ref, base_ref, out_ref, matrices):
    @pl.when(pl.program_id(0) == 0)
    def _():
        for c in range(WIDE):
            place_packed(matrices, c, above, c)
            place_packed(matrices, WIDE + c, below, c)

    out_ref[...] = (dot_nt(lhs_ref[...], matrices[...]) + base_ref[...]).astype(BF16)


def mix(kernel, transforms, lhs, base, dtype):
    cells, depth = lhs.shape
    tile = min(cells, 2 * MEMBERS)
    return pl.pallas_call(
        kernel,
        grid=(cells // tile,),
        out_shape=jax.ShapeDtypeStruct((cells, MEMBERS), dtype),
        in_specs=[pl.BlockSpec(t.shape, lambda i: (0, 0, 0)) for t in transforms] + [
            pl.BlockSpec((tile, depth), lambda i: (i, 0)),
            pl.BlockSpec((tile, base.shape[1]), lambda i: (i, 0)),
        ],
        out_specs=pl.BlockSpec((tile, MEMBERS), lambda i: (i, 0)),
        scratch_shapes=[pltpu.VMEM((MEMBERS, depth), BF16)],
        compiler_params=params(),
        cost_estimate=pl.CostEstimate(
            flops=2 * cells * depth * MEMBERS, bytes_accessed=cells * depth * 2, transcendentals=0),
    )(*transforms, lhs, base)


def on_device(obs_pert, obs_weight, innovation, batch_len, batch_owner, batch_points, batch_count,
              batch_taper, background, stencil, frac):
    lon_size, lat_size = lax.axis_size("lon"), lax.axis_size("lat")
    lat_pos, lon_pos = lax.axis_index("lat"), lax.axis_index("lon")
    me = lon_pos.astype(jnp.int32).reshape(1)
    pos = jnp.stack([lat_pos, lon_pos]).astype(jnp.int32)
    fixed = (me, batch_owner.T, batch_len, batch_points.T, batch_count, obs_weight, innovation, batch_taper.T,
             obs_pert)
    half = lon_size // 2

    def swap(value, offset):
        return lax.ppermute(value, "lon", [(i, i ^ offset) for i in range(lon_size)])

    far = batch_blocks(half, half, lon_size, *fixed)
    relayed = [far[0]] + [swap(far[i], i) for i in range(1, half)]
    near = batch_blocks(0, half, lon_size, *fixed)
    got = [near[0]] + [swap(near[i], i) for i in range(1, half)]
    relayed, _ = lax.optimization_barrier((relayed, near))
    far_edge, far_inner = relay_sums(relayed)
    far_edge, far_inner, background = lax.optimization_barrier((far_edge, far_inner, background))
    mid_lhs, rim_lhs, mean = cell_parts(PLON * lon_size, pos, stencil, frac, background)
    far_edge = swap(far_edge, half)
    far_inner, got, mid_lhs, rim_lhs, mean = lax.optimization_barrier((far_inner, got, mid_lhs, rim_lhs, mean))
    far_inner = swap(far_inner, half)

    left, right, edge, total, side = edge_transforms(got, far_edge)
    up = [(i, (i + 1) % lon_size) for i in range(lon_size)]
    down = [(j, i) for i, j in up]
    before = lax.ppermute(right, "lon", up)
    after = lax.ppermute(left, "lon", down)
    inner, *rows = inner_transforms(total, side, far_inner, left, right)
    rows = [rows[r].at[0].set(before[r]).at[PLON + 1].set(after[r]) for r in range(PLAT)]
    north = [(i, i + 1) for i in range(lat_size - 1)]
    south = [(j, i) for i, j in north]
    above = lax.ppermute(rows[PLAT - 1], "lat", north)
    below = lax.ppermute(rows[0], "lat", south)
    partial = mix(mid_kernel, [before, after, edge, inner], mid_lhs, mean, F32)
    return mix(rim_kernel, [above, below], rim_lhs, partial, BF16).reshape(background.shape)


def solution(mesh):
    return jax.shard_map(
        on_device,
        mesh=mesh,
        in_specs=(
            P(("lat", "lon"), None, None),
            P(("lat", "lon"), None),
            P(("lat", "lon"), None),
            P(("lat", "lon"), None),
            P(("lat", "lon"), None),
            P(("lat", "lon"), None),
            P(("lat", "lon")),
            P(("lat", "lon"), None),
            P("lat", "lon", None),
            P(None, "lat", "lon"),
            P(None, "lat", "lon"),
        ),
        out_specs=P("lat", "lon", None),
        check_vma=False,
    )
```

time: 117 us -> 87.8 us (0.75)
  waiting for transfers between devices: 30.6 us -> 10.9 us
  Pallas kernels: 54.8 us -> 46.9 us
  local copies, waits for them, and re-layouts: 8.32 us -> 4.77 us
  starting transfers between devices: 21.9 us -> 23.9 us
    ppermute x9 -> x10, waiting for transfers between devices: 30.6 us -> 10.9 us  [the longest x8 8.78 us: swap(): lax.ppermute(value, 'lon', [(i, i ^ offset) for i in range(lon_size)])]
    pallas_call x2, Pallas kernels: 17.8 us -> 11.2 us  [batch_blocks(): pl.pallas_call(functools.partial(gram_kernel, first, count, lon_size), ou...]
    unnamed x31 -> x24, local copies, waits for them, and re-layouts: 8.3 us -> 3.35 us
    ppermute x9 -> x10, starting transfers between devices: 17.7 us -> 19.7 us  [the longest x1 9.25 us: on_device(): above = lax.ppermute(rows[PLAT - 1], 'lat', north)]
    scatter x0 -> x2, local copies, waits for them, and re-layouts: none -> 1.42 us  [on_device(): rows[r].at[0].set(before[r]).at[PLON + 1].set(after[r])]
    pallas_call x5 -> x6, Pallas kernels: 37 us -> 35.7 us  [the longest x2 10.9 us: mix(): pl.pallas_call(kernel, grid=(cells // tile,), out_shape=jax.ShapeDtypeStr...]
  transfers between devices with their start and end apart: 11 -> 12, of which waited for: 4 -> 4; matrix products, arithmetic and copies ran while one was open for 2% -> 1% of each run, Pallas kernels for 25% -> 41%
where the time goes in v2:
time: 87.8 us; the launch traced here: 87.1 us
  Pallas kernels  46.9 us (53%)
  starting transfers between devices  23.9 us (27%)
  waiting for transfers between devices  10.9 us (12%)
  local copies, waits for them, and re-layouts  4.77 us (5%)
    pallas_call x2, Pallas kernels, batch_blocks(): pl.pallas_call(functools.partial(gram_kernel, first, count, lon_size), ou...  11.2 us
    pallas_call x2, Pallas kernels, mix(): pl.pallas_call(kernel, grid=(cells // tile,), out_shape=jax.ShapeDtypeStr...  10.9 us
    ppermute x1, starting transfers between devices, on_device(): above = lax.ppermute(rows[PLAT - 1], 'lat', north)  9.25 us
    ppermute x8, waiting for transfers between devices, swap(): lax.ppermute(value, 'lon', [(i, i ^ offset) for i in range(lon_size)])  8.78 us
    ppermute x8, starting transfers between devices, swap(): lax.ppermute(value, 'lon', [(i, i ^ offset) for i in range(lon_size)])  8.56 us
    pallas_call x1, Pallas kernels, cell_parts(): pl.pallas_call(functools.partial(cell_kernel, point_cols), grid=(rows,),...  8.38 us
    pallas_call x1, Pallas kernels, edge_transforms(): pl.pallas_call(functools.partial(edge_kernel, len(blocks)), out_shape=[co...  7.13 us
    pallas_call x1, Pallas kernels, inner_transforms(): pl.pallas_call(inner_kernel, out_shape=[jax.ShapeDtypeStruct((count, MEMB...  6.66 us
  transfers between devices with their start and end apart: 12, of which 4 were waited for; matrix products, arithmetic and copies ran while one was open for 1% of the time, Pallas kernels for 41%

profile of v2, /device:TPU:1, one launch (start us, length us, event | category | flops | bytes accessed | tf_op | source)
XLA Modules:
  0.0 87.1 jit_solution(15860079125323811727)
XLA Ops:
  0.0 5.6 %shard_map.109 = (bf16[1040,128]{1,0:T(8,128)(2,1)}, bf16[1040,128]{1,0:T(8,128)(2,1)}, bf16[1040,128]{1,0:T(8,128)(2,1)}, bf16[1040,128]{1,0:T(8,128)(2,1)}) custom-call(s32[1]{0:T(128)} %bitcast.me_ref, s32[1,32]{1,0:T(1,128)} %bitcast.10, s32[1,32]{1,0:T(1,128)} %len_ref.3, s32[3,32]{1,0:T(4,128)} %bitcast.6, s32[32]{0:T(128)} %num_ref.3, ...), custom_call_target="tpu_custom_call" | custom-call | flops 1073741824 | bytes 4194304 | tf_op jit(solution)/shard_map/pallas_call | solution.py:127
  5.6 2.1 %collective-permute-start = (bf16[1040,128]{1,0:T(8,128)(2,1)}, bf16[1040,128]{1,0:T(8,128)(2,1)S(1)}, u32[]{:S(2)}, u32[]{:S(2)}) collective-permute-start(bf16[1040,128]{1,0:T(8,128)(2,1)} %get-tuple-element.90), channel_id=1, source_target_pairs={{0,1},{1,0},{2,3},{3,2},{4,5},{5,4},{6,7},{7,6},{8,9},{9,8},{10,11... | collective-permute-start | bytes 798728 | tf_op jit(solution)/shard_map/ppermute | solution.py:477
  7.7 1.3 %collective-permute-start.1 = (bf16[1040,128]{1,0:T(8,128)(2,1)}, bf16[1040,128]{1,0:T(8,128)(2,1)S(1)}, u32[]{:S(2)}, u32[]{:S(2)}) collective-permute-start(bf16[1040,128]{1,0:T(8,128)(2,1)} %get-tuple-element.91), channel_id=1, source_target_pairs={{0,2},{1,3},{2,0},{3,1},{4,6},{5,7},{6,4},{7,5},{8,10},{9,11},{10,... | collective-permute-start | bytes 798728 | tf_op jit(solution)/shard_map/ppermute | solution.py:477
  9.0 5.6 %shard_map.110 = (bf16[1040,128]{1,0:T(8,128)(2,1)}, bf16[1040,128]{1,0:T(8,128)(2,1)}, bf16[1040,128]{1,0:T(8,128)(2,1)}, bf16[1040,128]{1,0:T(8,128)(2,1)}) custom-call(s32[1]{0:T(128)} %bitcast.me_ref, s32[1,32]{1,0:T(1,128)} %bitcast.11, s32[1,32]{1,0:T(1,128)} %len_ref.3, s32[3,32]{1,0:T(4,128)} %bitcast.7, s32[32]{0:T(128)} %num_ref.3, ...), custom_call_target="tpu_custom_call" | custom-call | flops 1073741824 | bytes 4194304 | tf_op jit(solution)/shard_map/pallas_call | solution.py:127
  14.6 1.4 %collective-permute-start.3 = (bf16[1040,128]{1,0:T(8,128)(2,1)}, bf16[1040,128]{1,0:T(8,128)(2,1)S(1)}, u32[]{:S(2)}, u32[]{:S(2)}) collective-permute-start(bf16[1040,128]{1,0:T(8,128)(2,1)} %get-tuple-element.94), channel_id=1, source_target_pairs={{0,1},{1,0},{2,3},{3,2},{4,5},{5,4},{6,7},{7,6},{8,9},{9,8},{10,11... | collective-permute-start | bytes 798728 | tf_op jit(solution)/shard_map/ppermute | solution.py:477
  16.0 1.3 %collective-permute-start.4 = (bf16[1040,128]{1,0:T(8,128)(2,1)}, bf16[1040,128]{1,0:T(8,128)(2,1)S(1)}, u32[]{:S(2)}, u32[]{:S(2)}) collective-permute-start(bf16[1040,128]{1,0:T(8,128)(2,1)} %get-tuple-element.95), channel_id=1, source_target_pairs={{0,2},{1,3},{2,0},{3,1},{4,6},{5,7},{6,4},{7,5},{8,10},{9,11},{10,... | collective-permute-start | bytes 798728 | tf_op jit(solution)/shard_map/ppermute | solution.py:477
  17.3 0.0 collective-permute-start.5
  17.3 0.0 collective-permute-done.1.refs_2_
  17.3 3.4 %collective-permute-done.2.refs_3_ = bf16[1040,128]{1,0:T(8,128)(2,1)S(1)} collective-permute-done((bf16[1040,128]{1,0:T(8,128)(2,1)}, bf16[1040,128]{1,0:T(8,128)(2,1)S(1)}, u32[]{:S(2)}, u32[]{:S(2)}) %collective-permute-start.2) | collective-permute-done | bytes 266272 | tf_op jit(solution)/shard_map/ppermute | solution.py:477
  20.7 0.7 copy-done.6
  21.4 2.6 %shard_map.111 = (bf16[4,272,128]{2,1,0:T(8,128)(2,1)}, bf16[4,272,128]{2,1,0:T(8,128)(2,1)}) custom-call(bf16[1040,128]{1,0:T(8,128)(2,1)} %get-tuple-element.97.refs_0_, bf16[1040,128]{1,0:T(8,128)(2,1)} %copy-done.4, bf16[1040,128]{1,0:T(8,128)(2,1)} %copy-done.5, bf16[1040,128]{1,0:T(8,128)(2,1)} %copy-done.6), custom_call_target="tpu_custom_call" | custom-call | flops 67108864 | bytes 2129920 | tf_op jit(solution)/shard_map/pallas_call | solution.py:211
  24.1 2.2 %collective-permute-start.6 = (bf16[4,272,128]{2,1,0:T(8,128)(2,1)}, bf16[4,272,128]{2,1,0:T(8,128)(2,1)S(1)}, u32[]{:S(2)}, u32[]{:S(2)}) collective-permute-start(bf16[4,272,128]{2,1,0:T(8,128)(2,1)} %get-tuple-element.112), channel_id=1, source_target_pairs={{0,4},{1,5},{2,6},{3,7},{4,0},{5,1},{6,2},{7,3},{8,12},{9,13},{10,... | collective-permute-start | bytes 835592 | tf_op jit(solution)/shard_map/ppermute | solution.py:477
  26.2 0.6 pad_add_fusion.pos_ref
  26.8 8.4 %shard_map.112 = (bf16[1024,3072]{1,0:T(8,128)(2,1)}, bf16[1024,3072]{1,0:T(8,128)(2,1)}, f32[1024,128]{1,0:T(8,128)}) custom-call(s32[2]{0:T(128)} %pad_add_fusion.pos_ref, s32[2,8,128]{2,1,0:T(8,128)} %stencil_ref.1, f32[2,8,128]{2,1,0:T(8,128)} %frac_ref.1, bf16[8,128,256]{2,1,0:T(8,128)(2,1)} %field_ref), custom_call_target="tpu_custom_call" | custom-call | flops 6291456 | bytes 13631488 | tf_op jit(solution)/shard_map/pallas_call | solution.py:390
  35.2 2.9 %collective-permute-done.5.refs_3_ = bf16[1040,128]{1,0:T(8,128)(2,1)S(1)} collective-permute-done((bf16[1040,128]{1,0:T(8,128)(2,1)}, bf16[1040,128]{1,0:T(8,128)(2,1)S(1)}, u32[]{:S(2)}, u32[]{:S(2)}) %collective-permute-start.5) | collective-permute-done | bytes 266272 | tf_op jit(solution)/shard_map/ppermute | solution.py:477
  38.1 0.3 collective-permute-start.7
  38.4 0.4 copy-done.11
  38.8 0.7 copy-done.7
  39.5 7.1 %shard_map.113 = (bf16[2,272,128]{2,1,0:T(8,128)(2,1)}, bf16[2,272,128]{2,1,0:T(8,128)(2,1)}, bf16[4,256,256]{2,1,0:T(8,128)(2,1)}, f32[4,256,128]{2,1,0:T(8,128)}, f32[3,8,128]{2,1,0:T(8,128)}) custom-call(bf16[1040,128]{1,0:T(8,128)(2,1)} %get-tuple-element.108.refs_0_, bf16[1040,128]{1,0:T(8,128)(2,1)} %copy-done.9, bf16[1040,128]{1,0:T(8,128)(2,1)} %copy-done.10, ...), custom_call_target="tpu_custom_call" | custom-call | flops 2013265920 | bytes 1572864 | tf_op jit(solution)/shard_map/pallas_call | solution.py:323
  46.6 1.1 %collective-permute-start.8 = (bf16[2,272,128]{2,1,0:T(8,128)(2,1)}, bf16[2,272,128]{2,1,0:T(8,128)(2,1)S(1)}, u32[]{:S(2)}, u32[]{:S(2)}) collective-permute-start(bf16[2,272,128]{2,1,0:T(8,128)(2,1)} %get-tuple-element.117.right_ref), channel_id=1, source_target_pairs={{0,1},{1,2},{2,3},{3,4},{4,5},{5,6},{6,7},{7,0},{8,9},{9,10},{10,1... | collective-permute-start | bytes 417800 | tf_op jit(solution)/shard_map/ppermute | solution.py:494
  47.7 3.1 %collective-permute-start.9 = (bf16[2,272,128]{2,1,0:T(8,128)(2,1)}, bf16[2,272,128]{2,1,0:T(8,128)(2,1)S(1)}, u32[]{:S(2)}, u32[]{:S(2)}) collective-permute-start(bf16[2,272,128]{2,1,0:T(8,128)(2,1)} %get-tuple-element.116.left_ref), channel_id=1, source_target_pairs={{1,0},{2,1},{3,2},{4,3},{5,4},{6,5},{7,6},{0,7},{9,8},{10,9},{11,1... | collective-permute-start | bytes 417800 | tf_op jit(solution)/shard_map/ppermute | solution.py:495
  50.8 2.5 %collective-permute-done.7.far_ref = bf16[4,272,128]{2,1,0:T(8,128)(2,1)S(1)} collective-permute-done((bf16[4,272,128]{2,1,0:T(8,128)(2,1)}, bf16[4,272,128]{2,1,0:T(8,128)(2,1)S(1)}, u32[]{:S(2)}, u32[]{:S(2)}) %collective-permute-start.7) | collective-permute-done | bytes 278560 | tf_op jit(solution)/shard_map/ppermute | solution.py:477
  53.3 0.7 copy-done.8
  54.0 6.7 %shard_map.114 = (bf16[4,256,256]{2,1,0:T(8,128)(2,1)}, bf16[6,272,128]{2,1,0:T(8,128)(2,1)}, bf16[6,272,128]{2,1,0:T(8,128)(2,1)}) custom-call(f32[4,256,128]{2,1,0:T(8,128)} %get-tuple-element.113.total_in, f32[3,8,128]{2,1,0:T(8,128)} %get-tuple-element.114.side_in, bf16[4,272,128]{2,1,0:T(8,128)(2,1)} %copy-done.8, ...), custom_call_target="tpu_custom_call" | custom-call | flops 2013265920 | bytes 786432 | tf_op jit(solution)/shard_map/pallas_call | solution.py:343
  60.7 0.7 slice_dynamic-update-slice_fusion.1
  61.4 0.7 slice_dynamic-update-slice_fusion
  62.1 9.3 %collective-permute-start.10 = (bf16[6,272,128]{2,1,0:T(8,128)(2,1)}, bf16[6,272,128]{2,1,0:T(8,128)(2,1)S(1)}, u32[]{:S(2)}, u32[]{:S(2)}) collective-permute-start(bf16[6,272,128]{2,1,0:T(8,128)(2,1)} %get-tuple-element.126), channel_id=1, source_target_pairs={{0,8},{8,16},{16,24},{1,9},{9,17},{17,25},{2,10},{10,18},{18,26},{... | collective-permute-start | bytes 1253384 | tf_op jit(solution)/shard_map/ppermute | solution.py:500
  71.4 1.9 %collective-permute-start.11 = (bf16[6,272,128]{2,1,0:T(8,128)(2,1)}, bf16[6,272,128]{2,1,0:T(8,128)(2,1)S(1)}, u32[]{:S(2)}, u32[]{:S(2)}) collective-permute-start(bf16[6,272,128]{2,1,0:T(8,128)(2,1)} %get-tuple-element.125), channel_id=1, source_target_pairs={{8,0},{16,8},{24,16},{9,1},{17,9},{25,17},{10,2},{18,10},{26,18},{... | collective-permute-start | bytes 1253384 | tf_op jit(solution)/shard_map/ppermute | solution.py:501
  73.3 5.5 %shard_map.115.base_ref = f32[1024,256]{1,0:T(8,128)} custom-call(bf16[2,272,128]{2,1,0:T(8,128)(2,1)} %copy-done, bf16[2,272,128]{2,1,0:T(8,128)(2,1)} %copy-done.1, bf16[4,256,256]{2,1,0:T(8,128)(2,1)} %get-tuple-element.121.edge, bf16[4,256,256]{2,1,0:T(8,128)(2,1)} %get-tuple-element.122.inner, bf16[1024,3072]{1,0:T(8,128)(2,1)} %get-tuple-element.123.lhs_ref, ...), custom_call_target="tpu_custom_call" | custom-call | flops 1610612736 | bytes 6291456 | tf_op jit(solution)/shard_map/pallas_call | solution.py:450
  78.8 2.1 %collective-permute-done.11.below = bf16[6,272,128]{2,1,0:T(8,128)(2,1)S(1)} collective-permute-done((bf16[6,272,128]{2,1,0:T(8,128)(2,1)}, bf16[6,272,128]{2,1,0:T(8,128)(2,1)S(1)}, u32[]{:S(2)}, u32[]{:S(2)}) %collective-permute-start.11) | collective-permute-done | bytes 417824 | tf_op jit(solution)/shard_map/ppermute | solution.py:501
  80.9 0.8 copy-done.3
  81.7 5.4 %shard_map.116 = bf16[1024,256]{1,0:T(8,128)(2,1)} custom-call(bf16[6,272,128]{2,1,0:T(8,128)(2,1)} %copy-done.2, bf16[6,272,128]{2,1,0:T(8,128)(2,1)} %copy-done.3, bf16[1024,3072]{1,0:T(8,128)(2,1)} %get-tuple-element.120.lhs_ref, f32[1024,256]{1,0:T(8,128)} %shard_map.115.base_ref), custom_call_target="tpu_custom_call" | custom-call | flops 1610612736 | bytes 6291456 | tf_op jit(solution)/shard_map/pallas_call | solution.py:450
  (27 shorter events, 0.1 us)
Async XLA Ops:
  5.6 11.7 %collective-permute-start = (bf16[1040,128]{1,0:T(8,128)(2,1)}, bf16[1040,128]{1,0:T(8,128)(2,1)S(1)}, u32[]{:S(2)}, u32[]{:S(2)}) collective-permute-start(bf16[1040,128]{1,0:T(8,128)(2,1)} %get-tuple-element.90), channel_id=1, source_target_pairs={{0,1},{1,0},{2,3},{3,2},{4,5},{5,4},{6,7},{7,6},{8,9},{9,8},{10,11... | collective-permute-start | bytes 798728 | tf_op jit(solution)/shard_map/ppermute | solution.py:477
  7.7 9.6 %collective-permute-start.1 = (bf16[1040,128]{1,0:T(8,128)(2,1)}, bf16[1040,128]{1,0:T(8,128)(2,1)S(1)}, u32[]{:S(2)}, u32[]{:S(2)}) collective-permute-start(bf16[1040,128]{1,0:T(8,128)(2,1)} %get-tuple-element.91), channel_id=1, source_target_pairs={{0,2},{1,3},{2,0},{3,1},{4,6},{5,7},{6,4},{7,5},{8,10},{9,11},{10,... | collective-permute-start | bytes 798728 | tf_op jit(solution)/shard_map/ppermute | solution.py:477
  9.0 11.7 %collective-permute-start.2 = (bf16[1040,128]{1,0:T(8,128)(2,1)}, bf16[1040,128]{1,0:T(8,128)(2,1)S(1)}, u32[]{:S(2)}, u32[]{:S(2)}) collective-permute-start(bf16[1040,128]{1,0:T(8,128)(2,1)} %get-tuple-element.92), channel_id=1, source_target_pairs={{0,3},{1,2},{2,1},{3,0},{4,7},{5,6},{6,5},{7,4},{8,11},{9,10},{10,... | collective-permute-start | bytes 798728 | tf_op jit(solution)/shard_map/ppermute | solution.py:477
  14.6 20.6 %collective-permute-start.3 = (bf16[1040,128]{1,0:T(8,128)(2,1)}, bf16[1040,128]{1,0:T(8,128)(2,1)S(1)}, u32[]{:S(2)}, u32[]{:S(2)}) collective-permute-start(bf16[1040,128]{1,0:T(8,128)(2,1)} %get-tuple-element.94), channel_id=1, source_target_pairs={{0,1},{1,0},{2,3},{3,2},{4,5},{5,4},{6,7},{7,6},{8,9},{9,8},{10,11... | collective-permute-start | bytes 798728 | tf_op jit(solution)/shard_map/ppermute | solution.py:477
  16.0 19.2 %collective-permute-start.4 = (bf16[1040,128]{1,0:T(8,128)(2,1)}, bf16[1040,128]{1,0:T(8,128)(2,1)S(1)}, u32[]{:S(2)}, u32[]{:S(2)}) collective-permute-start(bf16[1040,128]{1,0:T(8,128)(2,1)} %get-tuple-element.95), channel_id=1, source_target_pairs={{0,2},{1,3},{2,0},{3,1},{4,6},{5,7},{6,4},{7,5},{8,10},{9,11},{10,... | collective-permute-start | bytes 798728 | tf_op jit(solution)/shard_map/ppermute | solution.py:477
  17.3 3.4 %copy-start.4 = (bf16[1040,128]{1,0:T(8,128)(2,1)}, bf16[1040,128]{1,0:T(8,128)(2,1)S(1)}, u32[]{:S(2)}) copy-start(bf16[1040,128]{1,0:T(8,128)(2,1)S(1)} %collective-permute-done.refs_1_) | copy-start | bytes 798724
  17.3 20.8 %collective-permute-start.5 = (bf16[1040,128]{1,0:T(8,128)(2,1)}, bf16[1040,128]{1,0:T(8,128)(2,1)S(1)}, u32[]{:S(2)}, u32[]{:S(2)}) collective-permute-start(bf16[1040,128]{1,0:T(8,128)(2,1)} %get-tuple-element.96), channel_id=1, source_target_pairs={{0,3},{1,2},{2,1},{3,0},{4,7},{5,6},{6,5},{7,4},{8,11},{9,10},{10,... | collective-permute-start | bytes 798728 | tf_op jit(solution)/shard_map/ppermute | solution.py:477
  17.3 3.4 %copy-start.5 = (bf16[1040,128]{1,0:T(8,128)(2,1)}, bf16[1040,128]{1,0:T(8,128)(2,1)S(1)}, u32[]{:S(2)}) copy-start(bf16[1040,128]{1,0:T(8,128)(2,1)S(1)} %collective-permute-done.1.refs_2_) | copy-start | bytes 798724
  20.7 0.7 copy-start.6
  24.1 14.3 %collective-permute-start.6 = (bf16[4,272,128]{2,1,0:T(8,128)(2,1)}, bf16[4,272,128]{2,1,0:T(8,128)(2,1)S(1)}, u32[]{:S(2)}, u32[]{:S(2)}) collective-permute-start(bf16[4,272,128]{2,1,0:T(8,128)(2,1)} %get-tuple-element.112), channel_id=1, source_target_pairs={{0,4},{1,5},{2,6},{3,7},{4,0},{5,1},{6,2},{7,3},{8,12},{9,13},{10,... | collective-permute-start | bytes 835592 | tf_op jit(solution)/shard_map/ppermute | solution.py:477
  35.2 3.2 %copy-start.9 = (bf16[1040,128]{1,0:T(8,128)(2,1)}, bf16[1040,128]{1,0:T(8,128)(2,1)S(1)}, u32[]{:S(2)}) copy-start(bf16[1040,128]{1,0:T(8,128)(2,1)S(1)} %collective-permute-done.3.refs_1_) | copy-start | bytes 798724
  35.2 3.1 %copy-start.10 = (bf16[1040,128]{1,0:T(8,128)(2,1)}, bf16[1040,128]{1,0:T(8,128)(2,1)S(1)}, u32[]{:S(2)}) copy-start(bf16[1040,128]{1,0:T(8,128)(2,1)S(1)} %collective-permute-done.4.refs_2_) | copy-start | bytes 798724
  38.1 0.7 copy-start.11
  38.1 15.2 %collective-permute-start.7 = (bf16[4,272,128]{2,1,0:T(8,128)(2,1)}, bf16[4,272,128]{2,1,0:T(8,128)(2,1)S(1)}, u32[]{:S(2)}, u32[]{:S(2)}) collective-permute-start(bf16[4,272,128]{2,1,0:T(8,128)(2,1)} %get-tuple-element.115), channel_id=1, source_target_pairs={{0,4},{1,5},{2,6},{3,7},{4,0},{5,1},{6,2},{7,3},{8,12},{9,13},{10,... | collective-permute-start | bytes 835592 | tf_op jit(solution)/shard_map/ppermute | solution.py:477
  38.8 0.7 copy-start.7
  46.6 14.0 %collective-permute-start.8 = (bf16[2,272,128]{2,1,0:T(8,128)(2,1)}, bf16[2,272,128]{2,1,0:T(8,128)(2,1)S(1)}, u32[]{:S(2)}, u32[]{:S(2)}) collective-permute-start(bf16[2,272,128]{2,1,0:T(8,128)(2,1)} %get-tuple-element.117.right_ref), channel_id=1, source_target_pairs={{0,1},{1,2},{2,3},{3,4},{4,5},{5,6},{6,7},{7,0},{8,9},{9,10},{10,1... | collective-permute-start | bytes 417800 | tf_op jit(solution)/shard_map/ppermute | solution.py:494
  47.7 13.7 %collective-permute-start.9 = (bf16[2,272,128]{2,1,0:T(8,128)(2,1)}, bf16[2,272,128]{2,1,0:T(8,128)(2,1)S(1)}, u32[]{:S(2)}, u32[]{:S(2)}) collective-permute-start(bf16[2,272,128]{2,1,0:T(8,128)(2,1)} %get-tuple-element.116.left_ref), channel_id=1, source_target_pairs={{1,0},{2,1},{3,2},{4,3},{5,4},{6,5},{7,6},{0,7},{9,8},{10,9},{11,1... | collective-permute-start | bytes 417800 | tf_op jit(solution)/shard_map/ppermute | solution.py:495
  53.3 0.7 copy-start.8
  60.7 12.6 %copy-start = (bf16[2,272,128]{2,1,0:T(8,128)(2,1)}, bf16[2,272,128]{2,1,0:T(8,128)(2,1)S(1)}, u32[]{:S(2)}) copy-start(bf16[2,272,128]{2,1,0:T(8,128)(2,1)S(1)} %collective-permute-done.8.before) | copy-start | bytes 417796
  61.4 11.9 %copy-start.1 = (bf16[2,272,128]{2,1,0:T(8,128)(2,1)}, bf16[2,272,128]{2,1,0:T(8,128)(2,1)S(1)}, u32[]{:S(2)}) copy-start(bf16[2,272,128]{2,1,0:T(8,128)(2,1)S(1)} %collective-permute-done.9.after) | copy-start | bytes 417796
  62.1 16.7 %collective-permute-start.10 = (bf16[6,272,128]{2,1,0:T(8,128)(2,1)}, bf16[6,272,128]{2,1,0:T(8,128)(2,1)S(1)}, u32[]{:S(2)}, u32[]{:S(2)}) collective-permute-start(bf16[6,272,128]{2,1,0:T(8,128)(2,1)} %get-tuple-element.126), channel_id=1, source_target_pairs={{0,8},{8,16},{16,24},{1,9},{9,17},{17,25},{2,10},{10,18},{18,26},{... | collective-permute-start | bytes 1253384 | tf_op jit(solution)/shard_map/ppermute | solution.py:500
  71.4 9.6 %collective-permute-start.11 = (bf16[6,272,128]{2,1,0:T(8,128)(2,1)}, bf16[6,272,128]{2,1,0:T(8,128)(2,1)S(1)}, u32[]{:S(2)}, u32[]{:S(2)}) collective-permute-start(bf16[6,272,128]{2,1,0:T(8,128)(2,1)} %get-tuple-element.125), channel_id=1, source_target_pairs={{8,0},{16,8},{24,16},{9,1},{17,9},{25,17},{10,2},{18,10},{26,18},{... | collective-permute-start | bytes 1253384 | tf_op jit(solution)/shard_map/ppermute | solution.py:501
  78.8 2.1 %copy-start.2 = (bf16[6,272,128]{2,1,0:T(8,128)(2,1)}, bf16[6,272,128]{2,1,0:T(8,128)(2,1)S(1)}, u32[]{:S(2)}) copy-start(bf16[6,272,128]{2,1,0:T(8,128)(2,1)S(1)} %collective-permute-done.10.above) | copy-start | bytes 1253380
  80.9 0.8 copy-start.3

commit v3 on v2

--- a/solution.py
+++ b/solution.py
@@ -19,15 +19,15 @@
 PACKED = MEMBERS + TILE
 F32 = jnp.float32
 BF16 = jnp.bfloat16
-VMEM_LIMIT = 56 * 1024 * 1024
+MIB = 1024 * 1024
 
 SMEM_SPEC = pl.BlockSpec(memory_space=pltpu.SMEM)
 VMEM_SPEC = pl.BlockSpec(memory_space=pltpu.VMEM)
 ANY_SPEC = pl.BlockSpec(memory_space=pl.ANY)
 
 
-def params():
-    return pltpu.CompilerParams(vmem_limit_bytes=VMEM_LIMIT)
+def params(mebibytes):
+    return pltpu.CompilerParams(vmem_limit_bytes=mebibytes * MIB)
 
 
 def dot_nn(a, b):
@@ -42,11 +42,20 @@
     return lax.broadcasted_iota(jnp.int32, shape, dim)
 
 
-def gram_kernel(first, count, lon_size, me_ref, owner_ref, len_ref, points_ref, num_ref,
-                weight_ref, innov_ref, taper_ref, pert_ref, *rest):
-    outs, (source, filled, rows, w32, i32, t32, built, in_sem, out_sem) = rest[:count], rest[count:]
+def gram_kernel(first, count, lon_size, me_ref, *refs):
+    owner_hbm, len_hbm, points_hbm, num_hbm, weight_hbm, innov_hbm, taper_hbm, pert_ref = refs[:8]
+    outs = refs[8:8 + count]
+    (owner_ref, len_ref, points_ref, num_ref, weight_ref, innov_ref, taper_ref,
+     source, filled, rows, w32, i32, t32, built, small_sem, in_sem, out_sem) = refs[8 + count:]
     held, nobs, _ = pert_ref.shape
     me = me_ref[0]
+    loads = [
+        pltpu.make_async_copy(a, b, small_sem.at[n])
+        for n, (a, b) in enumerate((
+            (owner_hbm, owner_ref), (len_hbm, len_ref), (points_hbm, points_ref), (num_hbm, num_ref),
+            (weight_hbm, weight_ref), (innov_hbm, innov_ref), (taper_hbm, taper_ref)))]
+    for load in loads:
+        load.start()
 
     @pl.loop(0, lon_size)
     def _(k):
@@ -55,6 +64,8 @@
     @pl.loop(0, count * CAP)
     def _(s):
         source[first * CAP + s] = 0
+
+    loads[0].wait()
 
     @pl.loop(0, held)
     def _(b):
@@ -72,6 +83,8 @@
         for j in range(CAP):
             fetch(step, j).start()
 
+    for load in loads[1:]:
+        load.wait()
     w32[...] = weight_ref[...].astype(F32)
     i32[...] = innov_ref[...].astype(F32)
     t32[...] = jnp.concatenate(
@@ -122,14 +135,21 @@
         pltpu.make_async_copy(built.at[i], outs[i], out_sem.at[i]).wait()
 
 
-def batch_blocks(first, count, lon_size, me, owner, length, points, num, weight, innov, taper, pert):
+def batch_blocks(room, first, count, lon_size, me, owner, length, points, num, weight, innov, taper, pert):
     held, nobs, members = pert.shape
     return pl.pallas_call(
         functools.partial(gram_kernel, first, count, lon_size),
         out_shape=[jax.ShapeDtypeStruct((BLOCK, HALF), BF16)] * count,
-        in_specs=[SMEM_SPEC] * 5 + [VMEM_SPEC] * 3 + [ANY_SPEC],
+        in_specs=[SMEM_SPEC] + [ANY_SPEC] * 8,
         out_specs=[ANY_SPEC] * count,
         scratch_shapes=[
+            pltpu.SMEM(owner.shape, jnp.int32),
+            pltpu.SMEM(length.shape, jnp.int32),
+            pltpu.SMEM(points.shape, jnp.int32),
+            pltpu.SMEM(num.shape, jnp.int32),
+            pltpu.VMEM(weight.shape, BF16),
+            pltpu.VMEM(innov.shape, BF16),
+            pltpu.VMEM(taper.shape, BF16),
             pltpu.SMEM((lon_size * CAP,), jnp.int32),
             pltpu.SMEM((lon_size,), jnp.int32),
             pltpu.VMEM((count, CAP, nobs, members), BF16),
@@ -137,10 +157,11 @@
             pltpu.VMEM((held, nobs), F32),
             pltpu.VMEM((8, held), F32),
             pltpu.VMEM((count, BLOCK, HALF), BF16),
+            pltpu.SemaphoreType.DMA((7,)),
             pltpu.SemaphoreType.DMA((count, CAP)),
             pltpu.SemaphoreType.DMA((count,)),
         ],
-        compiler_params=params(),
+        compiler_params=params(room),
         cost_estimate=pl.CostEstimate(
             flops=count * CAP * 2 * nobs * members * members,
             bytes_accessed=count * CAP * nobs * members * 2, transcendentals=0),
@@ -220,7 +241,7 @@
             pltpu.VMEM((POINTS, MEMBERS, HALF), F32),
             pltpu.VMEM((3, POINTS, HALF), F32),
         ],
-        compiler_params=params(),
+        compiler_params=params(6 + len(blocks)),
         cost_estimate=pl.CostEstimate(
             flops=len(blocks) * CAP * POINTS * TILE * MEMBERS * HALF,
             bytes_accessed=len(blocks) * BLOCK * HALF * 4, transcendentals=0),
@@ -275,7 +296,8 @@
         inner = jnp.sum(root * shifts[i], axis=1, keepdims=True)
         mean_weight = jnp.sum(root * inner, axis=0, keepdims=True) * scales[i]
         result = root * jnp.sqrt((MEMBERS - 1) * scales[i])
-        full_ref[i] = (result + mean_weight).astype(BF16)
+        column = jnp.broadcast_to(mean_weight, (HALF, MEMBERS)).T
+        full_ref[i] = (result + jnp.concatenate([column, column], axis=1)).astype(BF16)
         triangle, corner, diagonal = pack(result)
         extra = jnp.concatenate(
             [diagonal, mean_weight[:, 0:HALF], mean_weight[:, HALF:MEMBERS], jnp.zeros((TILE - 3, HALF), F32)],
@@ -331,7 +353,7 @@
         in_specs=[VMEM_SPEC] * (len(blocks) + 1),
         out_specs=[VMEM_SPEC] * 5,
         scratch_shapes=newton_scratch(len(EDGE)) + [pltpu.VMEM((POINTS, MEMBERS, HALF), F32)],
-        compiler_params=params(),
+        compiler_params=params(12 + len(blocks)),
         cost_estimate=pl.CostEstimate(
             flops=len(EDGE) * 15 * 2 * MEMBERS ** 3, bytes_accessed=8 * MEMBERS * HALF * 6, transcendentals=0),
     )(*blocks, far)
@@ -346,7 +368,7 @@
         in_specs=[VMEM_SPEC] * 5,
         out_specs=[VMEM_SPEC] * (1 + PLAT),
         scratch_shapes=newton_scratch(count),
-        compiler_params=params(),
+        compiler_params=params(12),
         cost_estimate=pl.CostEstimate(
             flops=count * 15 * 2 * MEMBERS ** 3, bytes_accessed=count * MEMBERS * HALF * 6, transcendentals=0),
     )(total, side, far, left, right)
@@ -406,7 +428,7 @@
             pl.BlockSpec((width, len(RIM) * members), lambda i: (i, 0)),
             pl.BlockSpec((width, HALF), lambda i: (i, 0)),
         ],
-        compiler_params=params(),
+        compiler_params=params(12),
         cost_estimate=pl.CostEstimate(
             flops=cells * members * WINDOW, bytes_accessed=cells * members * (2 * WINDOW + 4), transcendentals=0),
     )(pos, stencil, frac, background)
@@ -415,49 +437,47 @@
 def place_packed(matrices, slot, ref, i):
     extra = ref[i, pl.ds(MEMBERS, TILE), :].astype(F32)
     full = unpack(ref[i, pl.ds(0, HALF), :].astype(F32), ref[i, pl.ds(HALF, HALF), :].astype(F32), extra[0:1])
-    full = full + jnp.concatenate([extra[1:2], extra[2:3]], axis=1)
-    matrices[:, slot * MEMBERS:(slot + 1) * MEMBERS] = full.astype(BF16)
+    row = jnp.concatenate([extra[1:2], extra[2:3]], axis=1)
+    column = jnp.broadcast_to(row, (HALF, MEMBERS)).T
+    full = full + jnp.concatenate([column, column], axis=1)
+    matrices[pl.ds(slot * MEMBERS, MEMBERS), :] = full.astype(BF16)
 
 
 def mid_kernel(before, after, edge, inner, lhs_ref, mean_ref, out_ref, matrices):
-    @pl.when(pl.program_id(0) == 0)
-    def _():
-        for r in range(PLAT):
-            place_packed(matrices, r * WIDE, before, r)
-            place_packed(matrices, r * WIDE + PLON + 1, after, r)
-            for c in range(PLON):
-                p = r * PLON + c
-                value = edge[EDGE.index(p)] if p in EDGE else inner[INNER.index(p)]
-                slot = r * WIDE + c + 1
-                matrices[:, slot * MEMBERS:(slot + 1) * MEMBERS] = value
-
-    out_ref[...] = dot_nt(lhs_ref[...], matrices[...]) + mean_ref[:, 0:1]
+    for r in range(PLAT):
+        place_packed(matrices, r * WIDE, before, r)
+        place_packed(matrices, r * WIDE + PLON + 1, after, r)
+        for c in range(PLON):
+            p = r * PLON + c
+            value = edge[EDGE.index(p)] if p in EDGE else inner[INNER.index(p)]
+            matrices[pl.ds((r * WIDE + c + 1) * MEMBERS, MEMBERS), :] = value
+
+    @pl.loop(0, lhs_ref.shape[0] // MEMBERS)
+    def _(t):
+        at = pl.ds(t * MEMBERS, MEMBERS)
+        out_ref[at, :] = dot_nn(lhs_ref[at, :], matrices[...]) + mean_ref[at, 0:1]
 
 
 def rim_kernel(above, below, lhs_ref, base_ref, out_ref, matrices):
-    @pl.when(pl.program_id(0) == 0)
-    def _():
-        for c in range(WIDE):
-            place_packed(matrices, c, above, c)
-            place_packed(matrices, WIDE + c, below, c)
-
-    out_ref[...] = (dot_nt(lhs_ref[...], matrices[...]) + base_ref[...]).astype(BF16)
+    for c in range(WIDE):
+        place_packed(matrices, c, above, c)
+        place_packed(matrices, WIDE + c, below, c)
+
+    @pl.loop(0, lhs_ref.shape[0] // MEMBERS)
+    def _(t):
+        at = pl.ds(t * MEMBERS, MEMBERS)
+        out_ref[at, :] = (dot_nn(lhs_ref[at, :], matrices[...]) + base_ref[at, :]).astype(BF16)
 
 
 def mix(kernel, transforms, lhs, base, dtype):
     cells, depth = lhs.shape
-    tile = min(cells, 2 * MEMBERS)
     return pl.pallas_call(
         kernel,
-        grid=(cells // tile,),
         out_shape=jax.ShapeDtypeStruct((cells, MEMBERS), dtype),
-        in_specs=[pl.BlockSpec(t.shape, lambda i: (0, 0, 0)) for t in transforms] + [
-            pl.BlockSpec((tile, depth), lambda i: (i, 0)),
-            pl.BlockSpec((tile, base.shape[1]), lambda i: (i, 0)),
-        ],
-        out_specs=pl.BlockSpec((tile, MEMBERS), lambda i: (i, 0)),
-        scratch_shapes=[pltpu.VMEM((MEMBERS, depth), BF16)],
-        compiler_params=params(),
+        in_specs=[VMEM_SPEC] * (len(transforms) + 2),
+        out_specs=VMEM_SPEC,
+        scratch_shapes=[pltpu.VMEM((depth, MEMBERS), BF16)],
+        compiler_params=params(20),
         cost_estimate=pl.CostEstimate(
             flops=2 * cells * depth * MEMBERS, bytes_accessed=cells * depth * 2, transcendentals=0),
     )(*transforms, lhs, base)
@@ -476,9 +496,9 @@
     def swap(value, offset):
         return lax.ppermute(value, "lon", [(i, i ^ offset) for i in range(lon_size)])
 
-    far = batch_blocks(half, half, lon_size, *fixed)
+    far = batch_blocks(57, half, half, lon_size, *fixed)
     relayed = [far[0]] + [swap(far[i], i) for i in range(1, half)]
-    near = batch_blocks(0, half, lon_size, *fixed)
+    near = batch_blocks(57, 0, half, lon_size, *fixed)
     got = [near[0]] + [swap(near[i], i) for i in range(1, half)]
     relayed, _ = lax.optimization_barrier((relayed, near))
     far_edge, far_inner = relay_sums(relayed)

time: 87.8 us -> 76.9 us (0.88)
  Pallas kernels: 46.9 us -> 33.2 us
  waiting for transfers between devices: 10.9 us -> 19.8 us
  local copies, waits for them, and re-layouts: 4.77 us -> 1.02 us
  starting transfers between devices: 23.9 us -> 21.3 us
    ppermute x8, waiting for transfers between devices: 8.78 us -> 15 us  [swap(): lax.ppermute(value, 'lon', [(i, i ^ offset) for i in range(lon_size)])]
    pallas_call x2, Pallas kernels: 10.9 us -> 6.42 us  [mix(): pl.pallas_call(kernel, out_shape=jax.ShapeDtypeStruct((cells, MEMBERS), d...]
    ppermute x1, starting transfers between devices: 9.25 us -> 5.42 us  [on_device(): above = lax.ppermute(rows[PLAT - 1], 'lat', north)]
    unnamed x24 -> x10, local copies, waits for them, and re-layouts: 3.35 us -> 0.98 us
    pallas_call x1, Pallas kernels: 8.38 us -> 6.02 us  [cell_parts(): pl.pallas_call(functools.partial(cell_kernel, point_cols), grid=(rows,),...]
    ppermute x1, waiting for transfers between devices: 2.14 us -> 4.4 us  [on_device(): below = lax.ppermute(rows[0], 'lat', south)]
    pallas_call x1, Pallas kernels: 6.66 us -> 4.46 us  [inner_transforms(): pl.pallas_call(inner_kernel, out_shape=[jax.ShapeDtypeStruct((count, MEMB...]
    pallas_call x1, Pallas kernels: 7.13 us -> 5.02 us  [edge_transforms(): pl.pallas_call(functools.partial(edge_kernel, len(blocks)), out_shape=[co...]
  transfers between devices with their start and end apart: 12 -> 12, of which waited for: 4 -> 6; matrix products, arithmetic and copies ran while one was open for 1% -> 0% of each run, Pallas kernels for 41% -> 32%
where the time goes in v3:
time: 76.9 us; the launch traced here: 75.5 us
  Pallas kernels  33.2 us (43%)
  starting transfers between devices  21.3 us (28%)
  waiting for transfers between devices  19.8 us (26%)
  local copies, waits for them, and re-layouts  1.02 us (1%)
    ppermute x8, waiting for transfers between devices, swap(): lax.ppermute(value, 'lon', [(i, i ^ offset) for i in range(lon_size)])  15 us
    pallas_call x2, Pallas kernels, batch_blocks(): pl.pallas_call(functools.partial(gram_kernel, first, count, lon_size), ou...  10.6 us
    ppermute x8, starting transfers between devices, swap(): lax.ppermute(value, 'lon', [(i, i ^ offset) for i in range(lon_size)])  9.75 us
    pallas_call x2, Pallas kernels, mix(): pl.pallas_call(kernel, out_shape=jax.ShapeDtypeStruct((cells, MEMBERS), d...  6.42 us
    pallas_call x1, Pallas kernels, cell_parts(): pl.pallas_call(functools.partial(cell_kernel, point_cols), grid=(rows,),...  6.02 us
    ppermute x1, starting transfers between devices, on_device(): above = lax.ppermute(rows[PLAT - 1], 'lat', north)  5.42 us
    pallas_call x1, Pallas kernels, edge_transforms(): pl.pallas_call(functools.partial(edge_kernel, len(blocks)), out_shape=[co...  5.02 us
    pallas_call x1, Pallas kernels, inner_transforms(): pl.pallas_call(inner_kernel, out_shape=[jax.ShapeDtypeStruct((count, MEMB...  4.46 us
  transfers between devices with their start and end apart: 12, of which 6 were waited for; matrix products, arithmetic and copies ran while one was open for 0% of the time, Pallas kernels for 32%

profile of v3, /device:TPU:1, one launch (start us, length us, event | category | flops | bytes accessed | tf_op | source)
XLA Modules:
  0.0 75.5 jit_solution(14570976437088516719)
XLA Ops:
  0.0 5.3 %shard_map.109 = (bf16[1040,128]{1,0:T(8,128)(2,1)}, bf16[1040,128]{1,0:T(8,128)(2,1)}, bf16[1040,128]{1,0:T(8,128)(2,1)}, bf16[1040,128]{1,0:T(8,128)(2,1)}) custom-call(s32[1]{0:T(128)} %bitcast.me_ref, s32[1,32]{1,0:T(1,128)} %bitcast.10, s32[1,32]{1,0:T(1,128)} %refs_1_.3, s32[3,32]{1,0:T(4,128)} %bitcast.6, s32[32]{0:T(128)} %refs_3_.3, ...), custom_call_target="tpu_custom_call" | custom-call | flops 1073741824 | bytes 4194304 | tf_op jit(solution)/shard_map/pallas_call | solution.py:140
  5.3 0.0 copy-start
  5.3 0.0 copy-start.2
  5.4 0.0 copy-start.3
  5.4 2.1 %collective-permute-start = (bf16[1040,128]{1,0:T(8,128)(2,1)}, bf16[1040,128]{1,0:T(8,128)(2,1)S(1)}, u32[]{:S(2)}, u32[]{:S(2)}) collective-permute-start(bf16[1040,128]{1,0:T(8,128)(2,1)} %get-tuple-element.90), channel_id=1, source_target_pairs={{0,1},{1,0},{2,3},{3,2},{4,5},{5,4},{6,7},{7,6},{8,9},{9,8},{10,11... | collective-permute-start | bytes 798728 | tf_op jit(solution)/shard_map/ppermute | solution.py:497
  7.5 1.3 %collective-permute-start.1 = (bf16[1040,128]{1,0:T(8,128)(2,1)}, bf16[1040,128]{1,0:T(8,128)(2,1)S(1)}, u32[]{:S(2)}, u32[]{:S(2)}) collective-permute-start(bf16[1040,128]{1,0:T(8,128)(2,1)} %get-tuple-element.91), channel_id=1, source_target_pairs={{0,2},{1,3},{2,0},{3,1},{4,6},{5,7},{6,4},{7,5},{8,10},{9,11},{10,... | collective-permute-start | bytes 798728 | tf_op jit(solution)/shard_map/ppermute | solution.py:497
  8.8 0.0 collective-permute-start.2
  8.8 5.3 %shard_map.110 = (bf16[1040,128]{1,0:T(8,128)(2,1)}, bf16[1040,128]{1,0:T(8,128)(2,1)}, bf16[1040,128]{1,0:T(8,128)(2,1)}, bf16[1040,128]{1,0:T(8,128)(2,1)}) custom-call(s32[1]{0:T(128)} %bitcast.me_ref, s32[1,32]{1,0:T(1,128)} %bitcast.11, s32[1,32]{1,0:T(1,128)} %refs_1_.3, s32[3,32]{1,0:T(4,128)} %bitcast.7, s32[32]{0:T(128)} %refs_3_.3, ...), custom_call_target="tpu_custom_call" | custom-call | flops 1073741824 | bytes 4194304 | tf_op jit(solution)/shard_map/pallas_call | solution.py:140
  14.1 1.4 %collective-permute-start.3 = (bf16[1040,128]{1,0:T(8,128)(2,1)}, bf16[1040,128]{1,0:T(8,128)(2,1)S(1)}, u32[]{:S(2)}, u32[]{:S(2)}) collective-permute-start(bf16[1040,128]{1,0:T(8,128)(2,1)} %get-tuple-element.94), channel_id=1, source_target_pairs={{0,1},{1,0},{2,3},{3,2},{4,5},{5,4},{6,7},{7,6},{8,9},{9,8},{10,11... | collective-permute-start | bytes 798728 | tf_op jit(solution)/shard_map/ppermute | solution.py:497
  15.5 1.3 %collective-permute-start.4 = (bf16[1040,128]{1,0:T(8,128)(2,1)}, bf16[1040,128]{1,0:T(8,128)(2,1)S(1)}, u32[]{:S(2)}, u32[]{:S(2)}) collective-permute-start(bf16[1040,128]{1,0:T(8,128)(2,1)} %get-tuple-element.95), channel_id=1, source_target_pairs={{0,2},{1,3},{2,0},{3,1},{4,6},{5,7},{6,4},{7,5},{8,10},{9,11},{10,... | collective-permute-start | bytes 798728 | tf_op jit(solution)/shard_map/ppermute | solution.py:497
  16.8 0.0 collective-permute-done.refs_1_
  16.8 0.0 collective-permute-start.5
  16.8 3.7 %collective-permute-done.2.refs_3_ = bf16[1040,128]{1,0:T(8,128)(2,1)S(1)} collective-permute-done((bf16[1040,128]{1,0:T(8,128)(2,1)}, bf16[1040,128]{1,0:T(8,128)(2,1)S(1)}, u32[]{:S(2)}, u32[]{:S(2)}) %collective-permute-start.2) | collective-permute-done | bytes 266272 | tf_op jit(solution)/shard_map/ppermute | solution.py:497
  20.5 0.6 shard_map.111
  21.1 2.2 %collective-permute-start.6 = (bf16[4,272,128]{2,1,0:T(8,128)(2,1)S(1)}, bf16[4,272,128]{2,1,0:T(8,128)(2,1)S(1)}, u32[]{:S(2)}, u32[]{:S(2)}) collective-permute-start(bf16[4,272,128]{2,1,0:T(8,128)(2,1)S(1)} %get-tuple-element.112), channel_id=1, source_target_pairs={{0,4},{1,5},{2,6},{3,7},{4,0},{5,1},{6,2},{7,3},{8,12},{9,13},{10,... | collective-permute-start | bytes 835592 | tf_op jit(solution)/shard_map/ppermute | solution.py:497
  23.4 0.1 pad_add_fusion.pos_ref
  23.5 6.0 %shard_map.112 = (bf16[1024,3072]{1,0:T(8,128)(2,1)S(1)}, bf16[1024,3072]{1,0:T(8,128)(2,1)S(1)}, f32[1024,128]{1,0:T(8,128)S(1)}) custom-call(s32[2]{0:T(128)S(1)} %pad_add_fusion.pos_ref, s32[2,8,128]{2,1,0:T(8,128)S(1)} %copy-done.2, f32[2,8,128]{2,1,0:T(8,128)S(1)} %copy-done.3, bf16[8,128,256]{2,1,0:T(8,128)(2,1)S(1)} %copy-done), custom_call_target="tpu_custom_call" | custom-call | flops 6291456 | bytes 13631488 | tf_op jit(solution)/shard_map/pallas_call | solution.py:412
  29.5 2.5 %collective-permute-done.4.refs_2_ = bf16[1040,128]{1,0:T(8,128)(2,1)S(1)} collective-permute-done((bf16[1040,128]{1,0:T(8,128)(2,1)}, bf16[1040,128]{1,0:T(8,128)(2,1)S(1)}, u32[]{:S(2)}, u32[]{:S(2)}) %collective-permute-start.4) | collective-permute-done | bytes 266272 | tf_op jit(solution)/shard_map/ppermute | solution.py:497
  32.0 5.8 %collective-permute-done.5.refs_3_ = bf16[1040,128]{1,0:T(8,128)(2,1)S(1)} collective-permute-done((bf16[1040,128]{1,0:T(8,128)(2,1)}, bf16[1040,128]{1,0:T(8,128)(2,1)S(1)}, u32[]{:S(2)}, u32[]{:S(2)}) %collective-permute-start.5) | collective-permute-done | bytes 266272 | tf_op jit(solution)/shard_map/ppermute | solution.py:497
  37.9 1.4 %collective-permute-start.7 = (bf16[4,272,128]{2,1,0:T(8,128)(2,1)S(1)}, bf16[4,272,128]{2,1,0:T(8,128)(2,1)S(1)}, u32[]{:S(2)}, u32[]{:S(2)}) collective-permute-start(bf16[4,272,128]{2,1,0:T(8,128)(2,1)S(1)} %get-tuple-element.115), channel_id=1, source_target_pairs={{0,4},{1,5},{2,6},{3,7},{4,0},{5,1},{6,2},{7,3},{8,12},{9,13},{10,... | collective-permute-start | bytes 835592 | tf_op jit(solution)/shard_map/ppermute | solution.py:497
  39.3 1.0 %copy-done.4 = bf16[1040,128]{1,0:T(8,128)(2,1)S(1)} copy-done((bf16[1040,128]{1,0:T(8,128)(2,1)S(1)}, bf16[1040,128]{1,0:T(8,128)(2,1)}, u32[]{:S(2)}) %copy-start.4) | copy-done | bytes 266264
  40.2 5.0 %shard_map.113 = (bf16[2,272,128]{2,1,0:T(8,128)(2,1)S(1)}, bf16[2,272,128]{2,1,0:T(8,128)(2,1)S(1)}, bf16[4,256,256]{2,1,0:T(8,128)(2,1)S(1)}, f32[4,256,128]{2,1,0:T(8,128)S(1)}, f32[3,8,128]{2,1,0:T(8,128)S(1)}) custom-call(bf16[1040,128]{1,0:T(8,128)(2,1)S(1)} %copy-done.4, bf16[1040,128]{1,0:T(8,128)(2,1)S(1)} %collective-permute-done.3.refs_1_, ...), custom_call_target="tpu_custom_call" | custom-call | flops 2013265920 | bytes 1572864 | tf_op jit(solution)/shard_map/pallas_call | solution.py:345
  45.2 0.3 collective-permute-start.8
  45.6 3.9 %collective-permute-start.9 = (bf16[2,272,128]{2,1,0:T(8,128)(2,1)S(1)}, bf16[2,272,128]{2,1,0:T(8,128)(2,1)S(1)}, u32[]{:S(2)}, u32[]{:S(2)}) collective-permute-start(bf16[2,272,128]{2,1,0:T(8,128)(2,1)S(1)} %get-tuple-element.116.left_ref), channel_id=1, source_target_pairs={{1,0},{2,1},{3,2},{4,3},{5,4},{6,5},{7,6},{0,7},{9,8},{10,9},{11,1... | collective-permute-start | bytes 417800 | tf_op jit(solution)/shard_map/ppermute | solution.py:515
  49.5 3.0 %collective-permute-done.7.far_ref = bf16[4,272,128]{2,1,0:T(8,128)(2,1)S(1)} collective-permute-done((bf16[4,272,128]{2,1,0:T(8,128)(2,1)S(1)}, bf16[4,272,128]{2,1,0:T(8,128)(2,1)S(1)}, u32[]{:S(2)}, u32[]{:S(2)}) %collective-permute-start.7) | collective-permute-done | bytes 278560 | tf_op jit(solution)/shard_map/ppermute | solution.py:497
  52.4 4.5 %shard_map.114 = (bf16[4,256,256]{2,1,0:T(8,128)(2,1)S(1)}, bf16[6,272,128]{2,1,0:T(8,128)(2,1)S(1)}, bf16[6,272,128]{2,1,0:T(8,128)(2,1)S(1)}) custom-call(f32[4,256,128]{2,1,0:T(8,128)S(1)} %get-tuple-element.113.total_in, f32[3,8,128]{2,1,0:T(8,128)S(1)} %get-tuple-element.114.side_in, bf16[4,272,128]{2,1,0:T(8,128)(2,1)S(1)} %collective-permute-done.7.far_ref, ...), custom_call_target="tpu_custom_call" | custom-call | flops 2013265920 | bytes 786432 | tf_op jit(solution)/shard_map/pallas_call | solution.py:365
  57.0 5.4 %collective-permute-start.10 = (bf16[6,272,128]{2,1,0:T(8,128)(2,1)S(1)}, bf16[6,272,128]{2,1,0:T(8,128)(2,1)S(1)}, u32[]{:S(2)}, u32[]{:S(2)}) collective-permute-start(bf16[6,272,128]{2,1,0:T(8,128)(2,1)S(1)} %get-tuple-element.126), channel_id=1, source_target_pairs={{0,8},{8,16},{16,24},{1,9},{9,17},{17,25},{2,10},{10,18},{18,26},{... | collective-permute-start | bytes 1253384 | tf_op jit(solution)/shard_map/ppermute | solution.py:520
  62.4 1.9 %collective-permute-start.11 = (bf16[6,272,128]{2,1,0:T(8,128)(2,1)S(1)}, bf16[6,272,128]{2,1,0:T(8,128)(2,1)S(1)}, u32[]{:S(2)}, u32[]{:S(2)}) collective-permute-start(bf16[6,272,128]{2,1,0:T(8,128)(2,1)S(1)} %get-tuple-element.125), channel_id=1, source_target_pairs={{8,0},{16,8},{24,16},{9,1},{17,9},{25,17},{10,2},{18,10},{26,18},{... | collective-permute-start | bytes 1253384 | tf_op jit(solution)/shard_map/ppermute | solution.py:521
  64.3 2.6 %shard_map.115.base_ref = f32[1024,256]{1,0:T(8,128)S(1)} custom-call(bf16[2,272,128]{2,1,0:T(8,128)(2,1)S(1)} %collective-permute-done.8.before, bf16[2,272,128]{2,1,0:T(8,128)(2,1)S(1)} %collective-permute-done.9.after, bf16[4,256,256]{2,1,0:T(8,128)(2,1)S(1)} %get-tuple-element.121.edge, bf16[4,256,256]{2,1,0:T(8,128)(2,1)S(1)} %get-tuple-element.122.inner, ...), custom_call_target="tpu_custom_call" | custom-call | flops 1610612736 | bytes 6291456 | tf_op jit(solution)/shard_map/pallas_call | solution.py:474
  66.9 0.4 collective-permute-done.10.above
  67.3 4.4 %collective-permute-done.11.below = bf16[6,272,128]{2,1,0:T(8,128)(2,1)S(1)} collective-permute-done((bf16[6,272,128]{2,1,0:T(8,128)(2,1)S(1)}, bf16[6,272,128]{2,1,0:T(8,128)(2,1)S(1)}, u32[]{:S(2)}, u32[]{:S(2)}) %collective-permute-start.11) | collective-permute-done | bytes 417824 | tf_op jit(solution)/shard_map/ppermute | solution.py:521
  71.7 3.8 %shard_map.116 = bf16[1024,256]{1,0:T(8,128)(2,1)} custom-call(bf16[6,272,128]{2,1,0:T(8,128)(2,1)S(1)} %collective-permute-done.10.above, bf16[6,272,128]{2,1,0:T(8,128)(2,1)S(1)} %collective-permute-done.11.below, bf16[1024,3072]{1,0:T(8,128)(2,1)S(1)} %get-tuple-element.120.lhs_ref, f32[1024,256]{1,0:T(8,128)S(1)} %shard_map.115.base_ref), custom_call_target="tpu_custom_call" | custom-call | flops 1610612736 | bytes 6291456 | tf_op jit(solution)/shard_map/pallas_call | solution.py:474
  (13 shorter events, 0.1 us)
Async XLA Ops:
  5.3 15.2 %copy-start.1 = (bf16[1040,128]{1,0:T(8,128)(2,1)S(1)}, bf16[1040,128]{1,0:T(8,128)(2,1)}, u32[]{:S(2)}) copy-start(bf16[1040,128]{1,0:T(8,128)(2,1)} %get-tuple-element.97.refs_0_) | copy-start | bytes 798724
  5.3 18.1 %copy-start = (bf16[8,128,256]{2,1,0:T(8,128)(2,1)S(1)}, bf16[8,128,256]{2,1,0:T(8,128)(2,1)}, u32[]{:S(2)}) copy-start(bf16[8,128,256]{2,1,0:T(8,128)(2,1)} %field_ref) | copy-start | bytes 1572868
  5.3 18.1 %copy-start.2 = (s32[2,8,128]{2,1,0:T(8,128)S(1)}, s32[2,8,128]{2,1,0:T(8,128)}, u32[]{:S(2)}) copy-start(s32[2,8,128]{2,1,0:T(8,128)} %stencil_ref.1) | copy-start | bytes 24580
  5.4 18.1 %copy-start.3 = (f32[2,8,128]{2,1,0:T(8,128)S(1)}, f32[2,8,128]{2,1,0:T(8,128)}, u32[]{:S(2)}) copy-start(f32[2,8,128]{2,1,0:T(8,128)} %frac_ref.1) | copy-start | bytes 24580
  5.4 11.4 %collective-permute-start = (bf16[1040,128]{1,0:T(8,128)(2,1)}, bf16[1040,128]{1,0:T(8,128)(2,1)S(1)}, u32[]{:S(2)}, u32[]{:S(2)}) collective-permute-start(bf16[1040,128]{1,0:T(8,128)(2,1)} %get-tuple-element.90), channel_id=1, source_target_pairs={{0,1},{1,0},{2,3},{3,2},{4,5},{5,4},{6,7},{7,6},{8,9},{9,8},{10,11... | collective-permute-start | bytes 798728 | tf_op jit(solution)/shard_map/ppermute | solution.py:497
  7.5 9.3 %collective-permute-start.1 = (bf16[1040,128]{1,0:T(8,128)(2,1)}, bf16[1040,128]{1,0:T(8,128)(2,1)S(1)}, u32[]{:S(2)}, u32[]{:S(2)}) collective-permute-start(bf16[1040,128]{1,0:T(8,128)(2,1)} %get-tuple-element.91), channel_id=1, source_target_pairs={{0,2},{1,3},{2,0},{3,1},{4,6},{5,7},{6,4},{7,5},{8,10},{9,11},{10,... | collective-permute-start | bytes 798728 | tf_op jit(solution)/shard_map/ppermute | solution.py:497
  8.8 11.7 %collective-permute-start.2 = (bf16[1040,128]{1,0:T(8,128)(2,1)}, bf16[1040,128]{1,0:T(8,128)(2,1)S(1)}, u32[]{:S(2)}, u32[]{:S(2)}) collective-permute-start(bf16[1040,128]{1,0:T(8,128)(2,1)} %get-tuple-element.92), channel_id=1, source_target_pairs={{0,3},{1,2},{2,1},{3,0},{4,7},{5,6},{6,5},{7,4},{8,11},{9,10},{10,... | collective-permute-start | bytes 798728 | tf_op jit(solution)/shard_map/ppermute | solution.py:497
  14.1 15.4 %collective-permute-start.3 = (bf16[1040,128]{1,0:T(8,128)(2,1)}, bf16[1040,128]{1,0:T(8,128)(2,1)S(1)}, u32[]{:S(2)}, u32[]{:S(2)}) collective-permute-start(bf16[1040,128]{1,0:T(8,128)(2,1)} %get-tuple-element.94), channel_id=1, source_target_pairs={{0,1},{1,0},{2,3},{3,2},{4,5},{5,4},{6,7},{7,6},{8,9},{9,8},{10,11... | collective-permute-start | bytes 798728 | tf_op jit(solution)/shard_map/ppermute | solution.py:497
  15.5 16.6 %collective-permute-start.4 = (bf16[1040,128]{1,0:T(8,128)(2,1)}, bf16[1040,128]{1,0:T(8,128)(2,1)S(1)}, u32[]{:S(2)}, u32[]{:S(2)}) collective-permute-start(bf16[1040,128]{1,0:T(8,128)(2,1)} %get-tuple-element.95), channel_id=1, source_target_pairs={{0,2},{1,3},{2,0},{3,1},{4,6},{5,7},{6,4},{7,5},{8,10},{9,11},{10,... | collective-permute-start | bytes 798728 | tf_op jit(solution)/shard_map/ppermute | solution.py:497
  16.8 21.1 %collective-permute-start.5 = (bf16[1040,128]{1,0:T(8,128)(2,1)}, bf16[1040,128]{1,0:T(8,128)(2,1)S(1)}, u32[]{:S(2)}, u32[]{:S(2)}) collective-permute-start(bf16[1040,128]{1,0:T(8,128)(2,1)} %get-tuple-element.96), channel_id=1, source_target_pairs={{0,3},{1,2},{2,1},{3,0},{4,7},{5,6},{6,5},{7,4},{8,11},{9,10},{10,... | collective-permute-start | bytes 798728 | tf_op jit(solution)/shard_map/ppermute | solution.py:497
  21.1 18.1 %collective-permute-start.6 = (bf16[4,272,128]{2,1,0:T(8,128)(2,1)S(1)}, bf16[4,272,128]{2,1,0:T(8,128)(2,1)S(1)}, u32[]{:S(2)}, u32[]{:S(2)}) collective-permute-start(bf16[4,272,128]{2,1,0:T(8,128)(2,1)S(1)} %get-tuple-element.112), channel_id=1, source_target_pairs={{0,4},{1,5},{2,6},{3,7},{4,0},{5,1},{6,2},{7,3},{8,12},{9,13},{10,... | collective-permute-start | bytes 835592 | tf_op jit(solution)/shard_map/ppermute | solution.py:497
  37.9 14.5 %collective-permute-start.7 = (bf16[4,272,128]{2,1,0:T(8,128)(2,1)S(1)}, bf16[4,272,128]{2,1,0:T(8,128)(2,1)S(1)}, u32[]{:S(2)}, u32[]{:S(2)}) collective-permute-start(bf16[4,272,128]{2,1,0:T(8,128)(2,1)S(1)} %get-tuple-element.115), channel_id=1, source_target_pairs={{0,4},{1,5},{2,6},{3,7},{4,0},{5,1},{6,2},{7,3},{8,12},{9,13},{10,... | collective-permute-start | bytes 835592 | tf_op jit(solution)/shard_map/ppermute | solution.py:497
  39.3 1.0 %copy-start.4 = (bf16[1040,128]{1,0:T(8,128)(2,1)S(1)}, bf16[1040,128]{1,0:T(8,128)(2,1)}, u32[]{:S(2)}) copy-start(bf16[1040,128]{1,0:T(8,128)(2,1)} %get-tuple-element.108.refs_0_) | copy-start | bytes 798724
  45.2 11.6 %collective-permute-start.8 = (bf16[2,272,128]{2,1,0:T(8,128)(2,1)S(1)}, bf16[2,272,128]{2,1,0:T(8,128)(2,1)S(1)}, u32[]{:S(2)}, u32[]{:S(2)}) collective-permute-start(bf16[2,272,128]{2,1,0:T(8,128)(2,1)S(1)} %get-tuple-element.117.right_ref), channel_id=1, source_target_pairs={{0,1},{1,2},{2,3},{3,4},{4,5},{5,6},{6,7},{7,0},{8,9},{9,10},{10,1... | collective-permute-start | bytes 417800 | tf_op jit(solution)/shard_map/ppermute | solution.py:514
  45.6 11.3 %collective-permute-start.9 = (bf16[2,272,128]{2,1,0:T(8,128)(2,1)S(1)}, bf16[2,272,128]{2,1,0:T(8,128)(2,1)S(1)}, u32[]{:S(2)}, u32[]{:S(2)}) collective-permute-start(bf16[2,272,128]{2,1,0:T(8,128)(2,1)S(1)} %get-tuple-element.116.left_ref), channel_id=1, source_target_pairs={{1,0},{2,1},{3,2},{4,3},{5,4},{6,5},{7,6},{0,7},{9,8},{10,9},{11,1... | collective-permute-start | bytes 417800 | tf_op jit(solution)/shard_map/ppermute | solution.py:515
  57.0 10.4 %collective-permute-start.10 = (bf16[6,272,128]{2,1,0:T(8,128)(2,1)S(1)}, bf16[6,272,128]{2,1,0:T(8,128)(2,1)S(1)}, u32[]{:S(2)}, u32[]{:S(2)}) collective-permute-start(bf16[6,272,128]{2,1,0:T(8,128)(2,1)S(1)} %get-tuple-element.126), channel_id=1, source_target_pairs={{0,8},{8,16},{16,24},{1,9},{9,17},{17,25},{2,10},{10,18},{18,26},{... | collective-permute-start | bytes 1253384 | tf_op jit(solution)/shard_map/ppermute | solution.py:520
  62.4 9.4 %collective-permute-start.11 = (bf16[6,272,128]{2,1,0:T(8,128)(2,1)S(1)}, bf16[6,272,128]{2,1,0:T(8,128)(2,1)S(1)}, u32[]{:S(2)}, u32[]{:S(2)}) collective-permute-start(bf16[6,272,128]{2,1,0:T(8,128)(2,1)S(1)} %get-tuple-element.125), channel_id=1, source_target_pairs={{8,0},{16,8},{24,16},{9,1},{17,9},{25,17},{10,2},{18,10},{26,18},{... | collective-permute-start | bytes 1253384 | tf_op jit(solution)/shard_map/ppermute | solution.py:521

commit v4 on v3

--- a/solution.py
+++ b/solution.py
@@ -222,18 +222,20 @@
     edge_ref, inner_ref, acc, side = refs[count:]
     sum_by_point(blocks, acc, side)
     for ref, listed in ((edge_ref, EDGE), (inner_ref, INNER)):
+        rows = []
         for i, p in enumerate(listed):
-            ref[i, pl.ds(0, MEMBERS), :] = acc[p].astype(BF16)
-            rows = [side[q, pl.ds(p, 1), :] for q in range(3)] + [jnp.zeros((TILE - 3, HALF), F32)]
-            ref[i, pl.ds(MEMBERS, TILE), :] = jnp.concatenate(rows, axis=0).astype(BF16)
+            ref[pl.ds(i * MEMBERS, MEMBERS), :] = acc[p].astype(BF16)
+            rows += [side[q, pl.ds(p, 1), :] for q in range(3)]
+        rows.append(jnp.zeros((TILE - len(rows), HALF), F32))
+        ref[pl.ds(len(listed) * MEMBERS, TILE), :] = jnp.concatenate(rows, axis=0).astype(BF16)
 
 
 def relay_sums(blocks):
     return pl.pallas_call(
         functools.partial(relay_kernel, len(blocks)),
         out_shape=[
-            jax.ShapeDtypeStruct((len(EDGE), PACKED, HALF), BF16),
-            jax.ShapeDtypeStruct((len(INNER), PACKED, HALF), BF16),
+            jax.ShapeDtypeStruct((len(EDGE) * MEMBERS + TILE, HALF), BF16),
+            jax.ShapeDtypeStruct((len(INNER) * MEMBERS + TILE, HALF), BF16),
         ],
         in_specs=[VMEM_SPEC] * len(blocks),
         out_specs=[VMEM_SPEC] * 2,
@@ -253,11 +255,11 @@
     eye = (iota((MEMBERS, MEMBERS), 0) == iota((MEMBERS, MEMBERS), 1)).astype(F32)
     scales, shifts = [], []
     points = range(len(listed))
+    extra = far_ref[pl.ds(len(listed) * MEMBERS, TILE), :].astype(F32)
     for i in points:
         p = listed[i]
-        packed = total_of(p) + far_ref[i, pl.ds(0, MEMBERS), :].astype(F32)
-        extra = far_ref[i, pl.ds(MEMBERS, TILE), :].astype(F32)
-        diagonal, low, high = [side_of(p)[q] + extra[q:q + 1] for q in range(3)]
+        packed = total_of(p) + far_ref[pl.ds(i * MEMBERS, MEMBERS), :].astype(F32)
+        diagonal, low, high = [side_of(p)[q] + extra[3 * i + q:3 * i + q + 1] for q in range(3)]
         shifts.append(jnp.concatenate([low, high], axis=1))
         system = unpack(packed[0:HALF], packed[HALF:MEMBERS], diagonal) + (MEMBERS - 1) * eye
         square = jnp.sum(jnp.sum(system * system, axis=0, keepdims=True), axis=1, keepdims=True)
@@ -281,8 +283,7 @@
 
     advance()
 
-    @pl.loop(0, ITERS - 2)
-    def _(sweep):
+    for sweep in range(ITERS - 2):
         for i in points:
             value = 1.5 * z32[i] - 0.5 * dot_nn(wb[i], zb[i])
             z32[i] = value
@@ -302,15 +303,17 @@
         extra = jnp.concatenate(
             [diagonal, mean_weight[:, 0:HALF], mean_weight[:, HALF:MEMBERS], jnp.zeros((TILE - 3, HALF), F32)],
             axis=0)
-        ref, where = packed_out(listed[i])
-        ref[where, pl.ds(0, HALF), :] = triangle.astype(BF16)
-        ref[where, pl.ds(HALF, HALF), :] = corner.astype(BF16)
-        ref[where, pl.ds(MEMBERS, TILE), :] = extra.astype(BF16)
+        for ref, where in packed_out(listed[i]):
+            ref[where, pl.ds(0, HALF), :] = triangle.astype(BF16)
+            ref[where, pl.ds(HALF, HALF), :] = corner.astype(BF16)
+            ref[where, pl.ds(MEMBERS, TILE), :] = extra.astype(BF16)
 
 
 def edge_kernel(count, *refs):
     blocks = refs[:count]
-    far_ref, left_ref, right_ref, full_ref, total_ref, side_ref, w32, z32, wb, gb, zb, acc = refs[count:]
+    far_ref, left_ref, right_ref = refs[count:count + 3]
+    rows = refs[count + 3:count + 3 + PLAT]
+    full_ref, total_ref, side_ref, w32, z32, wb, gb, zb, acc = refs[count + 3 + PLAT:]
     sum_by_point(blocks, acc, side_ref)
     for i, p in enumerate(INNER):
         total_ref[i] = acc[p]
@@ -319,20 +322,18 @@
         lambda p: acc[p],
         lambda p: [side_ref[q, pl.ds(p, 1), :] for q in range(3)],
         far_ref, (w32, z32, wb, gb, zb), full_ref,
-        lambda p: (left_ref if p % PLON == 0 else right_ref, p // PLON))
-
-
-def inner_kernel(total_in, side_in, far_ref, left_ref, right_ref, full_ref, *refs):
+        lambda p: [
+            (left_ref if p % PLON == 0 else right_ref, p // PLON), (rows[p // PLON], 0 if p % PLON == 0 else 1)])
+
+
+def inner_kernel(total_in, side_in, far_ref, full_ref, *refs):
     rows, scratch = refs[:PLAT], refs[PLAT:]
     transform_points(
         INNER,
         lambda p: total_in[INNER.index(p)],
         lambda p: [side_in[q, pl.ds(p, 1), :] for q in range(3)],
         far_ref, scratch, full_ref,
-        lambda p: (rows[p // PLON], p % PLON + 1))
-    for r in range(PLAT):
-        rows[r][1] = left_ref[r]
-        rows[r][PLON] = right_ref[r]
+        lambda p: [(rows[p // PLON], p % PLON)])
 
 
 def newton_scratch(count):
@@ -346,12 +347,13 @@
         functools.partial(edge_kernel, len(blocks)),
         out_shape=[
             columns, columns,
+            *[jax.ShapeDtypeStruct((2, PACKED, HALF), BF16)] * PLAT,
             jax.ShapeDtypeStruct((len(EDGE), MEMBERS, MEMBERS), BF16),
             jax.ShapeDtypeStruct((len(INNER), MEMBERS, HALF), F32),
             jax.ShapeDtypeStruct((3, POINTS, HALF), F32),
         ],
         in_specs=[VMEM_SPEC] * (len(blocks) + 1),
-        out_specs=[VMEM_SPEC] * 5,
+        out_specs=[VMEM_SPEC] * (5 + PLAT),
         scratch_shapes=newton_scratch(len(EDGE)) + [pltpu.VMEM((POINTS, MEMBERS, HALF), F32)],
         compiler_params=params(12 + len(blocks)),
         cost_estimate=pl.CostEstimate(
@@ -359,19 +361,19 @@
     )(*blocks, far)
 
 
-def inner_transforms(total, side, far, left, right):
+def inner_transforms(total, side, far):
     count = total.shape[0]
-    row = jax.ShapeDtypeStruct((PLON + 2, PACKED, HALF), BF16)
+    row = jax.ShapeDtypeStruct((PLON, PACKED, HALF), BF16)
     return pl.pallas_call(
         inner_kernel,
         out_shape=[jax.ShapeDtypeStruct((count, MEMBERS, MEMBERS), BF16)] + [row] * PLAT,
-        in_specs=[VMEM_SPEC] * 5,
+        in_specs=[VMEM_SPEC] * 3,
         out_specs=[VMEM_SPEC] * (1 + PLAT),
         scratch_shapes=newton_scratch(count),
         compiler_params=params(12),
         cost_estimate=pl.CostEstimate(
             flops=count * 15 * 2 * MEMBERS ** 3, bytes_accessed=count * MEMBERS * HALF * 6, transcendentals=0),
-    )(total, side, far, left, right)
+    )(total, side, far)
 
 
 WIDE = PLON + 2
@@ -380,10 +382,16 @@
 RIM = list(range(WIDE)) + list(range(WINDOW - WIDE, WINDOW))
 
 
-def cell_kernel(point_cols, pos_ref, stencil_ref, frac_ref, field_ref, mid_ref, rim_ref, mean_ref):
+def cell_kernel(point_cols, pos_ref, stencil_ref, frac_ref, field_ref, kept_in, mid_ref, rim_ref, mean_ref,
+                kept_out):
     width = stencil_ref.shape[2]
     lat_pos, lon_pos = pos_ref[0], pos_ref[1]
     i = pl.program_id(0)
+
+    @pl.when(i == 0)
+    def _():
+        kept_out[...] = kept_in[...]
+
     ids = iota((HALF, width), 0)
     field = field_ref[0].astype(F32)
     mean = jnp.mean(field, axis=1, keepdims=True)
@@ -406,7 +414,7 @@
             ref[:, n * MEMBERS:(n + 1) * MEMBERS] = (dev * turned[:, point:point + 1]).astype(BF16)
 
 
-def cell_parts(point_cols, pos, stencil, frac, background):
+def cell_parts(point_cols, pos, stencil, frac, background, kept):
     rows, width, members = background.shape
     cells = rows * width
     return pl.pallas_call(
@@ -416,22 +424,25 @@
             jax.ShapeDtypeStruct((cells, len(MID) * members), BF16),
             jax.ShapeDtypeStruct((cells, len(RIM) * members), BF16),
             jax.ShapeDtypeStruct((cells, HALF), F32),
+            jax.ShapeDtypeStruct(kept.shape, kept.dtype),
         ],
         in_specs=[
             SMEM_SPEC,
             pl.BlockSpec(stencil.shape, lambda i: (0, 0, 0)),
             pl.BlockSpec(frac.shape, lambda i: (0, 0, 0)),
             pl.BlockSpec((1, width, members), lambda i: (i, 0, 0)),
+            pl.BlockSpec(kept.shape, lambda i: (0, 0)),
         ],
         out_specs=[
             pl.BlockSpec((width, len(MID) * members), lambda i: (i, 0)),
             pl.BlockSpec((width, len(RIM) * members), lambda i: (i, 0)),
             pl.BlockSpec((width, HALF), lambda i: (i, 0)),
+            pl.BlockSpec(kept.shape, lambda i: (0, 0)),
         ],
         compiler_params=params(12),
         cost_estimate=pl.CostEstimate(
             flops=cells * members * WINDOW, bytes_accessed=cells * members * (2 * WINDOW + 4), transcendentals=0),
-    )(pos, stencil, frac, background)
+    )(pos, stencil, frac, background, kept)
 
 
 def place_packed(matrices, slot, ref, i):
@@ -452,21 +463,17 @@
             value = edge[EDGE.index(p)] if p in EDGE else inner[INNER.index(p)]
             matrices[pl.ds((r * WIDE + c + 1) * MEMBERS, MEMBERS), :] = value
 
-    @pl.loop(0, lhs_ref.shape[0] // MEMBERS)
-    def _(t):
-        at = pl.ds(t * MEMBERS, MEMBERS)
-        out_ref[at, :] = dot_nn(lhs_ref[at, :], matrices[...]) + mean_ref[at, 0:1]
-
-
-def rim_kernel(above, below, lhs_ref, base_ref, out_ref, matrices):
-    for c in range(WIDE):
-        place_packed(matrices, c, above, c)
-        place_packed(matrices, WIDE + c, below, c)
-
-    @pl.loop(0, lhs_ref.shape[0] // MEMBERS)
-    def _(t):
-        at = pl.ds(t * MEMBERS, MEMBERS)
-        out_ref[at, :] = (dot_nn(lhs_ref[at, :], matrices[...]) + base_ref[at, :]).astype(BF16)
+    out_ref[...] = dot_nn(lhs_ref[...], matrices[...]) + mean_ref[:, 0:1]
+
+
+def rim_kernel(above_edge, below_edge, above, below, lhs_ref, base_ref, out_ref, matrices):
+    for row, edge, rest in ((0, above_edge, above), (1, below_edge, below)):
+        for i, c in enumerate((0, PLON - 1)):
+            place_packed(matrices, row * WIDE + c + 1, edge, i)
+        for i, c in enumerate([-1] + list(range(1, PLON - 1)) + [PLON]):
+            place_packed(matrices, row * WIDE + c + 1, rest, i)
+
+    out_ref[...] = (dot_nn(lhs_ref[...], matrices[...]) + base_ref[...]).astype(BF16)
 
 
 def mix(kernel, transforms, lhs, base, dtype):
@@ -496,31 +503,37 @@
     def swap(value, offset):
         return lax.ppermute(value, "lon", [(i, i ^ offset) for i in range(lon_size)])
 
-    far = batch_blocks(57, half, half, lon_size, *fixed)
-    relayed = [far[0]] + [swap(far[i], i) for i in range(1, half)]
-    near = batch_blocks(57, 0, half, lon_size, *fixed)
-    got = [near[0]] + [swap(near[i], i) for i in range(1, half)]
-    relayed, _ = lax.optimization_barrier((relayed, near))
-    far_edge, far_inner = relay_sums(relayed)
+    far = batch_blocks(57, half + 1, half - 1, lon_size, *fixed)
+    relayed = [swap(far[i - 1], i) for i in range(1, half)]
+    *near, own_far = batch_blocks(57, 1, half, lon_size, *fixed)
+    got = [swap(near[i - 1], i) for i in range(1, half)]
+    obs_pert, near, own_far = lax.optimization_barrier((obs_pert, near, own_far))
+    own_near, = batch_blocks(57, 0, 1, lon_size, *fixed[:-1], obs_pert)
+    relayed, own_near = lax.optimization_barrier((relayed, own_near))
+    far_edge, far_inner = relay_sums([own_far] + relayed)
     far_edge, far_inner, background = lax.optimization_barrier((far_edge, far_inner, background))
-    mid_lhs, rim_lhs, mean = cell_parts(PLON * lon_size, pos, stencil, frac, background)
+    mid_lhs, rim_lhs, mean, own_near = cell_parts(PLON * lon_size, pos, stencil, frac, background, own_near)
+    got = [own_near] + got
     far_edge = swap(far_edge, half)
     far_inner, got, mid_lhs, rim_lhs, mean = lax.optimization_barrier((far_inner, got, mid_lhs, rim_lhs, mean))
     far_inner = swap(far_inner, half)
 
-    left, right, edge, total, side = edge_transforms(got, far_edge)
+    left, right, *edge_rows, edge, total, side = edge_transforms(got, far_edge)
     up = [(i, (i + 1) % lon_size) for i in range(lon_size)]
     down = [(j, i) for i, j in up]
+    north = [(i, i + 1) for i in range(lat_size - 1)]
+    south = [(j, i) for i, j in north]
     before = lax.ppermute(right, "lon", up)
     after = lax.ppermute(left, "lon", down)
-    inner, *rows = inner_transforms(total, side, far_inner, left, right)
-    rows = [rows[r].at[0].set(before[r]).at[PLON + 1].set(after[r]) for r in range(PLAT)]
-    north = [(i, i + 1) for i in range(lat_size - 1)]
-    south = [(j, i) for i, j in north]
+    above_edge = lax.ppermute(edge_rows[PLAT - 1], "lat", north)
+    below_edge = lax.ppermute(edge_rows[0], "lat", south)
+    far_inner, above_edge, below_edge = lax.optimization_barrier((far_inner, above_edge, below_edge))
+    inner, *rows = inner_transforms(total, side, far_inner)
+    rows = [rows[r].at[0].set(before[r]).at[PLON - 1].set(after[r]) for r in range(PLAT)]
     above = lax.ppermute(rows[PLAT - 1], "lat", north)
     below = lax.ppermute(rows[0], "lat", south)
     partial = mix(mid_kernel, [before, after, edge, inner], mid_lhs, mean, F32)
-    return mix(rim_kernel, [above, below], rim_lhs, partial, BF16).reshape(background.shape)
+    return mix(rim_kernel, [above_edge, below_edge, above, below], rim_lhs, partial, BF16).reshape(background.shape)
 
 
 def solution(mesh):

time: 76.9 us -> 70.8 us (0.921); the launches traced: 75.5 us -> 70.3 us
  waiting for transfers between devices: 19.8 us -> 8.68 us
  starting transfers between devices: 21.3 us -> 27.9 us
    ppermute x8, waiting for transfers between devices: 15 us -> 6.65 us  [swap(): lax.ppermute(value, 'lon', [(i, i ^ offset) for i in range(lon_size)])]
    ppermute x0 -> x2, starting transfers between devices: none -> 7.08 us  [the longest x1 5.16 us: on_device(): above_edge = lax.ppermute(edge_rows[PLAT - 1], 'lat', north)]
    ppermute x1, waiting for transfers between devices: 4.4 us -> 0.16 us  [on_device(): below = lax.ppermute(rows[0], 'lat', south)]
    pallas_call x2 -> x3, Pallas kernels: 10.6 us -> 13.7 us  [batch_blocks(): pl.pallas_call(functools.partial(gram_kernel, first, count, lon_size), ou...]
    pallas_call x2, Pallas kernels: 6.42 us -> 4.68 us  [mix(): pl.pallas_call(kernel, out_shape=jax.ShapeDtypeStruct((cells, MEMBERS), d...]
    pallas_call x1, Pallas kernels: 5.02 us -> 3.82 us  [edge_transforms(): pl.pallas_call(functools.partial(edge_kernel, len(blocks)), out_shape=[co...]
    pallas_call x1, Pallas kernels: 4.46 us -> 3.47 us  [inner_transforms(): pl.pallas_call(inner_kernel, out_shape=[jax.ShapeDtypeStruct((count, MEMB...]
    ppermute x1, waiting for transfers between devices: 0.41 us -> 1.18 us  [on_device(): above = lax.ppermute(rows[PLAT - 1], 'lat', north)]
  transfers between devices with their start and end apart: 12 -> 14, of which waited for: 6 -> 6; matrix products, arithmetic and copies ran while one was open for 0% -> 0% of each run, Pallas kernels for 32% -> 36%
where the time goes in v4:
time: 70.8 us; the launch traced here: 70.3 us
  Pallas kernels  32.5 us (46%)
  starting transfers between devices  27.9 us (39%)
  waiting for transfers between devices  8.68 us (12%)
  local copies, waits for them, and re-layouts  1.02 us (1%)
    pallas_call x3, Pallas kernels, batch_blocks(): pl.pallas_call(functools.partial(gram_kernel, first, count, lon_size), ou...  13.7 us
    ppermute x8, starting transfers between devices, swap(): lax.ppermute(value, 'lon', [(i, i ^ offset) for i in range(lon_size)])  9.97 us
    ppermute x8, waiting for transfers between devices, swap(): lax.ppermute(value, 'lon', [(i, i ^ offset) for i in range(lon_size)])  6.65 us
    pallas_call x1, Pallas kernels, cell_parts(): pl.pallas_call(functools.partial(cell_kernel, point_cols), grid=(rows,),...  6.19 us
    ppermute x1, starting transfers between devices, on_device(): above_edge = lax.ppermute(edge_rows[PLAT - 1], 'lat', north)  5.16 us
    ppermute x1, starting transfers between devices, on_device(): above = lax.ppermute(rows[PLAT - 1], 'lat', north)  4.69 us
    pallas_call x2, Pallas kernels, mix(): pl.pallas_call(kernel, out_shape=jax.ShapeDtypeStruct((cells, MEMBERS), d...  4.68 us
    ppermute x1, starting transfers between devices, on_device(): after = lax.ppermute(left, 'lon', down)  3.91 us
  transfers between devices with their start and end apart: 14, of which 6 were waited for; matrix products, arithmetic and copies ran while one was open for 0% of the time, Pallas kernels for 36%

profile of v4, /device:TPU:1, one launch (start us, length us, event | category | flops | bytes accessed | tf_op | source)
XLA Modules:
  0.0 70.3 jit_solution(4256990115759751086)
XLA Ops:
  0.0 4.8 %shard_map.110 = (bf16[1040,128]{1,0:T(8,128)(2,1)}, bf16[1040,128]{1,0:T(8,128)(2,1)}, bf16[1040,128]{1,0:T(8,128)(2,1)}) custom-call(s32[1]{0:T(128)} %bitcast.me_ref, s32[1,32]{1,0:T(1,128)} %bitcast.12, s32[1,32]{1,0:T(1,128)} %refs_1_.5, s32[3,32]{1,0:T(4,128)} %bitcast.6, s32[32]{0:T(128)} %refs_3_.5, bf16[32,512]{1,0:T(8,128)(2,1)} %refs_4_.5, ...), custom_call_target="tpu_custom_call" | custom-call | flops 805306368 | bytes 3145728 | tf_op jit(solution)/shard_map/pallas_call | solution.py:140
  4.8 2.1 %collective-permute-start = (bf16[1040,128]{1,0:T(8,128)(2,1)}, bf16[1040,128]{1,0:T(8,128)(2,1)S(1)}, u32[]{:S(2)}, u32[]{:S(2)}) collective-permute-start(bf16[1040,128]{1,0:T(8,128)(2,1)} %get-tuple-element.101), channel_id=1, source_target_pairs={{0,1},{1,0},{2,3},{3,2},{4,5},{5,4},{6,7},{7,6},{8,9},{9,8},{10,11... | collective-permute-start | bytes 798728 | tf_op jit(solution)/shard_map/ppermute | solution.py:504
  6.9 1.3 %collective-permute-start.1 = (bf16[1040,128]{1,0:T(8,128)(2,1)}, bf16[1040,128]{1,0:T(8,128)(2,1)S(1)}, u32[]{:S(2)}, u32[]{:S(2)}) collective-permute-start(bf16[1040,128]{1,0:T(8,128)(2,1)} %get-tuple-element.102), channel_id=1, source_target_pairs={{0,2},{1,3},{2,0},{3,1},{4,6},{5,7},{6,4},{7,5},{8,10},{9,11},{10,... | collective-permute-start | bytes 798728 | tf_op jit(solution)/shard_map/ppermute | solution.py:504
  8.2 5.3 %shard_map.109 = (bf16[1040,128]{1,0:T(8,128)(2,1)}, bf16[1040,128]{1,0:T(8,128)(2,1)}, bf16[1040,128]{1,0:T(8,128)(2,1)}, bf16[1040,128]{1,0:T(8,128)(2,1)}) custom-call(s32[1]{0:T(128)} %bitcast.me_ref, s32[1,32]{1,0:T(1,128)} %bitcast.13, s32[1,32]{1,0:T(1,128)} %refs_1_.5, s32[3,32]{1,0:T(4,128)} %bitcast.7, s32[32]{0:T(128)} %refs_3_.5, ...), custom_call_target="tpu_custom_call" | custom-call | flops 1073741824 | bytes 4194304 | tf_op jit(solution)/shard_map/pallas_call | solution.py:140
  13.5 0.0 copy-start.1
  13.5 0.0 copy-start.3
  13.5 1.4 %collective-permute-start.3 = (bf16[1040,128]{1,0:T(8,128)(2,1)}, bf16[1040,128]{1,0:T(8,128)(2,1)S(1)}, u32[]{:S(2)}, u32[]{:S(2)}) collective-permute-start(bf16[1040,128]{1,0:T(8,128)(2,1)} %get-tuple-element.96), channel_id=1, source_target_pairs={{0,1},{1,0},{2,3},{3,2},{4,5},{5,4},{6,7},{7,6},{8,9},{9,8},{10,11... | collective-permute-start | bytes 798728 | tf_op jit(solution)/shard_map/ppermute | solution.py:504
  14.9 1.3 %collective-permute-start.4 = (bf16[1040,128]{1,0:T(8,128)(2,1)}, bf16[1040,128]{1,0:T(8,128)(2,1)S(1)}, u32[]{:S(2)}, u32[]{:S(2)}) collective-permute-start(bf16[1040,128]{1,0:T(8,128)(2,1)} %get-tuple-element.97), channel_id=1, source_target_pairs={{0,2},{1,3},{2,0},{3,1},{4,6},{5,7},{6,4},{7,5},{8,10},{9,11},{10,... | collective-permute-start | bytes 798728 | tf_op jit(solution)/shard_map/ppermute | solution.py:504
  16.2 3.6 %shard_map.111.kept_in = bf16[1040,128]{1,0:T(8,128)(2,1)} custom-call(s32[1]{0:T(128)} %bitcast.me_ref, s32[1,32]{1,0:T(1,128)} %bitcast.14, s32[1,32]{1,0:T(1,128)} %refs_1_.5, s32[3,32]{1,0:T(4,128)} %bitcast.8, s32[32]{0:T(128)} %refs_3_.5, bf16[32,512]{1,0:T(8,128)(2,1)} %refs_4_.5, bf16[32,512]{1,0:T(8,128)(2,1)} %refs_5_.5, bf16[3,32]{1,0:T(4,128)(2,1)} %bitcast.11, ...), custom_call_target="tpu_custom_call" | custom-call | flops 268435456 | bytes 1048576 | tf_op jit(solution)/shard_map/pallas_call | solution.py:140
  19.9 0.1 collective-permute-start.5
  20.0 0.6 shard_map.112
  20.6 2.5 %collective-permute-start.7 = (bf16[1040,128]{1,0:T(8,128)(2,1)S(1)}, bf16[1040,128]{1,0:T(8,128)(2,1)S(1)}, u32[]{:S(2)}, u32[]{:S(2)}) collective-permute-start(bf16[1040,128]{1,0:T(8,128)(2,1)S(1)} %get-tuple-element.122), channel_id=1, source_target_pairs={{0,4},{1,5},{2,6},{3,7},{4,0},{5,1},{6,2},{7,3},{8,12},{9,13},{10,... | collective-permute-start | bytes 798728 | tf_op jit(solution)/shard_map/ppermute | solution.py:504
  23.1 0.1 pad_add_fusion.pos_ref
  23.2 0.9 %copy-done = bf16[1040,128]{1,0:T(8,128)(2,1)S(1)} copy-done((bf16[1040,128]{1,0:T(8,128)(2,1)S(1)}, bf16[1040,128]{1,0:T(8,128)(2,1)}, u32[]{:S(2)}) %copy-start) | copy-done | bytes 266264
  24.2 6.2 %shard_map.113 = (bf16[1024,3072]{1,0:T(8,128)(2,1)S(1)}, bf16[1024,3072]{1,0:T(8,128)(2,1)S(1)}, f32[1024,128]{1,0:T(8,128)S(1)}, bf16[1040,128]{1,0:T(8,128)(2,1)S(1)}) custom-call(s32[2]{0:T(128)S(1)} %pad_add_fusion.pos_ref, s32[2,8,128]{2,1,0:T(8,128)S(1)} %copy-done.3, f32[2,8,128]{2,1,0:T(8,128)S(1)} %copy-done.4, bf16[8,128,256]{2,1,0:T(8,128)(2,1)S(1)} %copy-done.1, ...), custom_call_target="tpu_custom_call" | custom-call | flops 6291456 | bytes 13631488 | tf_op jit(solution)/shard_map/pallas_call | solution.py:420
  30.4 0.8 %collective-permute-done.4.refs_2_ = bf16[1040,128]{1,0:T(8,128)(2,1)S(1)} collective-permute-done((bf16[1040,128]{1,0:T(8,128)(2,1)}, bf16[1040,128]{1,0:T(8,128)(2,1)S(1)}, u32[]{:S(2)}, u32[]{:S(2)}) %collective-permute-start.4) | collective-permute-done | bytes 266272 | tf_op jit(solution)/shard_map/ppermute | solution.py:504
  31.2 5.8 %collective-permute-done.5.refs_3_ = bf16[1040,128]{1,0:T(8,128)(2,1)S(1)} collective-permute-done((bf16[1040,128]{1,0:T(8,128)(2,1)S(1)}, bf16[1040,128]{1,0:T(8,128)(2,1)S(1)}, u32[]{:S(2)}, u32[]{:S(2)}) %collective-permute-start.5) | collective-permute-done | bytes 266272 | tf_op jit(solution)/shard_map/ppermute | solution.py:504
  37.0 1.3 %collective-permute-start.6 = (bf16[1040,128]{1,0:T(8,128)(2,1)S(1)}, bf16[1040,128]{1,0:T(8,128)(2,1)S(1)}, u32[]{:S(2)}, u32[]{:S(2)}) collective-permute-start(bf16[1040,128]{1,0:T(8,128)(2,1)S(1)} %get-tuple-element.117), channel_id=1, source_target_pairs={{0,4},{1,5},{2,6},{3,7},{4,0},{5,1},{6,2},{7,3},{8,12},{9,13},{10,... | collective-permute-start | bytes 798728 | tf_op jit(solution)/shard_map/ppermute | solution.py:504
  38.3 3.8 %shard_map.114 = (bf16[2,272,128]{2,1,0:T(8,128)(2,1)S(1)}, bf16[2,272,128]{2,1,0:T(8,128)(2,1)S(1)}, bf16[2,272,128]{2,1,0:T(8,128)(2,1)S(1)}, bf16[2,272,128]{...) custom-call(bf16[1040,128]{1,0:T(8,128)(2,1)S(1)} %get-tuple-element, ...), custom_call_target="tpu_custom_call" | custom-call | flops 2013265920 | bytes 1572864 | tf_op jit(solution)/shard_map/pallas_call | solution.py:346
  42.1 5.2 %collective-permute-start.8 = (bf16[2,272,128]{2,1,0:T(8,128)(2,1)S(1)}, bf16[2,272,128]{2,1,0:T(8,128)(2,1)S(1)}, u32[]{:S(2)}, u32[]{:S(2)}) collective-permute-start(bf16[2,272,128]{2,1,0:T(8,128)(2,1)S(1)} %get-tuple-element.123), channel_id=1, source_target_pairs={{0,8},{8,16},{16,24},{1,9},{9,17},{17,25},{2,10},{10,18},{18,26},{... | collective-permute-start | bytes 417800 | tf_op jit(solution)/shard_map/ppermute | solution.py:528
  47.3 1.9 %collective-permute-start.9 = (bf16[2,272,128]{2,1,0:T(8,128)(2,1)S(1)}, bf16[2,272,128]{2,1,0:T(8,128)(2,1)S(1)}, u32[]{:S(2)}, u32[]{:S(2)}) collective-permute-start(bf16[2,272,128]{2,1,0:T(8,128)(2,1)S(1)} %get-tuple-element.124), channel_id=1, source_target_pairs={{8,0},{16,8},{24,16},{9,1},{17,9},{25,17},{10,2},{18,10},{26,18},{... | collective-permute-start | bytes 417800 | tf_op jit(solution)/shard_map/ppermute | solution.py:529
  49.2 0.3 collective-permute-start.10
  49.5 3.9 %collective-permute-start.11 = (bf16[2,272,128]{2,1,0:T(8,128)(2,1)S(1)}, bf16[2,272,128]{2,1,0:T(8,128)(2,1)S(1)}, u32[]{:S(2)}, u32[]{:S(2)}) collective-permute-start(bf16[2,272,128]{2,1,0:T(8,128)(2,1)S(1)} %get-tuple-element.132), channel_id=1, source_target_pairs={{1,0},{2,1},{3,2},{4,3},{5,4},{6,5},{7,6},{0,7},{9,8},{10,9},{11,1... | collective-permute-start | bytes 417800 | tf_op jit(solution)/shard_map/ppermute | solution.py:527
  53.5 0.5 collective-permute-done.9.below_edge
  54.0 3.5 %shard_map.115 = (bf16[4,256,256]{2,1,0:T(8,128)(2,1)S(1)}, bf16[4,272,128]{2,1,0:T(8,128)(2,1)S(1)}, bf16[4,272,128]{2,1,0:T(8,128)(2,1)S(1)}) custom-call(f32[4,256,128]{2,1,0:T(8,128)S(1)} %get-tuple-element.127.total_in, f32[3,8,128]{2,1,0:T(8,128)S(1)} %get-tuple-element.128.side_in, bf16[1040,128]{1,0:T(8,128)(2,1)S(1)} %collective-permute-done.6.far_ref), custom_call_target="tpu_custom_call" | custom-call | flops 2013265920 | bytes 786432 | tf_op jit(solution)/shard_map/pallas_call | solution.py:367
  57.5 0.2 collective-permute-done.11.after
  57.7 1.9 %collective-permute-start.13 = (bf16[4,272,128]{2,1,0:T(8,128)(2,1)S(1)}, bf16[4,272,128]{2,1,0:T(8,128)(2,1)S(1)}, u32[]{:S(2)}, u32[]{:S(2)}) collective-permute-start(bf16[4,272,128]{2,1,0:T(8,128)(2,1)S(1)} %get-tuple-element.139), channel_id=1, source_target_pairs={{8,0},{16,8},{24,16},{9,1},{17,9},{25,17},{10,2},{18,10},{26,18},{... | collective-permute-start | bytes 835592 | tf_op jit(solution)/shard_map/ppermute | solution.py:534
  59.6 4.7 %collective-permute-start.12 = (bf16[4,272,128]{2,1,0:T(8,128)(2,1)S(1)}, bf16[4,272,128]{2,1,0:T(8,128)(2,1)S(1)}, u32[]{:S(2)}, u32[]{:S(2)}) collective-permute-start(bf16[4,272,128]{2,1,0:T(8,128)(2,1)S(1)} %get-tuple-element.140), channel_id=1, source_target_pairs={{0,8},{8,16},{16,24},{1,9},{9,17},{17,25},{2,10},{10,18},{18,26},{... | collective-permute-start | bytes 835592 | tf_op jit(solution)/shard_map/ppermute | solution.py:533
  64.3 1.9 %shard_map.116.base_ref = f32[1024,256]{1,0:T(8,128)S(1)} custom-call(bf16[2,272,128]{2,1,0:T(8,128)(2,1)S(1)} %collective-permute-done.10.before, bf16[2,272,128]{2,1,0:T(8,128)(2,1)S(1)} %collective-permute-done.11.after, bf16[4,256,256]{2,1,0:T(8,128)(2,1)S(1)} %get-tuple-element.135.edge, bf16[4,256,256]{2,1,0:T(8,128)(2,1)S(1)} %get-tuple-element.136.inner, ...), custom_call_target="tpu_custom_call" | custom-call | flops 1610612736 | bytes 6291456 | tf_op jit(solution)/shard_map/pallas_call | solution.py:481
  66.3 0.2 collective-permute-done.13.below
  66.4 1.2 %collective-permute-done.12.above = bf16[4,272,128]{2,1,0:T(8,128)(2,1)S(1)} collective-permute-done((bf16[4,272,128]{2,1,0:T(8,128)(2,1)S(1)}, bf16[4,272,128]{2,1,0:T(8,128)(2,1)S(1)}, u32[]{:S(2)}, u32[]{:S(2)}) %collective-permute-start.12) | collective-permute-done | bytes 278560 | tf_op jit(solution)/shard_map/ppermute | solution.py:533
  67.6 2.7 %shard_map.117 = bf16[1024,256]{1,0:T(8,128)(2,1)} custom-call(bf16[2,272,128]{2,1,0:T(8,128)(2,1)S(1)} %collective-permute-done.8.above_edge, bf16[2,272,128]{2,1,0:T(8,128)(2,1)S(1)} %collective-permute-done.9.below_edge, bf16[4,272,128]{2,1,0:T(8,128)(2,1)S(1)} %collective-permute-done.12.above, bf16[4,272,128]{2,1,0:T(8,128)(2,1)S(1)} %collective-permute-done.13.below, ...), custom_call_target="tpu_custom_call" | custom-call | flops 1610612736 | bytes 6291456 | tf_op jit(solution)/shard_map/pallas_call | solution.py:481
  (20 shorter events, 0.1 us)
Async XLA Ops:
  4.8 15.1 %collective-permute-start = (bf16[1040,128]{1,0:T(8,128)(2,1)}, bf16[1040,128]{1,0:T(8,128)(2,1)S(1)}, u32[]{:S(2)}, u32[]{:S(2)}) collective-permute-start(bf16[1040,128]{1,0:T(8,128)(2,1)} %get-tuple-element.101), channel_id=1, source_target_pairs={{0,1},{1,0},{2,3},{3,2},{4,5},{5,4},{6,7},{7,6},{8,9},{9,8},{10,11... | collective-permute-start | bytes 798728 | tf_op jit(solution)/shard_map/ppermute | solution.py:504
  6.9 13.1 %collective-permute-start.1 = (bf16[1040,128]{1,0:T(8,128)(2,1)}, bf16[1040,128]{1,0:T(8,128)(2,1)S(1)}, u32[]{:S(2)}, u32[]{:S(2)}) collective-permute-start(bf16[1040,128]{1,0:T(8,128)(2,1)} %get-tuple-element.102), channel_id=1, source_target_pairs={{0,2},{1,3},{2,0},{3,1},{4,6},{5,7},{6,4},{7,5},{8,10},{9,11},{10,... | collective-permute-start | bytes 798728 | tf_op jit(solution)/shard_map/ppermute | solution.py:504
  8.2 11.8 %collective-permute-start.2 = (bf16[1040,128]{1,0:T(8,128)(2,1)}, bf16[1040,128]{1,0:T(8,128)(2,1)S(1)}, u32[]{:S(2)}, u32[]{:S(2)}) collective-permute-start(bf16[1040,128]{1,0:T(8,128)(2,1)} %get-tuple-element.103), channel_id=1, source_target_pairs={{0,3},{1,2},{2,1},{3,0},{4,7},{5,6},{6,5},{7,4},{8,11},{9,10},{10,... | collective-permute-start | bytes 798728 | tf_op jit(solution)/shard_map/ppermute | solution.py:504
  13.5 6.4 %copy-start.5 = (bf16[1040,128]{1,0:T(8,128)(2,1)S(1)}, bf16[1040,128]{1,0:T(8,128)(2,1)}, u32[]{:S(2)}) copy-start(bf16[1040,128]{1,0:T(8,128)(2,1)} %get-tuple-element.98) | copy-start | bytes 798724
  13.5 6.5 %copy-start.2 = (bf16[1040,128]{1,0:T(8,128)(2,1)S(1)}, bf16[1040,128]{1,0:T(8,128)(2,1)}, u32[]{:S(2)}) copy-start(bf16[1040,128]{1,0:T(8,128)(2,1)} %get-tuple-element.100.refs_0_) | copy-start | bytes 798724
  13.5 9.7 %copy-start.1 = (bf16[8,128,256]{2,1,0:T(8,128)(2,1)S(1)}, bf16[8,128,256]{2,1,0:T(8,128)(2,1)}, u32[]{:S(2)}) copy-start(bf16[8,128,256]{2,1,0:T(8,128)(2,1)} %field_ref) | copy-start | bytes 1572868
  13.5 9.7 %copy-start.3 = (s32[2,8,128]{2,1,0:T(8,128)S(1)}, s32[2,8,128]{2,1,0:T(8,128)}, u32[]{:S(2)}) copy-start(s32[2,8,128]{2,1,0:T(8,128)} %stencil_ref.1) | copy-start | bytes 24580
  13.5 9.7 %copy-start.4 = (f32[2,8,128]{2,1,0:T(8,128)S(1)}, f32[2,8,128]{2,1,0:T(8,128)}, u32[]{:S(2)}) copy-start(f32[2,8,128]{2,1,0:T(8,128)} %frac_ref.1) | copy-start | bytes 24580
  13.5 16.8 %collective-permute-start.3 = (bf16[1040,128]{1,0:T(8,128)(2,1)}, bf16[1040,128]{1,0:T(8,128)(2,1)S(1)}, u32[]{:S(2)}, u32[]{:S(2)}) collective-permute-start(bf16[1040,128]{1,0:T(8,128)(2,1)} %get-tuple-element.96), channel_id=1, source_target_pairs={{0,1},{1,0},{2,3},{3,2},{4,5},{5,4},{6,7},{7,6},{8,9},{9,8},{10,11... | collective-permute-start | bytes 798728 | tf_op jit(solution)/shard_map/ppermute | solution.py:504
  14.9 16.2 %collective-permute-start.4 = (bf16[1040,128]{1,0:T(8,128)(2,1)}, bf16[1040,128]{1,0:T(8,128)(2,1)S(1)}, u32[]{:S(2)}, u32[]{:S(2)}) collective-permute-start(bf16[1040,128]{1,0:T(8,128)(2,1)} %get-tuple-element.97), channel_id=1, source_target_pairs={{0,2},{1,3},{2,0},{3,1},{4,6},{5,7},{6,4},{7,5},{8,10},{9,11},{10,... | collective-permute-start | bytes 798728 | tf_op jit(solution)/shard_map/ppermute | solution.py:504
  19.9 17.1 %collective-permute-start.5 = (bf16[1040,128]{1,0:T(8,128)(2,1)S(1)}, bf16[1040,128]{1,0:T(8,128)(2,1)S(1)}, u32[]{:S(2)}, u32[]{:S(2)}) collective-permute-start(bf16[1040,128]{1,0:T(8,128)(2,1)S(1)} %copy-done.5), channel_id=1, source_target_pairs={{0,3},{1,2},{2,1},{3,0},{4,7},{5,6},{6,5},{7,4},{8,11},{9,10},{10,... | collective-permute-start | bytes 798728 | tf_op jit(solution)/shard_map/ppermute | solution.py:504
  20.6 17.7 %collective-permute-start.7 = (bf16[1040,128]{1,0:T(8,128)(2,1)S(1)}, bf16[1040,128]{1,0:T(8,128)(2,1)S(1)}, u32[]{:S(2)}, u32[]{:S(2)}) collective-permute-start(bf16[1040,128]{1,0:T(8,128)(2,1)S(1)} %get-tuple-element.122), channel_id=1, source_target_pairs={{0,4},{1,5},{2,6},{3,7},{4,0},{5,1},{6,2},{7,3},{8,12},{9,13},{10,... | collective-permute-start | bytes 798728 | tf_op jit(solution)/shard_map/ppermute | solution.py:504
  23.2 1.0 %copy-start = (bf16[1040,128]{1,0:T(8,128)(2,1)S(1)}, bf16[1040,128]{1,0:T(8,128)(2,1)}, u32[]{:S(2)}) copy-start(bf16[1040,128]{1,0:T(8,128)(2,1)} %shard_map.111.kept_in) | copy-start | bytes 798724
  37.0 16.4 %collective-permute-start.6 = (bf16[1040,128]{1,0:T(8,128)(2,1)S(1)}, bf16[1040,128]{1,0:T(8,128)(2,1)S(1)}, u32[]{:S(2)}, u32[]{:S(2)}) collective-permute-start(bf16[1040,128]{1,0:T(8,128)(2,1)S(1)} %get-tuple-element.117), channel_id=1, source_target_pairs={{0,4},{1,5},{2,6},{3,7},{4,0},{5,1},{6,2},{7,3},{8,12},{9,13},{10,... | collective-permute-start | bytes 798728 | tf_op jit(solution)/shard_map/ppermute | solution.py:504
  42.1 11.3 %collective-permute-start.8 = (bf16[2,272,128]{2,1,0:T(8,128)(2,1)S(1)}, bf16[2,272,128]{2,1,0:T(8,128)(2,1)S(1)}, u32[]{:S(2)}, u32[]{:S(2)}) collective-permute-start(bf16[2,272,128]{2,1,0:T(8,128)(2,1)S(1)} %get-tuple-element.123), channel_id=1, source_target_pairs={{0,8},{8,16},{16,24},{1,9},{9,17},{17,25},{2,10},{10,18},{18,26},{... | collective-permute-start | bytes 417800 | tf_op jit(solution)/shard_map/ppermute | solution.py:528
  47.3 6.7 %collective-permute-start.9 = (bf16[2,272,128]{2,1,0:T(8,128)(2,1)S(1)}, bf16[2,272,128]{2,1,0:T(8,128)(2,1)S(1)}, u32[]{:S(2)}, u32[]{:S(2)}) collective-permute-start(bf16[2,272,128]{2,1,0:T(8,128)(2,1)S(1)} %get-tuple-element.124), channel_id=1, source_target_pairs={{8,0},{16,8},{24,16},{9,1},{17,9},{25,17},{10,2},{18,10},{26,18},{... | collective-permute-start | bytes 417800 | tf_op jit(solution)/shard_map/ppermute | solution.py:529
  49.2 8.2 %collective-permute-start.10 = (bf16[2,272,128]{2,1,0:T(8,128)(2,1)S(1)}, bf16[2,272,128]{2,1,0:T(8,128)(2,1)S(1)}, u32[]{:S(2)}, u32[]{:S(2)}) collective-permute-start(bf16[2,272,128]{2,1,0:T(8,128)(2,1)S(1)} %get-tuple-element.131), channel_id=1, source_target_pairs={{0,1},{1,2},{2,3},{3,4},{4,5},{5,6},{6,7},{7,0},{8,9},{9,10},{10,1... | collective-permute-start | bytes 417800 | tf_op jit(solution)/shard_map/ppermute | solution.py:526
  49.5 8.1 %collective-permute-start.11 = (bf16[2,272,128]{2,1,0:T(8,128)(2,1)S(1)}, bf16[2,272,128]{2,1,0:T(8,128)(2,1)S(1)}, u32[]{:S(2)}, u32[]{:S(2)}) collective-permute-start(bf16[2,272,128]{2,1,0:T(8,128)(2,1)S(1)} %get-tuple-element.132), channel_id=1, source_target_pairs={{1,0},{2,1},{3,2},{4,3},{5,4},{6,5},{7,6},{0,7},{9,8},{10,9},{11,1... | collective-permute-start | bytes 417800 | tf_op jit(solution)/shard_map/ppermute | solution.py:527
  57.7 8.7 %collective-permute-start.13 = (bf16[4,272,128]{2,1,0:T(8,128)(2,1)S(1)}, bf16[4,272,128]{2,1,0:T(8,128)(2,1)S(1)}, u32[]{:S(2)}, u32[]{:S(2)}) collective-permute-start(bf16[4,272,128]{2,1,0:T(8,128)(2,1)S(1)} %get-tuple-element.139), channel_id=1, source_target_pairs={{8,0},{16,8},{24,16},{9,1},{17,9},{25,17},{10,2},{18,10},{26,18},{... | collective-permute-start | bytes 835592 | tf_op jit(solution)/shard_map/ppermute | solution.py:534
  59.6 8.0 %collective-permute-start.12 = (bf16[4,272,128]{2,1,0:T(8,128)(2,1)S(1)}, bf16[4,272,128]{2,1,0:T(8,128)(2,1)S(1)}, u32[]{:S(2)}, u32[]{:S(2)}) collective-permute-start(bf16[4,272,128]{2,1,0:T(8,128)(2,1)S(1)} %get-tuple-element.140), channel_id=1, source_target_pairs={{0,8},{8,16},{16,24},{1,9},{9,17},{17,25},{2,10},{10,18},{18,26},{... | collective-permute-start | bytes 835592 | tf_op jit(solution)/shard_map/ppermute | solution.py:533

commit v5 on v4

--- a/solution.py
+++ b/solution.py
@@ -309,19 +309,34 @@
             ref[where, pl.ds(MEMBERS, TILE), :] = extra.astype(BF16)
 
 
-def edge_kernel(count, *refs):
-    blocks = refs[:count]
-    far_ref, left_ref, right_ref = refs[count:count + 3]
-    rows = refs[count + 3:count + 3 + PLAT]
-    full_ref, total_ref, side_ref, w32, z32, wb, gb, zb, acc = refs[count + 3 + PLAT:]
-    sum_by_point(blocks, acc, side_ref)
-    for i, p in enumerate(INNER):
-        total_ref[i] = acc[p]
+def sum_kernel(count, *refs):
+    total_ref, side_ref = refs[count:]
+    sum_by_point(refs[:count], total_ref, side_ref)
+
+
+def near_sums(blocks):
+    count = len(blocks)
+    return pl.pallas_call(
+        functools.partial(sum_kernel, count),
+        out_shape=[
+            jax.ShapeDtypeStruct((POINTS, MEMBERS, HALF), F32),
+            jax.ShapeDtypeStruct((3, POINTS, HALF), F32),
+        ],
+        in_specs=[VMEM_SPEC] * count,
+        out_specs=[VMEM_SPEC] * 2,
+        compiler_params=params(6 + count),
+        cost_estimate=pl.CostEstimate(
+            flops=count * CAP * POINTS * TILE * MEMBERS * HALF, bytes_accessed=count * BLOCK * HALF * 8, transcendentals=0),
+    )(*blocks)
+
+
+def edge_kernel(total_in, side_in, far_ref, left_ref, right_ref, *refs):
+    rows, (full_ref, *scratch) = refs[:PLAT], refs[PLAT:]
     transform_points(
         EDGE,
-        lambda p: acc[p],
-        lambda p: [side_ref[q, pl.ds(p, 1), :] for q in range(3)],
-        far_ref, (w32, z32, wb, gb, zb), full_ref,
+        lambda p: total_in[p],
+        lambda p: [side_in[q, pl.ds(p, 1), :] for q in range(3)],
+        far_ref, scratch, full_ref,
         lambda p: [
             (left_ref if p % PLON == 0 else right_ref, p // PLON), (rows[p // PLON], 0 if p % PLON == 0 else 1)])
 
@@ -330,7 +345,7 @@
     rows, scratch = refs[:PLAT], refs[PLAT:]
     transform_points(
         INNER,
-        lambda p: total_in[INNER.index(p)],
+        lambda p: total_in[p],
         lambda p: [side_in[q, pl.ds(p, 1), :] for q in range(3)],
         far_ref, scratch, full_ref,
         lambda p: [(rows[p // PLON], p % PLON)])
@@ -341,28 +356,24 @@
     return [pltpu.VMEM(shape, F32)] * 2 + [pltpu.VMEM(shape, BF16)] * 3
 
 
-def edge_transforms(blocks, far):
+def edge_transforms(total, side, far):
+    count = len(EDGE)
     columns = jax.ShapeDtypeStruct((PLAT, PACKED, HALF), BF16)
-    return pl.pallas_call(
-        functools.partial(edge_kernel, len(blocks)),
-        out_shape=[
-            columns, columns,
-            *[jax.ShapeDtypeStruct((2, PACKED, HALF), BF16)] * PLAT,
-            jax.ShapeDtypeStruct((len(EDGE), MEMBERS, MEMBERS), BF16),
-            jax.ShapeDtypeStruct((len(INNER), MEMBERS, HALF), F32),
-            jax.ShapeDtypeStruct((3, POINTS, HALF), F32),
-        ],
-        in_specs=[VMEM_SPEC] * (len(blocks) + 1),
-        out_specs=[VMEM_SPEC] * (5 + PLAT),
-        scratch_shapes=newton_scratch(len(EDGE)) + [pltpu.VMEM((POINTS, MEMBERS, HALF), F32)],
-        compiler_params=params(12 + len(blocks)),
-        cost_estimate=pl.CostEstimate(
-            flops=len(EDGE) * 15 * 2 * MEMBERS ** 3, bytes_accessed=8 * MEMBERS * HALF * 6, transcendentals=0),
-    )(*blocks, far)
+    row = jax.ShapeDtypeStruct((2, PACKED, HALF), BF16)
+    return pl.pallas_call(
+        edge_kernel,
+        out_shape=[columns, columns] + [row] * PLAT + [jax.ShapeDtypeStruct((count, MEMBERS, MEMBERS), BF16)],
+        in_specs=[VMEM_SPEC] * 3,
+        out_specs=[VMEM_SPEC] * (3 + PLAT),
+        scratch_shapes=newton_scratch(count),
+        compiler_params=params(12),
+        cost_estimate=pl.CostEstimate(
+            flops=count * 15 * 2 * MEMBERS ** 3, bytes_accessed=count * MEMBERS * HALF * 6, transcendentals=0),
+    )(total, side, far)
 
 
 def inner_transforms(total, side, far):
-    count = total.shape[0]
+    count = len(INNER)
     row = jax.ShapeDtypeStruct((PLON, PACKED, HALF), BF16)
     return pl.pallas_call(
         inner_kernel,
@@ -504,9 +515,9 @@
         return lax.ppermute(value, "lon", [(i, i ^ offset) for i in range(lon_size)])
 
     far = batch_blocks(57, half + 1, half - 1, lon_size, *fixed)
-    relayed = [swap(far[i - 1], i) for i in range(1, half)]
+    relayed = [swap(far[i - 1], i) for i in range(half - 1, 0, -1)]
     *near, own_far = batch_blocks(57, 1, half, lon_size, *fixed)
-    got = [swap(near[i - 1], i) for i in range(1, half)]
+    got = [swap(near[i - 1], i) for i in range(half - 1, 0, -1)]
     obs_pert, near, own_far = lax.optimization_barrier((obs_pert, near, own_far))
     own_near, = batch_blocks(57, 0, 1, lon_size, *fixed[:-1], obs_pert)
     relayed, own_near = lax.optimization_barrier((relayed, own_near))
@@ -515,10 +526,11 @@
     mid_lhs, rim_lhs, mean, own_near = cell_parts(PLON * lon_size, pos, stencil, frac, background, own_near)
     got = [own_near] + got
     far_edge = swap(far_edge, half)
-    far_inner, got, mid_lhs, rim_lhs, mean = lax.optimization_barrier((far_inner, got, mid_lhs, rim_lhs, mean))
+    far_inner, mid_lhs, rim_lhs, mean = lax.optimization_barrier((far_inner, mid_lhs, rim_lhs, mean))
     far_inner = swap(far_inner, half)
 
-    left, right, *edge_rows, edge, total, side = edge_transforms(got, far_edge)
+    total, side = near_sums(got)
+    left, right, *edge_rows, edge = edge_transforms(total, side, far_edge)
     up = [(i, (i + 1) % lon_size) for i in range(lon_size)]
     down = [(j, i) for i, j in up]
     north = [(i, i + 1) for i in range(lat_size - 1)]

time: 70.8 us -> 69.8 us (0.986)
  starting transfers between devices: 27.9 us -> 26.5 us
    ppermute x1, starting transfers between devices: 0.31 us -> 1.67 us  [on_device(): before = lax.ppermute(right, 'lon', up)]
    ppermute x8, starting transfers between devices: 9.97 us -> 8.86 us  [swap(): lax.ppermute(value, 'lon', [(i, i ^ offset) for i in range(lon_size)])]
    ppermute x1, starting transfers between devices: 3.91 us -> 3.11 us  [on_device(): after = lax.ppermute(left, 'lon', down)]
    ppermute x1, starting transfers between devices: 5.16 us -> 4.39 us  [on_device(): above_edge = lax.ppermute(edge_rows[PLAT - 1], 'lat', north)]
    pallas_call x1 -> x2, Pallas kernels: 3.82 us -> 4.12 us  [the longest x1 3.47 us: edge_transforms(): pl.pallas_call(edge_kernel, out_shape=[columns, columns] + [row] * PLAT +...]
where the time goes in v5:
time: 69.8 us; the launch traced here: 69.4 us
  Pallas kernels  32.7 us (47%)
  starting transfers between devices  26.5 us (38%)
  waiting for transfers between devices  8.79 us (13%)
  local copies, waits for them, and re-layouts  1.02 us (1%)
    pallas_call x3, Pallas kernels, batch_blocks(): pl.pallas_call(functools.partial(gram_kernel, first, count, lon_size), ou...  13.6 us
    ppermute x8, starting transfers between devices, swap(): lax.ppermute(value, 'lon', [(i, i ^ offset) for i in range(lon_size)])  8.86 us
    ppermute x8, waiting for transfers between devices, swap(): lax.ppermute(value, 'lon', [(i, i ^ offset) for i in range(lon_size)])  6.68 us
    pallas_call x1, Pallas kernels, cell_parts(): pl.pallas_call(functools.partial(cell_kernel, point_cols), grid=(rows,),...  6.19 us
    pallas_call x2, Pallas kernels, mix(): pl.pallas_call(kernel, out_shape=jax.ShapeDtypeStruct((cells, MEMBERS), d...  4.68 us
    ppermute x1, starting transfers between devices, on_device(): above = lax.ppermute(rows[PLAT - 1], 'lat', north)  4.57 us
    ppermute x1, starting transfers between devices, on_device(): above_edge = lax.ppermute(edge_rows[PLAT - 1], 'lat', north)  4.39 us
    pallas_call x1, Pallas kernels, inner_transforms(): pl.pallas_call(inner_kernel, out_shape=[jax.ShapeDtypeStruct((count, MEMB...  3.47 us
  transfers between devices with their start and end apart: 14, of which 6 were waited for; matrix products, arithmetic and copies ran while one was open for 0% of the time, Pallas kernels for 36%

profile of v5, /device:TPU:1, one launch (start us, length us, event | category | flops | bytes accessed | tf_op | source)
XLA Modules:
  0.0 69.4 jit_solution(6458875727529487242)
XLA Ops:
  0.0 4.7 %shard_map.110 = (bf16[1040,128]{1,0:T(8,128)(2,1)}, bf16[1040,128]{1,0:T(8,128)(2,1)}, bf16[1040,128]{1,0:T(8,128)(2,1)}) custom-call(s32[1]{0:T(128)} %bitcast.me_ref, s32[1,32]{1,0:T(1,128)} %bitcast.12, s32[1,32]{1,0:T(1,128)} %refs_1_.5, s32[3,32]{1,0:T(4,128)} %bitcast.6, s32[32]{0:T(128)} %refs_3_.5, bf16[32,512]{1,0:T(8,128)(2,1)} %refs_4_.5, ...), custom_call_target="tpu_custom_call" | custom-call | flops 805306368 | bytes 3145728 | tf_op jit(solution)/shard_map/pallas_call | solution.py:140
  4.7 3.1 %collective-permute-start = (bf16[1040,128]{1,0:T(8,128)(2,1)}, bf16[1040,128]{1,0:T(8,128)(2,1)S(1)}, u32[]{:S(2)}, u32[]{:S(2)}) collective-permute-start(bf16[1040,128]{1,0:T(8,128)(2,1)} %get-tuple-element.97), channel_id=1, source_target_pairs={{0,3},{1,2},{2,1},{3,0},{4,7},{5,6},{6,5},{7,4},{8,11},{9,10},{10,... | collective-permute-start | bytes 798728 | tf_op jit(solution)/shard_map/ppermute | solution.py:515
  7.9 0.2 collective-permute-start.1
  8.0 0.2 collective-permute-start.2
  8.2 5.3 %shard_map.109 = (bf16[1040,128]{1,0:T(8,128)(2,1)}, bf16[1040,128]{1,0:T(8,128)(2,1)}, bf16[1040,128]{1,0:T(8,128)(2,1)}, bf16[1040,128]{1,0:T(8,128)(2,1)}) custom-call(s32[1]{0:T(128)} %bitcast.me_ref, s32[1,32]{1,0:T(1,128)} %bitcast.13, s32[1,32]{1,0:T(1,128)} %refs_1_.5, s32[3,32]{1,0:T(4,128)} %bitcast.7, s32[32]{0:T(128)} %refs_3_.5, ...), custom_call_target="tpu_custom_call" | custom-call | flops 1073741824 | bytes 4194304 | tf_op jit(solution)/shard_map/pallas_call | solution.py:140
  13.6 1.3 %collective-permute-start.6 = (bf16[1040,128]{1,0:T(8,128)(2,1)}, bf16[1040,128]{1,0:T(8,128)(2,1)S(1)}, u32[]{:S(2)}, u32[]{:S(2)}) collective-permute-start(bf16[1040,128]{1,0:T(8,128)(2,1)} %get-tuple-element.92), channel_id=1, source_target_pairs={{0,1},{1,0},{2,3},{3,2},{4,5},{5,4},{6,7},{7,6},{8,9},{9,8},{10,11... | collective-permute-start | bytes 798728 | tf_op jit(solution)/shard_map/ppermute | solution.py:515
  14.9 1.3 %collective-permute-start.5 = (bf16[1040,128]{1,0:T(8,128)(2,1)}, bf16[1040,128]{1,0:T(8,128)(2,1)S(1)}, u32[]{:S(2)}, u32[]{:S(2)}) collective-permute-start(bf16[1040,128]{1,0:T(8,128)(2,1)} %get-tuple-element.93), channel_id=1, source_target_pairs={{0,2},{1,3},{2,0},{3,1},{4,6},{5,7},{6,4},{7,5},{8,10},{9,11},{10,... | collective-permute-start | bytes 798728 | tf_op jit(solution)/shard_map/ppermute | solution.py:515
  16.2 3.6 %shard_map.111.kept_in = bf16[1040,128]{1,0:T(8,128)(2,1)} custom-call(s32[1]{0:T(128)} %bitcast.me_ref, s32[1,32]{1,0:T(1,128)} %bitcast.14, s32[1,32]{1,0:T(1,128)} %refs_1_.5, s32[3,32]{1,0:T(4,128)} %bitcast.8, s32[32]{0:T(128)} %refs_3_.5, bf16[32,512]{1,0:T(8,128)(2,1)} %refs_4_.5, bf16[32,512]{1,0:T(8,128)(2,1)} %refs_5_.5, bf16[3,32]{1,0:T(4,128)(2,1)} %bitcast.11, ...), custom_call_target="tpu_custom_call" | custom-call | flops 268435456 | bytes 1048576 | tf_op jit(solution)/shard_map/pallas_call | solution.py:140
  19.9 0.2 collective-permute-start.4
  20.0 0.6 collective-permute-done.2.refs_3_
  20.6 0.6 shard_map.112
  21.3 2.5 %collective-permute-start.7 = (bf16[1040,128]{1,0:T(8,128)(2,1)S(1)}, bf16[1040,128]{1,0:T(8,128)(2,1)S(1)}, u32[]{:S(2)}, u32[]{:S(2)}) collective-permute-start(bf16[1040,128]{1,0:T(8,128)(2,1)S(1)} %get-tuple-element.116), channel_id=1, source_target_pairs={{0,4},{1,5},{2,6},{3,7},{4,0},{5,1},{6,2},{7,3},{8,12},{9,13},{10,... | collective-permute-start | bytes 798728 | tf_op jit(solution)/shard_map/ppermute | solution.py:515
  23.8 0.1 pad_add_fusion.pos_ref
  23.9 0.9 %copy-done = bf16[1040,128]{1,0:T(8,128)(2,1)S(1)} copy-done((bf16[1040,128]{1,0:T(8,128)(2,1)S(1)}, bf16[1040,128]{1,0:T(8,128)(2,1)}, u32[]{:S(2)}) %copy-start) | copy-done | bytes 266264
  24.8 6.2 %shard_map.113 = (bf16[1024,3072]{1,0:T(8,128)(2,1)S(1)}, bf16[1024,3072]{1,0:T(8,128)(2,1)S(1)}, f32[1024,128]{1,0:T(8,128)S(1)}, bf16[1040,128]{1,0:T(8,128)(2,1)S(1)}) custom-call(s32[2]{0:T(128)S(1)} %pad_add_fusion.pos_ref, s32[2,8,128]{2,1,0:T(8,128)S(1)} %copy-done.3, f32[2,8,128]{2,1,0:T(8,128)S(1)} %copy-done.4, bf16[8,128,256]{2,1,0:T(8,128)(2,1)S(1)} %copy-done.1, ...), custom_call_target="tpu_custom_call" | custom-call | flops 6291456 | bytes 13631488 | tf_op jit(solution)/shard_map/pallas_call | solution.py:431
  31.0 0.1 collective-permute-start.3
  31.1 0.1 collective-permute-done.5.refs_2_
  31.2 6.0 %collective-permute-done.4.refs_1_ = bf16[1040,128]{1,0:T(8,128)(2,1)S(1)} collective-permute-done((bf16[1040,128]{1,0:T(8,128)(2,1)S(1)}, bf16[1040,128]{1,0:T(8,128)(2,1)S(1)}, u32[]{:S(2)}, u32[]{:S(2)}) %collective-permute-start.4) | collective-permute-done | bytes 266272 | tf_op jit(solution)/shard_map/ppermute | solution.py:515
  37.2 0.6 shard_map.114
  37.8 3.5 %shard_map.115 = (bf16[2,272,128]{2,1,0:T(8,128)(2,1)S(1)}, bf16[2,272,128]{2,1,0:T(8,128)(2,1)S(1)}, bf16[2,272,128]{2,1,0:T(8,128)(2,1)S(1)}, bf16[2,272,128]{2,1,0:T(8,128)(2,1)S(1)}, bf16[4,256,256]{2,1,0:T(8,128)(2,1)S(1)}) custom-call(f32[8,256,128]{2,1,0:T(8,128)S(1)} %get-tuple-element.114.total_in, f32[3,8,128]{2,1,0:T(8,128)S(1)} %get-tuple-element.115.side_in, ...), custom_call_target="tpu_custom_call" | custom-call | flops 2013265920 | bytes 786432 | tf_op jit(solution)/shard_map/pallas_call | solution.py:363
  41.3 4.4 %collective-permute-start.8 = (bf16[2,272,128]{2,1,0:T(8,128)(2,1)S(1)}, bf16[2,272,128]{2,1,0:T(8,128)(2,1)S(1)}, u32[]{:S(2)}, u32[]{:S(2)}) collective-permute-start(bf16[2,272,128]{2,1,0:T(8,128)(2,1)S(1)} %get-tuple-element.117), channel_id=1, source_target_pairs={{0,8},{8,16},{16,24},{1,9},{9,17},{17,25},{2,10},{10,18},{18,26},{... | collective-permute-start | bytes 417800 | tf_op jit(solution)/shard_map/ppermute | solution.py:540
  45.7 1.9 %collective-permute-start.9 = (bf16[2,272,128]{2,1,0:T(8,128)(2,1)S(1)}, bf16[2,272,128]{2,1,0:T(8,128)(2,1)S(1)}, u32[]{:S(2)}, u32[]{:S(2)}) collective-permute-start(bf16[2,272,128]{2,1,0:T(8,128)(2,1)S(1)} %get-tuple-element.118), channel_id=1, source_target_pairs={{8,0},{16,8},{24,16},{9,1},{17,9},{25,17},{10,2},{18,10},{26,18},{... | collective-permute-start | bytes 417800 | tf_op jit(solution)/shard_map/ppermute | solution.py:541
  47.6 1.7 %collective-permute-start.10 = (bf16[2,272,128]{2,1,0:T(8,128)(2,1)S(1)}, bf16[2,272,128]{2,1,0:T(8,128)(2,1)S(1)}, u32[]{:S(2)}, u32[]{:S(2)}) collective-permute-start(bf16[2,272,128]{2,1,0:T(8,128)(2,1)S(1)} %get-tuple-element.123), channel_id=1, source_target_pairs={{0,1},{1,2},{2,3},{3,4},{4,5},{5,6},{6,7},{7,0},{8,9},{9,10},{10,1... | collective-permute-start | bytes 417800 | tf_op jit(solution)/shard_map/ppermute | solution.py:538
  49.3 3.1 %collective-permute-start.11 = (bf16[2,272,128]{2,1,0:T(8,128)(2,1)S(1)}, bf16[2,272,128]{2,1,0:T(8,128)(2,1)S(1)}, u32[]{:S(2)}, u32[]{:S(2)}) collective-permute-start(bf16[2,272,128]{2,1,0:T(8,128)(2,1)S(1)} %get-tuple-element.124), channel_id=1, source_target_pairs={{1,0},{2,1},{3,2},{4,3},{5,4},{6,5},{7,6},{0,7},{9,8},{10,9},{11,1... | collective-permute-start | bytes 417800 | tf_op jit(solution)/shard_map/ppermute | solution.py:539
  52.4 3.5 %shard_map.116 = (bf16[4,256,256]{2,1,0:T(8,128)(2,1)S(1)}, bf16[4,272,128]{2,1,0:T(8,128)(2,1)S(1)}, bf16[4,272,128]{2,1,0:T(8,128)(2,1)S(1)}) custom-call(f32[8,256,128]{2,1,0:T(8,128)S(1)} %get-tuple-element.114.total_in, f32[3,8,128]{2,1,0:T(8,128)S(1)} %get-tuple-element.115.side_in, bf16[1040,128]{1,0:T(8,128)(2,1)S(1)} %collective-permute-done.3.far_ref), custom_call_target="tpu_custom_call" | custom-call | flops 2013265920 | bytes 786432 | tf_op jit(solution)/shard_map/pallas_call | solution.py:378
  55.9 0.8 %collective-permute-done.11.after = bf16[2,272,128]{2,1,0:T(8,128)(2,1)S(1)} collective-permute-done((bf16[2,272,128]{2,1,0:T(8,128)(2,1)S(1)}, bf16[2,272,128]{2,1,0:T(8,128)(2,1)S(1)}, u32[]{:S(2)}, u32[]{:S(2)}) %collective-permute-start.11) | collective-permute-done | bytes 139296 | tf_op jit(solution)/shard_map/ppermute | solution.py:539
  56.7 2.0 %collective-permute-start.13 = (bf16[4,272,128]{2,1,0:T(8,128)(2,1)S(1)}, bf16[4,272,128]{2,1,0:T(8,128)(2,1)S(1)}, u32[]{:S(2)}, u32[]{:S(2)}) collective-permute-start(bf16[4,272,128]{2,1,0:T(8,128)(2,1)S(1)} %get-tuple-element.131), channel_id=1, source_target_pairs={{8,0},{16,8},{24,16},{9,1},{17,9},{25,17},{10,2},{18,10},{26,18},{... | collective-permute-start | bytes 835592 | tf_op jit(solution)/shard_map/ppermute | solution.py:546
  58.8 4.6 %collective-permute-start.12 = (bf16[4,272,128]{2,1,0:T(8,128)(2,1)S(1)}, bf16[4,272,128]{2,1,0:T(8,128)(2,1)S(1)}, u32[]{:S(2)}, u32[]{:S(2)}) collective-permute-start(bf16[4,272,128]{2,1,0:T(8,128)(2,1)S(1)} %get-tuple-element.132), channel_id=1, source_target_pairs={{0,8},{8,16},{16,24},{1,9},{9,17},{17,25},{2,10},{10,18},{18,26},{... | collective-permute-start | bytes 835592 | tf_op jit(solution)/shard_map/ppermute | solution.py:545
  63.3 1.9 %shard_map.117.base_ref = f32[1024,256]{1,0:T(8,128)S(1)} custom-call(bf16[2,272,128]{2,1,0:T(8,128)(2,1)S(1)} %collective-permute-done.10.before, bf16[2,272,128]{2,1,0:T(8,128)(2,1)S(1)} %collective-permute-done.11.after, bf16[4,256,256]{2,1,0:T(8,128)(2,1)S(1)} %get-tuple-element.127.edge, bf16[4,256,256]{2,1,0:T(8,128)(2,1)S(1)} %get-tuple-element.128.inner, ...), custom_call_target="tpu_custom_call" | custom-call | flops 1610612736 | bytes 6291456 | tf_op jit(solution)/shard_map/pallas_call | solution.py:492
  65.3 0.2 collective-permute-done.13.below
  65.4 1.2 %collective-permute-done.12.above = bf16[4,272,128]{2,1,0:T(8,128)(2,1)S(1)} collective-permute-done((bf16[4,272,128]{2,1,0:T(8,128)(2,1)S(1)}, bf16[4,272,128]{2,1,0:T(8,128)(2,1)S(1)}, u32[]{:S(2)}, u32[]{:S(2)}) %collective-permute-start.12) | collective-permute-done | bytes 278560 | tf_op jit(solution)/shard_map/ppermute | solution.py:545
  66.6 2.7 %shard_map.118 = bf16[1024,256]{1,0:T(8,128)(2,1)} custom-call(bf16[2,272,128]{2,1,0:T(8,128)(2,1)S(1)} %collective-permute-done.8.above_edge, bf16[2,272,128]{2,1,0:T(8,128)(2,1)S(1)} %collective-permute-done.9.below_edge, bf16[4,272,128]{2,1,0:T(8,128)(2,1)S(1)} %collective-permute-done.12.above, bf16[4,272,128]{2,1,0:T(8,128)(2,1)S(1)} %collective-permute-done.13.below, ...), custom_call_target="tpu_custom_call" | custom-call | flops 1610612736 | bytes 6291456 | tf_op jit(solution)/shard_map/pallas_call | solution.py:492
  (21 shorter events, 0.1 us)
Async XLA Ops:
  4.7 15.1 %collective-permute-start = (bf16[1040,128]{1,0:T(8,128)(2,1)}, bf16[1040,128]{1,0:T(8,128)(2,1)S(1)}, u32[]{:S(2)}, u32[]{:S(2)}) collective-permute-start(bf16[1040,128]{1,0:T(8,128)(2,1)} %get-tuple-element.97), channel_id=1, source_target_pairs={{0,3},{1,2},{2,1},{3,0},{4,7},{5,6},{6,5},{7,4},{8,11},{9,10},{10,... | collective-permute-start | bytes 798728 | tf_op jit(solution)/shard_map/ppermute | solution.py:515
  7.9 12.1 %collective-permute-start.1 = (bf16[1040,128]{1,0:T(8,128)(2,1)}, bf16[1040,128]{1,0:T(8,128)(2,1)S(1)}, u32[]{:S(2)}, u32[]{:S(2)}) collective-permute-start(bf16[1040,128]{1,0:T(8,128)(2,1)} %get-tuple-element.98), channel_id=1, source_target_pairs={{0,2},{1,3},{2,0},{3,1},{4,6},{5,7},{6,4},{7,5},{8,10},{9,11},{10,... | collective-permute-start | bytes 798728 | tf_op jit(solution)/shard_map/ppermute | solution.py:515
  8.0 12.6 %collective-permute-start.2 = (bf16[1040,128]{1,0:T(8,128)(2,1)}, bf16[1040,128]{1,0:T(8,128)(2,1)S(1)}, u32[]{:S(2)}, u32[]{:S(2)}) collective-permute-start(bf16[1040,128]{1,0:T(8,128)(2,1)} %get-tuple-element.99), channel_id=1, source_target_pairs={{0,1},{1,0},{2,3},{3,2},{4,5},{5,4},{6,7},{7,6},{8,9},{9,8},{10,11... | collective-permute-start | bytes 798728 | tf_op jit(solution)/shard_map/ppermute | solution.py:515
  13.5 6.3 %copy-start.5 = (bf16[1040,128]{1,0:T(8,128)(2,1)S(1)}, bf16[1040,128]{1,0:T(8,128)(2,1)}, u32[]{:S(2)}) copy-start(bf16[1040,128]{1,0:T(8,128)(2,1)} %get-tuple-element.94) | copy-start | bytes 798724
  13.5 7.1 %copy-start.2 = (bf16[1040,128]{1,0:T(8,128)(2,1)S(1)}, bf16[1040,128]{1,0:T(8,128)(2,1)}, u32[]{:S(2)}) copy-start(bf16[1040,128]{1,0:T(8,128)(2,1)} %get-tuple-element.96.refs_0_) | copy-start | bytes 798724
  13.5 10.3 %copy-start.1 = (bf16[8,128,256]{2,1,0:T(8,128)(2,1)S(1)}, bf16[8,128,256]{2,1,0:T(8,128)(2,1)}, u32[]{:S(2)}) copy-start(bf16[8,128,256]{2,1,0:T(8,128)(2,1)} %field_ref) | copy-start | bytes 1572868
  13.6 10.3 %copy-start.3 = (s32[2,8,128]{2,1,0:T(8,128)S(1)}, s32[2,8,128]{2,1,0:T(8,128)}, u32[]{:S(2)}) copy-start(s32[2,8,128]{2,1,0:T(8,128)} %stencil_ref.1) | copy-start | bytes 24580
  13.6 10.3 %copy-start.4 = (f32[2,8,128]{2,1,0:T(8,128)S(1)}, f32[2,8,128]{2,1,0:T(8,128)}, u32[]{:S(2)}) copy-start(f32[2,8,128]{2,1,0:T(8,128)} %frac_ref.1) | copy-start | bytes 24580
  13.6 17.5 %collective-permute-start.6 = (bf16[1040,128]{1,0:T(8,128)(2,1)}, bf16[1040,128]{1,0:T(8,128)(2,1)S(1)}, u32[]{:S(2)}, u32[]{:S(2)}) collective-permute-start(bf16[1040,128]{1,0:T(8,128)(2,1)} %get-tuple-element.92), channel_id=1, source_target_pairs={{0,1},{1,0},{2,3},{3,2},{4,5},{5,4},{6,7},{7,6},{8,9},{9,8},{10,11... | collective-permute-start | bytes 798728 | tf_op jit(solution)/shard_map/ppermute | solution.py:515
  14.9 16.3 %collective-permute-start.5 = (bf16[1040,128]{1,0:T(8,128)(2,1)}, bf16[1040,128]{1,0:T(8,128)(2,1)S(1)}, u32[]{:S(2)}, u32[]{:S(2)}) collective-permute-start(bf16[1040,128]{1,0:T(8,128)(2,1)} %get-tuple-element.93), channel_id=1, source_target_pairs={{0,2},{1,3},{2,0},{3,1},{4,6},{5,7},{6,4},{7,5},{8,10},{9,11},{10,... | collective-permute-start | bytes 798728 | tf_op jit(solution)/shard_map/ppermute | solution.py:515
  19.9 17.3 %collective-permute-start.4 = (bf16[1040,128]{1,0:T(8,128)(2,1)S(1)}, bf16[1040,128]{1,0:T(8,128)(2,1)S(1)}, u32[]{:S(2)}, u32[]{:S(2)}) collective-permute-start(bf16[1040,128]{1,0:T(8,128)(2,1)S(1)} %copy-done.5), channel_id=1, source_target_pairs={{0,3},{1,2},{2,1},{3,0},{4,7},{5,6},{6,5},{7,4},{8,11},{9,10},{10,... | collective-permute-start | bytes 798728 | tf_op jit(solution)/shard_map/ppermute | solution.py:515
  21.3 16.5 %collective-permute-start.7 = (bf16[1040,128]{1,0:T(8,128)(2,1)S(1)}, bf16[1040,128]{1,0:T(8,128)(2,1)S(1)}, u32[]{:S(2)}, u32[]{:S(2)}) collective-permute-start(bf16[1040,128]{1,0:T(8,128)(2,1)S(1)} %get-tuple-element.116), channel_id=1, source_target_pairs={{0,4},{1,5},{2,6},{3,7},{4,0},{5,1},{6,2},{7,3},{8,12},{9,13},{10,... | collective-permute-start | bytes 798728 | tf_op jit(solution)/shard_map/ppermute | solution.py:515
  23.9 1.0 %copy-start = (bf16[1040,128]{1,0:T(8,128)(2,1)S(1)}, bf16[1040,128]{1,0:T(8,128)(2,1)}, u32[]{:S(2)}) copy-start(bf16[1040,128]{1,0:T(8,128)(2,1)} %shard_map.111.kept_in) | copy-start | bytes 798724
  31.0 21.4 %collective-permute-start.3 = (bf16[1040,128]{1,0:T(8,128)(2,1)S(1)}, bf16[1040,128]{1,0:T(8,128)(2,1)S(1)}, u32[]{:S(2)}, u32[]{:S(2)}) collective-permute-start(bf16[1040,128]{1,0:T(8,128)(2,1)S(1)} %get-tuple-element.112), channel_id=1, source_target_pairs={{0,4},{1,5},{2,6},{3,7},{4,0},{5,1},{6,2},{7,3},{8,12},{9,13},{10,... | collective-permute-start | bytes 798728 | tf_op jit(solution)/shard_map/ppermute | solution.py:515
  41.3 11.1 %collective-permute-start.8 = (bf16[2,272,128]{2,1,0:T(8,128)(2,1)S(1)}, bf16[2,272,128]{2,1,0:T(8,128)(2,1)S(1)}, u32[]{:S(2)}, u32[]{:S(2)}) collective-permute-start(bf16[2,272,128]{2,1,0:T(8,128)(2,1)S(1)} %get-tuple-element.117), channel_id=1, source_target_pairs={{0,8},{8,16},{16,24},{1,9},{9,17},{17,25},{2,10},{10,18},{18,26},{... | collective-permute-start | bytes 417800 | tf_op jit(solution)/shard_map/ppermute | solution.py:540
  45.7 6.7 %collective-permute-start.9 = (bf16[2,272,128]{2,1,0:T(8,128)(2,1)S(1)}, bf16[2,272,128]{2,1,0:T(8,128)(2,1)S(1)}, u32[]{:S(2)}, u32[]{:S(2)}) collective-permute-start(bf16[2,272,128]{2,1,0:T(8,128)(2,1)S(1)} %get-tuple-element.118), channel_id=1, source_target_pairs={{8,0},{16,8},{24,16},{9,1},{17,9},{25,17},{10,2},{18,10},{26,18},{... | collective-permute-start | bytes 417800 | tf_op jit(solution)/shard_map/ppermute | solution.py:541
  47.6 8.3 %collective-permute-start.10 = (bf16[2,272,128]{2,1,0:T(8,128)(2,1)S(1)}, bf16[2,272,128]{2,1,0:T(8,128)(2,1)S(1)}, u32[]{:S(2)}, u32[]{:S(2)}) collective-permute-start(bf16[2,272,128]{2,1,0:T(8,128)(2,1)S(1)} %get-tuple-element.123), channel_id=1, source_target_pairs={{0,1},{1,2},{2,3},{3,4},{4,5},{5,6},{6,7},{7,0},{8,9},{9,10},{10,1... | collective-permute-start | bytes 417800 | tf_op jit(solution)/shard_map/ppermute | solution.py:538
  49.3 7.4 %collective-permute-start.11 = (bf16[2,272,128]{2,1,0:T(8,128)(2,1)S(1)}, bf16[2,272,128]{2,1,0:T(8,128)(2,1)S(1)}, u32[]{:S(2)}, u32[]{:S(2)}) collective-permute-start(bf16[2,272,128]{2,1,0:T(8,128)(2,1)S(1)} %get-tuple-element.124), channel_id=1, source_target_pairs={{1,0},{2,1},{3,2},{4,3},{5,4},{6,5},{7,6},{0,7},{9,8},{10,9},{11,1... | collective-permute-start | bytes 417800 | tf_op jit(solution)/shard_map/ppermute | solution.py:539
  56.7 8.7 %collective-permute-start.13 = (bf16[4,272,128]{2,1,0:T(8,128)(2,1)S(1)}, bf16[4,272,128]{2,1,0:T(8,128)(2,1)S(1)}, u32[]{:S(2)}, u32[]{:S(2)}) collective-permute-start(bf16[4,272,128]{2,1,0:T(8,128)(2,1)S(1)} %get-tuple-element.131), channel_id=1, source_target_pairs={{8,0},{16,8},{24,16},{9,1},{17,9},{25,17},{10,2},{18,10},{26,18},{... | collective-permute-start | bytes 835592 | tf_op jit(solution)/shard_map/ppermute | solution.py:546
  58.8 7.9 %collective-permute-start.12 = (bf16[4,272,128]{2,1,0:T(8,128)(2,1)S(1)}, bf16[4,272,128]{2,1,0:T(8,128)(2,1)S(1)}, u32[]{:S(2)}, u32[]{:S(2)}) collective-permute-start(bf16[4,272,128]{2,1,0:T(8,128)(2,1)S(1)} %get-tuple-element.132), channel_id=1, source_target_pairs={{0,8},{8,16},{16,24},{1,9},{9,17},{17,25},{2,10},{10,18},{18,26},{... | collective-permute-start | bytes 835592 | tf_op jit(solution)/shard_map/ppermute | solution.py:545

commit v6 on v5

--- a/solution.py
+++ b/solution.py
@@ -389,11 +389,21 @@
 
 WIDE = PLON + 2
 WINDOW = (PLAT + 2) * WIDE
-MID = list(range(WIDE, WINDOW - WIDE))
-RIM = list(range(WIDE)) + list(range(WINDOW - WIDE, WINDOW))
-
-
-def cell_kernel(point_cols, pos_ref, stencil_ref, frac_ref, field_ref, kept_in, mid_ref, rim_ref, mean_ref,
+
+
+def window_id(row, column):
+    return (row + 1) * WIDE + column + 1
+
+
+ENDS = (0, PLON - 1)
+REST = [-1] + list(range(1, PLON - 1)) + [PLON]
+OWN = [window_id(r, c) for r in range(PLAT) for c in range(PLON)]
+SIDE = [window_id(r, c) for c in (-1, PLON) for r in range(PLAT)] + [
+    window_id(r, c) for r in (-1, PLAT) for c in ENDS]
+RIM = [window_id(r, c) for r in (-1, PLAT) for c in REST]
+
+
+def cell_kernel(point_cols, pos_ref, stencil_ref, frac_ref, field_ref, kept_in, own_ref, edge_ref, rim_ref, mean_ref,
                 kept_out):
     width = stencil_ref.shape[2]
     lat_pos, lon_pos = pos_ref[0], pos_ref[1]
@@ -420,7 +430,7 @@
     weights = weights + jnp.where(corner + 1 == ids, (1.0 - y) * x, 0.0)
     weights = weights + jnp.where(corner + WIDE + 1 == ids, y * x, 0.0)
     turned = weights.T
-    for ref, listed in ((mid_ref, MID), (rim_ref, RIM)):
+    for ref, listed in ((own_ref, OWN), (edge_ref, SIDE), (rim_ref, RIM)):
         for n, point in enumerate(listed):
             ref[:, n * MEMBERS:(n + 1) * MEMBERS] = (dev * turned[:, point:point + 1]).astype(BF16)
 
@@ -432,7 +442,8 @@
         functools.partial(cell_kernel, point_cols),
         grid=(rows,),
         out_shape=[
-            jax.ShapeDtypeStruct((cells, len(MID) * members), BF16),
+            jax.ShapeDtypeStruct((cells, len(OWN) * members), BF16),
+            jax.ShapeDtypeStruct((cells, len(SIDE) * members), BF16),
             jax.ShapeDtypeStruct((cells, len(RIM) * members), BF16),
             jax.ShapeDtypeStruct((cells, HALF), F32),
             jax.ShapeDtypeStruct(kept.shape, kept.dtype),
@@ -445,7 +456,8 @@
             pl.BlockSpec(kept.shape, lambda i: (0, 0)),
         ],
         out_specs=[
-            pl.BlockSpec((width, len(MID) * members), lambda i: (i, 0)),
+            pl.BlockSpec((width, len(OWN) * members), lambda i: (i, 0)),
+            pl.BlockSpec((width, len(SIDE) * members), lambda i: (i, 0)),
             pl.BlockSpec((width, len(RIM) * members), lambda i: (i, 0)),
             pl.BlockSpec((width, HALF), lambda i: (i, 0)),
             pl.BlockSpec(kept.shape, lambda i: (0, 0)),
@@ -465,25 +477,24 @@
     matrices[pl.ds(slot * MEMBERS, MEMBERS), :] = full.astype(BF16)
 
 
-def mid_kernel(before, after, edge, inner, lhs_ref, mean_ref, out_ref, matrices):
-    for r in range(PLAT):
-        place_packed(matrices, r * WIDE, before, r)
-        place_packed(matrices, r * WIDE + PLON + 1, after, r)
-        for c in range(PLON):
-            p = r * PLON + c
-            value = edge[EDGE.index(p)] if p in EDGE else inner[INNER.index(p)]
-            matrices[pl.ds((r * WIDE + c + 1) * MEMBERS, MEMBERS), :] = value
-
+def own_kernel(edge, inner, lhs_ref, mean_ref, out_ref, matrices):
+    for p in range(POINTS):
+        value = edge[EDGE.index(p)] if p in EDGE else inner[INNER.index(p)]
+        matrices[pl.ds(p * MEMBERS, MEMBERS), :] = value
     out_ref[...] = dot_nn(lhs_ref[...], matrices[...]) + mean_ref[:, 0:1]
 
 
-def rim_kernel(above_edge, below_edge, above, below, lhs_ref, base_ref, out_ref, matrices):
-    for row, edge, rest in ((0, above_edge, above), (1, below_edge, below)):
-        for i, c in enumerate((0, PLON - 1)):
-            place_packed(matrices, row * WIDE + c + 1, edge, i)
-        for i, c in enumerate([-1] + list(range(1, PLON - 1)) + [PLON]):
-            place_packed(matrices, row * WIDE + c + 1, rest, i)
-
+def side_kernel(before, after, above_edge, below_edge, lhs_ref, base_ref, out_ref, matrices):
+    for n, ref in enumerate((before, after, above_edge, below_edge)):
+        for i in range(2):
+            place_packed(matrices, 2 * n + i, ref, i)
+    out_ref[...] = dot_nn(lhs_ref[...], matrices[...]) + base_ref[...]
+
+
+def rim_kernel(above, below, lhs_ref, base_ref, out_ref, matrices):
+    for n, ref in enumerate((above, below)):
+        for i in range(PLON):
+            place_packed(matrices, n * PLON + i, ref, i)
     out_ref[...] = (dot_nn(lhs_ref[...], matrices[...]) + base_ref[...]).astype(BF16)
 
 
@@ -523,10 +534,10 @@
     relayed, own_near = lax.optimization_barrier((relayed, own_near))
     far_edge, far_inner = relay_sums([own_far] + relayed)
     far_edge, far_inner, background = lax.optimization_barrier((far_edge, far_inner, background))
-    mid_lhs, rim_lhs, mean, own_near = cell_parts(PLON * lon_size, pos, stencil, frac, background, own_near)
+    own_lhs, side_lhs, rim_lhs, mean, own_near = cell_parts(PLON * lon_size, pos, stencil, frac, background, own_near)
     got = [own_near] + got
     far_edge = swap(far_edge, half)
-    far_inner, mid_lhs, rim_lhs, mean = lax.optimization_barrier((far_inner, mid_lhs, rim_lhs, mean))
+    far_inner, own_lhs, side_lhs, rim_lhs, mean = lax.optimization_barrier((far_inner, own_lhs, side_lhs, rim_lhs, mean))
     far_inner = swap(far_inner, half)
 
     total, side = near_sums(got)
@@ -541,11 +552,13 @@
     below_edge = lax.ppermute(edge_rows[0], "lat", south)
     far_inner, above_edge, below_edge = lax.optimization_barrier((far_inner, above_edge, below_edge))
     inner, *rows = inner_transforms(total, side, far_inner)
+    partial = mix(own_kernel, [edge, inner], own_lhs, mean, F32)
+    rows, partial = lax.optimization_barrier((rows, partial))
     rows = [rows[r].at[0].set(before[r]).at[PLON - 1].set(after[r]) for r in range(PLAT)]
     above = lax.ppermute(rows[PLAT - 1], "lat", north)
     below = lax.ppermute(rows[0], "lat", south)
-    partial = mix(mid_kernel, [before, after, edge, inner], mid_lhs, mean, F32)
-    return mix(rim_kernel, [above_edge, below_edge, above, below], rim_lhs, partial, BF16).reshape(background.shape)
+    partial = mix(side_kernel, [before, after, above_edge, below_edge], side_lhs, partial, F32)
+    return mix(rim_kernel, [above, below], rim_lhs, partial, BF16).reshape(background.shape)
 
 
 def solution(mesh):

time: 69.8 us -> 70.2 us (level); the launches traced: 69.4 us -> 68.8 us
    ppermute x1, waiting for transfers between devices: 0.76 us -> 0.01 us  [on_device(): after = lax.ppermute(left, 'lon', down)]
    ppermute x1, waiting for transfers between devices: 0.16 us -> 0.88 us  [on_device(): below = lax.ppermute(rows[0], 'lat', south)]
    pallas_call x2 -> x3, Pallas kernels: 4.68 us -> 4.83 us  [mix(): pl.pallas_call(kernel, out_shape=jax.ShapeDtypeStruct((cells, MEMBERS), d...]
  transfers between devices with their start and end apart: 14 -> 14, of which waited for: 6 -> 5; matrix products, arithmetic and copies ran while one was open for 0% -> 0% of each run, Pallas kernels for 36% -> 38%
where the time goes in v6:
time: 70.2 us; the launch traced here: 68.8 us
  Pallas kernels  33 us (47%)
  starting transfers between devices  25.9 us (37%)
  waiting for transfers between devices  8.64 us (12%)
  local copies, waits for them, and re-layouts  1.01 us (1%)
    pallas_call x3, Pallas kernels, batch_blocks(): pl.pallas_call(functools.partial(gram_kernel, first, count, lon_size), ou...  13.8 us
    ppermute x8, starting transfers between devices, swap(): lax.ppermute(value, 'lon', [(i, i ^ offset) for i in range(lon_size)])  8.87 us
    ppermute x8, waiting for transfers between devices, swap(): lax.ppermute(value, 'lon', [(i, i ^ offset) for i in range(lon_size)])  6.57 us
    pallas_call x1, Pallas kernels, cell_parts(): pl.pallas_call(functools.partial(cell_kernel, point_cols), grid=(rows,),...  6.19 us
    pallas_call x3, Pallas kernels, mix(): pl.pallas_call(kernel, out_shape=jax.ShapeDtypeStruct((cells, MEMBERS), d...  4.83 us
    ppermute x1, starting transfers between devices, on_device(): above_edge = lax.ppermute(edge_rows[PLAT - 1], 'lat', north)  4.4 us
    ppermute x1, starting transfers between devices, on_device(): above = lax.ppermute(rows[PLAT - 1], 'lat', north)  4.01 us
    pallas_call x1, Pallas kernels, inner_transforms(): pl.pallas_call(inner_kernel, out_shape=[jax.ShapeDtypeStruct((count, MEMB...  3.47 us
  transfers between devices with their start and end apart: 14, of which 5 were waited for; matrix products, arithmetic and copies ran while one was open for 0% of the time, Pallas kernels for 38%

profile of v6, /device:TPU:1, one launch (start us, length us, event | category | flops | bytes accessed | tf_op | source)
XLA Modules:
  0.0 68.8 jit_solution(4186315171198589306)
XLA Ops:
  0.0 4.7 %shard_map.110 = (bf16[1040,128]{1,0:T(8,128)(2,1)}, bf16[1040,128]{1,0:T(8,128)(2,1)}, bf16[1040,128]{1,0:T(8,128)(2,1)}) custom-call(s32[1]{0:T(128)} %bitcast.1.me_ref, s32[1,32]{1,0:T(1,128)} %bitcast.12, s32[1,32]{1,0:T(1,128)} %refs_1_.5, s32[3,32]{1,0:T(4,128)} %bitcast.6, s32[32]{0:T(128)} %refs_3_.5, bf16[32,512]{1,0:T(8,128)(2,1)} %refs_4_.5, ...), custom_call_target="tpu_custom_call" | custom-call | flops 805306368 | bytes 3145728 | tf_op jit(solution)/shard_map/pallas_call | solution.py:140
  4.7 3.1 %collective-permute-start = (bf16[1040,128]{1,0:T(8,128)(2,1)}, bf16[1040,128]{1,0:T(8,128)(2,1)S(1)}, u32[]{:S(2)}, u32[]{:S(2)}) collective-permute-start(bf16[1040,128]{1,0:T(8,128)(2,1)} %get-tuple-element.102), channel_id=1, source_target_pairs={{0,3},{1,2},{2,1},{3,0},{4,7},{5,6},{6,5},{7,4},{8,11},{9,10},{10,... | collective-permute-start | bytes 798728 | tf_op jit(solution)/shard_map/ppermute | solution.py:526
  7.9 0.2 collective-permute-start.1
  8.0 0.2 collective-permute-start.2
  8.2 5.3 %shard_map.109 = (bf16[1040,128]{1,0:T(8,128)(2,1)}, bf16[1040,128]{1,0:T(8,128)(2,1)}, bf16[1040,128]{1,0:T(8,128)(2,1)}, bf16[1040,128]{1,0:T(8,128)(2,1)}) custom-call(s32[1]{0:T(128)} %bitcast.1.me_ref, s32[1,32]{1,0:T(1,128)} %bitcast.13, s32[1,32]{1,0:T(1,128)} %refs_1_.5, s32[3,32]{1,0:T(4,128)} %bitcast.7, s32[32]{0:T(128)} %refs_3_.5, ...), custom_call_target="tpu_custom_call" | custom-call | flops 1073741824 | bytes 4194304 | tf_op jit(solution)/shard_map/pallas_call | solution.py:140
  13.5 1.3 %collective-permute-start.5 = (bf16[1040,128]{1,0:T(8,128)(2,1)}, bf16[1040,128]{1,0:T(8,128)(2,1)S(1)}, u32[]{:S(2)}, u32[]{:S(2)}) collective-permute-start(bf16[1040,128]{1,0:T(8,128)(2,1)} %get-tuple-element.97), channel_id=1, source_target_pairs={{0,1},{1,0},{2,3},{3,2},{4,5},{5,4},{6,7},{7,6},{8,9},{9,8},{10,11... | collective-permute-start | bytes 798728 | tf_op jit(solution)/shard_map/ppermute | solution.py:526
  14.9 1.3 %collective-permute-start.4 = (bf16[1040,128]{1,0:T(8,128)(2,1)}, bf16[1040,128]{1,0:T(8,128)(2,1)S(1)}, u32[]{:S(2)}, u32[]{:S(2)}) collective-permute-start(bf16[1040,128]{1,0:T(8,128)(2,1)} %get-tuple-element.98), channel_id=1, source_target_pairs={{0,2},{1,3},{2,0},{3,1},{4,6},{5,7},{6,4},{7,5},{8,10},{9,11},{10,... | collective-permute-start | bytes 798728 | tf_op jit(solution)/shard_map/ppermute | solution.py:526
  16.2 3.7 %shard_map.111.kept_in = bf16[1040,128]{1,0:T(8,128)(2,1)} custom-call(s32[1]{0:T(128)} %bitcast.1.me_ref, s32[1,32]{1,0:T(1,128)} %bitcast.14, s32[1,32]{1,0:T(1,128)} %refs_1_.5, s32[3,32]{1,0:T(4,128)} %bitcast.8, s32[32]{0:T(128)} %refs_3_.5, bf16[32,512]{1,0:T(8,128)(2,1)} %refs_4_.5, bf16[32,512]{1,0:T(8,128)(2,1)} %refs_5_.5, bf16[3,32]{1,0:T(4,128)(2,1)} %bitcast.11, ...), custom_call_target="tpu_custom_call" | custom-call | flops 268435456 | bytes 1048576 | tf_op jit(solution)/shard_map/pallas_call | solution.py:140
  20.0 0.1 collective-permute-start.3
  20.1 0.5 collective-permute-done.2.refs_3_
  20.6 0.6 shard_map.112
  21.3 2.5 %collective-permute-start.7 = (bf16[1040,128]{1,0:T(8,128)(2,1)S(1)}, bf16[1040,128]{1,0:T(8,128)(2,1)S(1)}, u32[]{:S(2)}, u32[]{:S(2)}) collective-permute-start(bf16[1040,128]{1,0:T(8,128)(2,1)S(1)} %get-tuple-element.122), channel_id=1, source_target_pairs={{0,4},{1,5},{2,6},{3,7},{4,0},{5,1},{6,2},{7,3},{8,12},{9,13},{10,... | collective-permute-start | bytes 798728 | tf_op jit(solution)/shard_map/ppermute | solution.py:526
  23.8 0.1 pad_add_fusion.pos_ref
  23.9 0.9 %copy-done = bf16[1040,128]{1,0:T(8,128)(2,1)S(1)} copy-done((bf16[1040,128]{1,0:T(8,128)(2,1)S(1)}, bf16[1040,128]{1,0:T(8,128)(2,1)}, u32[]{:S(2)}) %copy-start) | copy-done | bytes 266264
  24.8 6.2 %shard_map.113 = (bf16[1024,2048]{1,0:T(8,128)(2,1)S(1)}, bf16[1024,2048]{1,0:T(8,128)(2,1)S(1)}, bf16[1024,2048]{1,0:T(8,128)(2,1)S(1)}, f32[1024,128]{1,0:T(8,128)S(1)}, bf16[1040,128]{1,0:T(8,128)(2,1)S(1)}) custom-call(s32[2]{0:T(128)S(1)} %pad_add_fusion.pos_ref, s32[2,8,128]{2,1,0:T(8,128)S(1)} %copy-done.3, f32[2,8,128]{2,1,0:T(8,128)S(1)} %copy-done.4, ...), custom_call_target="tpu_custom_call" | custom-call | flops 6291456 | bytes 13631488 | tf_op jit(solution)/shard_map/pallas_call | solution.py:441
  31.0 0.1 collective-permute-start.6
  31.1 0.1 collective-permute-done.4.refs_2_
  31.2 6.0 %collective-permute-done.3.refs_1_ = bf16[1040,128]{1,0:T(8,128)(2,1)S(1)} collective-permute-done((bf16[1040,128]{1,0:T(8,128)(2,1)S(1)}, bf16[1040,128]{1,0:T(8,128)(2,1)S(1)}, u32[]{:S(2)}, u32[]{:S(2)}) %collective-permute-start.3) | collective-permute-done | bytes 266272 | tf_op jit(solution)/shard_map/ppermute | solution.py:526
  37.2 0.6 shard_map.114
  37.8 3.5 %shard_map.115 = (bf16[2,272,128]{2,1,0:T(8,128)(2,1)S(1)}, bf16[2,272,128]{2,1,0:T(8,128)(2,1)S(1)}, bf16[2,272,128]{2,1,0:T(8,128)(2,1)S(1)}, bf16[2,272,128]{2,1,0:T(8,128)(2,1)S(1)}, bf16[4,256,256]{2,1,0:T(8,128)(2,1)S(1)}) custom-call(f32[8,256,128]{2,1,0:T(8,128)S(1)} %get-tuple-element.114.total_in, f32[3,8,128]{2,1,0:T(8,128)S(1)} %get-tuple-element.115.side_in, ...), custom_call_target="tpu_custom_call" | custom-call | flops 2013265920 | bytes 786432 | tf_op jit(solution)/shard_map/pallas_call | solution.py:363
  41.3 4.4 %collective-permute-start.8 = (bf16[2,272,128]{2,1,0:T(8,128)(2,1)S(1)}, bf16[2,272,128]{2,1,0:T(8,128)(2,1)S(1)}, u32[]{:S(2)}, u32[]{:S(2)}) collective-permute-start(bf16[2,272,128]{2,1,0:T(8,128)(2,1)S(1)} %get-tuple-element.123), channel_id=1, source_target_pairs={{0,8},{8,16},{16,24},{1,9},{9,17},{17,25},{2,10},{10,18},{18,26},{... | collective-permute-start | bytes 417800 | tf_op jit(solution)/shard_map/ppermute | solution.py:551
  45.7 1.9 %collective-permute-start.9 = (bf16[2,272,128]{2,1,0:T(8,128)(2,1)S(1)}, bf16[2,272,128]{2,1,0:T(8,128)(2,1)S(1)}, u32[]{:S(2)}, u32[]{:S(2)}) collective-permute-start(bf16[2,272,128]{2,1,0:T(8,128)(2,1)S(1)} %get-tuple-element.124), channel_id=1, source_target_pairs={{8,0},{16,8},{24,16},{9,1},{17,9},{25,17},{10,2},{18,10},{26,18},{... | collective-permute-start | bytes 417800 | tf_op jit(solution)/shard_map/ppermute | solution.py:552
  47.6 1.7 %collective-permute-start.10 = (bf16[2,272,128]{2,1,0:T(8,128)(2,1)S(1)}, bf16[2,272,128]{2,1,0:T(8,128)(2,1)S(1)}, u32[]{:S(2)}, u32[]{:S(2)}) collective-permute-start(bf16[2,272,128]{2,1,0:T(8,128)(2,1)S(1)} %get-tuple-element.133), channel_id=1, source_target_pairs={{0,1},{1,2},{2,3},{3,4},{4,5},{5,6},{6,7},{7,0},{8,9},{9,10},{10,1... | collective-permute-start | bytes 417800 | tf_op jit(solution)/shard_map/ppermute | solution.py:549
  49.3 3.1 %collective-permute-start.11 = (bf16[2,272,128]{2,1,0:T(8,128)(2,1)S(1)}, bf16[2,272,128]{2,1,0:T(8,128)(2,1)S(1)}, u32[]{:S(2)}, u32[]{:S(2)}) collective-permute-start(bf16[2,272,128]{2,1,0:T(8,128)(2,1)S(1)} %get-tuple-element.134), channel_id=1, source_target_pairs={{1,0},{2,1},{3,2},{4,3},{5,4},{6,5},{7,6},{0,7},{9,8},{10,9},{11,1... | collective-permute-start | bytes 417800 | tf_op jit(solution)/shard_map/ppermute | solution.py:550
  52.4 3.5 %shard_map.116 = (bf16[4,256,256]{2,1,0:T(8,128)(2,1)S(1)}, bf16[4,272,128]{2,1,0:T(8,128)(2,1)S(1)}, bf16[4,272,128]{2,1,0:T(8,128)(2,1)S(1)}) custom-call(f32[8,256,128]{2,1,0:T(8,128)S(1)} %get-tuple-element.114.total_in, f32[3,8,128]{2,1,0:T(8,128)S(1)} %get-tuple-element.115.side_in, bf16[1040,128]{1,0:T(8,128)(2,1)S(1)} %collective-permute-done.6.far_ref), custom_call_target="tpu_custom_call" | custom-call | flops 2013265920 | bytes 786432 | tf_op jit(solution)/shard_map/pallas_call | solution.py:378
  55.9 1.2 %shard_map.117.base_ref = f32[1024,256]{1,0:T(8,128)S(1)} custom-call(bf16[4,256,256]{2,1,0:T(8,128)(2,1)S(1)} %get-tuple-element.128.edge, bf16[4,256,256]{2,1,0:T(8,128)(2,1)S(1)} %get-tuple-element.129.inner, bf16[1024,2048]{1,0:T(8,128)(2,1)S(1)} %get-tuple-element.130.lhs_ref, f32[1024,128]{1,0:T(8,128)S(1)} %get-tuple-element.131.mean_ref), custom_call_target="tpu_custom_call" | custom-call | flops 1073741824 | bytes 4194304 | tf_op jit(solution)/shard_map/pallas_call | solution.py:503
  57.2 1.9 %collective-permute-start.13 = (bf16[4,272,128]{2,1,0:T(8,128)(2,1)S(1)}, bf16[4,272,128]{2,1,0:T(8,128)(2,1)S(1)}, u32[]{:S(2)}, u32[]{:S(2)}) collective-permute-start(bf16[4,272,128]{2,1,0:T(8,128)(2,1)S(1)} %get-tuple-element.141), channel_id=1, source_target_pairs={{8,0},{16,8},{24,16},{9,1},{17,9},{25,17},{10,2},{18,10},{26,18},{... | collective-permute-start | bytes 835592 | tf_op jit(solution)/shard_map/ppermute | solution.py:559
  59.1 4.0 %collective-permute-start.12 = (bf16[4,272,128]{2,1,0:T(8,128)(2,1)S(1)}, bf16[4,272,128]{2,1,0:T(8,128)(2,1)S(1)}, u32[]{:S(2)}, u32[]{:S(2)}) collective-permute-start(bf16[4,272,128]{2,1,0:T(8,128)(2,1)S(1)} %get-tuple-element.142), channel_id=1, source_target_pairs={{0,8},{8,16},{16,24},{1,9},{9,17},{17,25},{2,10},{10,18},{18,26},{... | collective-permute-start | bytes 835592 | tf_op jit(solution)/shard_map/ppermute | solution.py:558
  63.2 1.4 %shard_map.118.base_ref = f32[1024,256]{1,0:T(8,128)S(1)} custom-call(bf16[2,272,128]{2,1,0:T(8,128)(2,1)S(1)} %collective-permute-done.10.before, bf16[2,272,128]{2,1,0:T(8,128)(2,1)S(1)} %collective-permute-done.11.after, bf16[2,272,128]{2,1,0:T(8,128)(2,1)S(1)} %collective-permute-done.8.above_edge, ...), custom_call_target="tpu_custom_call" | custom-call | flops 1073741824 | bytes 4194304 | tf_op jit(solution)/shard_map/pallas_call | solution.py:503
  64.6 0.9 %collective-permute-done.13.below = bf16[4,272,128]{2,1,0:T(8,128)(2,1)S(1)} collective-permute-done((bf16[4,272,128]{2,1,0:T(8,128)(2,1)S(1)}, bf16[4,272,128]{2,1,0:T(8,128)(2,1)S(1)}, u32[]{:S(2)}, u32[]{:S(2)}) %collective-permute-start.13) | collective-permute-done | bytes 278560 | tf_op jit(solution)/shard_map/ppermute | solution.py:559
  65.4 1.2 %collective-permute-done.12.above = bf16[4,272,128]{2,1,0:T(8,128)(2,1)S(1)} collective-permute-done((bf16[4,272,128]{2,1,0:T(8,128)(2,1)S(1)}, bf16[4,272,128]{2,1,0:T(8,128)(2,1)S(1)}, u32[]{:S(2)}, u32[]{:S(2)}) %collective-permute-start.12) | collective-permute-done | bytes 278560 | tf_op jit(solution)/shard_map/ppermute | solution.py:558
  66.6 2.2 %shard_map.119 = bf16[1024,256]{1,0:T(8,128)(2,1)} custom-call(bf16[4,272,128]{2,1,0:T(8,128)(2,1)S(1)} %collective-permute-done.12.above, bf16[4,272,128]{2,1,0:T(8,128)(2,1)S(1)} %collective-permute-done.13.below, bf16[1024,2048]{1,0:T(8,128)(2,1)S(1)} %get-tuple-element.136.lhs_ref, f32[1024,256]{1,0:T(8,128)S(1)} %shard_map.118.base_ref), custom_call_target="tpu_custom_call" | custom-call | flops 1073741824 | bytes 4194304 | tf_op jit(solution)/shard_map/pallas_call | solution.py:503
  (22 shorter events, 0.1 us)
Async XLA Ops:
  4.7 15.2 %collective-permute-start = (bf16[1040,128]{1,0:T(8,128)(2,1)}, bf16[1040,128]{1,0:T(8,128)(2,1)S(1)}, u32[]{:S(2)}, u32[]{:S(2)}) collective-permute-start(bf16[1040,128]{1,0:T(8,128)(2,1)} %get-tuple-element.102), channel_id=1, source_target_pairs={{0,3},{1,2},{2,1},{3,0},{4,7},{5,6},{6,5},{7,4},{8,11},{9,10},{10,... | collective-permute-start | bytes 798728 | tf_op jit(solution)/shard_map/ppermute | solution.py:526
  7.9 12.2 %collective-permute-start.1 = (bf16[1040,128]{1,0:T(8,128)(2,1)}, bf16[1040,128]{1,0:T(8,128)(2,1)S(1)}, u32[]{:S(2)}, u32[]{:S(2)}) collective-permute-start(bf16[1040,128]{1,0:T(8,128)(2,1)} %get-tuple-element.103), channel_id=1, source_target_pairs={{0,2},{1,3},{2,0},{3,1},{4,6},{5,7},{6,4},{7,5},{8,10},{9,11},{10,... | collective-permute-start | bytes 798728 | tf_op jit(solution)/shard_map/ppermute | solution.py:526
  8.0 12.6 %collective-permute-start.2 = (bf16[1040,128]{1,0:T(8,128)(2,1)}, bf16[1040,128]{1,0:T(8,128)(2,1)S(1)}, u32[]{:S(2)}, u32[]{:S(2)}) collective-permute-start(bf16[1040,128]{1,0:T(8,128)(2,1)} %get-tuple-element.104), channel_id=1, source_target_pairs={{0,1},{1,0},{2,3},{3,2},{4,5},{5,4},{6,7},{7,6},{8,9},{9,8},{10,11... | collective-permute-start | bytes 798728 | tf_op jit(solution)/shard_map/ppermute | solution.py:526
  13.5 17.6 %collective-permute-start.5 = (bf16[1040,128]{1,0:T(8,128)(2,1)}, bf16[1040,128]{1,0:T(8,128)(2,1)S(1)}, u32[]{:S(2)}, u32[]{:S(2)}) collective-permute-start(bf16[1040,128]{1,0:T(8,128)(2,1)} %get-tuple-element.97), channel_id=1, source_target_pairs={{0,1},{1,0},{2,3},{3,2},{4,5},{5,4},{6,7},{7,6},{8,9},{9,8},{10,11... | collective-permute-start | bytes 798728 | tf_op jit(solution)/shard_map/ppermute | solution.py:526
  14.9 16.3 %collective-permute-start.4 = (bf16[1040,128]{1,0:T(8,128)(2,1)}, bf16[1040,128]{1,0:T(8,128)(2,1)S(1)}, u32[]{:S(2)}, u32[]{:S(2)}) collective-permute-start(bf16[1040,128]{1,0:T(8,128)(2,1)} %get-tuple-element.98), channel_id=1, source_target_pairs={{0,2},{1,3},{2,0},{3,1},{4,6},{5,7},{6,4},{7,5},{8,10},{9,11},{10,... | collective-permute-start | bytes 798728 | tf_op jit(solution)/shard_map/ppermute | solution.py:526
  16.2 3.8 %copy-start.5 = (bf16[1040,128]{1,0:T(8,128)(2,1)S(1)}, bf16[1040,128]{1,0:T(8,128)(2,1)}, u32[]{:S(2)}) copy-start(bf16[1040,128]{1,0:T(8,128)(2,1)} %get-tuple-element.99) | copy-start | bytes 798724
  16.2 4.5 %copy-start.2 = (bf16[1040,128]{1,0:T(8,128)(2,1)S(1)}, bf16[1040,128]{1,0:T(8,128)(2,1)}, u32[]{:S(2)}) copy-start(bf16[1040,128]{1,0:T(8,128)(2,1)} %get-tuple-element.101.refs_0_) | copy-start | bytes 798724
  16.2 7.7 %copy-start.1 = (bf16[8,128,256]{2,1,0:T(8,128)(2,1)S(1)}, bf16[8,128,256]{2,1,0:T(8,128)(2,1)}, u32[]{:S(2)}) copy-start(bf16[8,128,256]{2,1,0:T(8,128)(2,1)} %field_ref) | copy-start | bytes 1572868
  16.2 7.7 %copy-start.3 = (s32[2,8,128]{2,1,0:T(8,128)S(1)}, s32[2,8,128]{2,1,0:T(8,128)}, u32[]{:S(2)}) copy-start(s32[2,8,128]{2,1,0:T(8,128)} %stencil_ref.1) | copy-start | bytes 24580
  16.2 7.7 %copy-start.4 = (f32[2,8,128]{2,1,0:T(8,128)S(1)}, f32[2,8,128]{2,1,0:T(8,128)}, u32[]{:S(2)}) copy-start(f32[2,8,128]{2,1,0:T(8,128)} %frac_ref.1) | copy-start | bytes 24580
  20.0 17.2 %collective-permute-start.3 = (bf16[1040,128]{1,0:T(8,128)(2,1)S(1)}, bf16[1040,128]{1,0:T(8,128)(2,1)S(1)}, u32[]{:S(2)}, u32[]{:S(2)}) collective-permute-start(bf16[1040,128]{1,0:T(8,128)(2,1)S(1)} %copy-done.5), channel_id=1, source_target_pairs={{0,3},{1,2},{2,1},{3,0},{4,7},{5,6},{6,5},{7,4},{8,11},{9,10},{10,... | collective-permute-start | bytes 798728 | tf_op jit(solution)/shard_map/ppermute | solution.py:526
  21.3 16.5 %collective-permute-start.7 = (bf16[1040,128]{1,0:T(8,128)(2,1)S(1)}, bf16[1040,128]{1,0:T(8,128)(2,1)S(1)}, u32[]{:S(2)}, u32[]{:S(2)}) collective-permute-start(bf16[1040,128]{1,0:T(8,128)(2,1)S(1)} %get-tuple-element.122), channel_id=1, source_target_pairs={{0,4},{1,5},{2,6},{3,7},{4,0},{5,1},{6,2},{7,3},{8,12},{9,13},{10,... | collective-permute-start | bytes 798728 | tf_op jit(solution)/shard_map/ppermute | solution.py:526
  23.9 1.0 %copy-start = (bf16[1040,128]{1,0:T(8,128)(2,1)S(1)}, bf16[1040,128]{1,0:T(8,128)(2,1)}, u32[]{:S(2)}) copy-start(bf16[1040,128]{1,0:T(8,128)(2,1)} %shard_map.111.kept_in) | copy-start | bytes 798724
  31.0 21.4 %collective-permute-start.6 = (bf16[1040,128]{1,0:T(8,128)(2,1)S(1)}, bf16[1040,128]{1,0:T(8,128)(2,1)S(1)}, u32[]{:S(2)}, u32[]{:S(2)}) collective-permute-start(bf16[1040,128]{1,0:T(8,128)(2,1)S(1)} %get-tuple-element.121), channel_id=1, source_target_pairs={{0,4},{1,5},{2,6},{3,7},{4,0},{5,1},{6,2},{7,3},{8,12},{9,13},{10,... | collective-permute-start | bytes 798728 | tf_op jit(solution)/shard_map/ppermute | solution.py:526
  41.3 11.1 %collective-permute-start.8 = (bf16[2,272,128]{2,1,0:T(8,128)(2,1)S(1)}, bf16[2,272,128]{2,1,0:T(8,128)(2,1)S(1)}, u32[]{:S(2)}, u32[]{:S(2)}) collective-permute-start(bf16[2,272,128]{2,1,0:T(8,128)(2,1)S(1)} %get-tuple-element.123), channel_id=1, source_target_pairs={{0,8},{8,16},{16,24},{1,9},{9,17},{17,25},{2,10},{10,18},{18,26},{... | collective-permute-start | bytes 417800 | tf_op jit(solution)/shard_map/ppermute | solution.py:551
  45.7 6.7 %collective-permute-start.9 = (bf16[2,272,128]{2,1,0:T(8,128)(2,1)S(1)}, bf16[2,272,128]{2,1,0:T(8,128)(2,1)S(1)}, u32[]{:S(2)}, u32[]{:S(2)}) collective-permute-start(bf16[2,272,128]{2,1,0:T(8,128)(2,1)S(1)} %get-tuple-element.124), channel_id=1, source_target_pairs={{8,0},{16,8},{24,16},{9,1},{17,9},{25,17},{10,2},{18,10},{26,18},{... | collective-permute-start | bytes 417800 | tf_op jit(solution)/shard_map/ppermute | solution.py:552
  47.6 9.5 %collective-permute-start.10 = (bf16[2,272,128]{2,1,0:T(8,128)(2,1)S(1)}, bf16[2,272,128]{2,1,0:T(8,128)(2,1)S(1)}, u32[]{:S(2)}, u32[]{:S(2)}) collective-permute-start(bf16[2,272,128]{2,1,0:T(8,128)(2,1)S(1)} %get-tuple-element.133), channel_id=1, source_target_pairs={{0,1},{1,2},{2,3},{3,4},{4,5},{5,6},{6,7},{7,0},{8,9},{9,10},{10,1... | collective-permute-start | bytes 417800 | tf_op jit(solution)/shard_map/ppermute | solution.py:549
  49.3 7.9 %collective-permute-start.11 = (bf16[2,272,128]{2,1,0:T(8,128)(2,1)S(1)}, bf16[2,272,128]{2,1,0:T(8,128)(2,1)S(1)}, u32[]{:S(2)}, u32[]{:S(2)}) collective-permute-start(bf16[2,272,128]{2,1,0:T(8,128)(2,1)S(1)} %get-tuple-element.134), channel_id=1, source_target_pairs={{1,0},{2,1},{3,2},{4,3},{5,4},{6,5},{7,6},{0,7},{9,8},{10,9},{11,1... | collective-permute-start | bytes 417800 | tf_op jit(solution)/shard_map/ppermute | solution.py:550
  57.2 8.2 %collective-permute-start.13 = (bf16[4,272,128]{2,1,0:T(8,128)(2,1)S(1)}, bf16[4,272,128]{2,1,0:T(8,128)(2,1)S(1)}, u32[]{:S(2)}, u32[]{:S(2)}) collective-permute-start(bf16[4,272,128]{2,1,0:T(8,128)(2,1)S(1)} %get-tuple-element.141), channel_id=1, source_target_pairs={{8,0},{16,8},{24,16},{9,1},{17,9},{25,17},{10,2},{18,10},{26,18},{... | collective-permute-start | bytes 835592 | tf_op jit(solution)/shard_map/ppermute | solution.py:559
  59.1 7.5 %collective-permute-start.12 = (bf16[4,272,128]{2,1,0:T(8,128)(2,1)S(1)}, bf16[4,272,128]{2,1,0:T(8,128)(2,1)S(1)}, u32[]{:S(2)}, u32[]{:S(2)}) collective-permute-start(bf16[4,272,128]{2,1,0:T(8,128)(2,1)S(1)} %get-tuple-element.142), channel_id=1, source_target_pairs={{0,8},{8,16},{16,24},{1,9},{9,17},{17,25},{2,10},{10,18},{18,26},{... | collective-permute-start | bytes 835592 | tf_op jit(solution)/shard_map/ppermute | solution.py:558
